TPU v7x, 32 devices: a whole 2x2x4 slice. The times are simulated.
32 devices in a mesh: expert: 16 (over z, y, core), dp: 2 (over x).
Axes of the slice: x: 2, y: 2, z: 4, core: 2. Of those that a mesh axis runs over, the one named last changes fastest.
Arguments:
- tokens: bfloat16 [1024, 2048], P(('expert', 'dp')), may hold values from -6 to 6
- expert_ids: int32 [1024, 8], P(('expert', 'dp')), may hold values from 0 to 15, all different within a row; in each aligned block of 32 rows (0 to 31, 32 to 63, ...) at most 32 rows name the same one
- gate_weights: bfloat16 [1024, 8], P(('expert', 'dp')), may hold values from 0.049804688 to 0.25
- cotangent: bfloat16 [1024, 2048], P(('expert', 'dp')), may hold values from -12 to 12
- w_gate: bfloat16 [16, 768, 2048], P('expert'), may hold values from -0.125 to 0.125
- w_up: bfloat16 [16, 768, 2048], P('expert'), may hold values from -0.125 to 0.125
- w_down: bfloat16 [16, 2048, 768], P('expert'), may hold values from -0.21875 to 0.21875
Outputs:
- token_grad: bfloat16 [1024, 2048], P(('expert', 'dp'))
- gate_grad: bfloat16 [1024, 8], P(('expert', 'dp'))
- grad_gate: bfloat16 [16, 768, 2048], P('expert', 'dp')
- grad_up: bfloat16 [16, 768, 2048], P('expert', 'dp')
- grad_down_t: bfloat16 [16, 768, 2048], P('expert', 'dp')
Inputs may be any that keep to these rules, and one draw needn't show every extreme that they name: `expert_ids`: each token names 8 different experts. Among the tokens of one device (aligned blocks of 32 rows), no expert is named by more than 32 of them, a bound that some block reaches.
All inputs are finite; a program needn't handle non-finite values.
Results may differ from a plain program's by a relative error of at most 0.017.
Values may be sent and summed in bfloat16 or wider, within the bound.
No kernel may reach another device: no remote copies, remote signals or barrier semaphores. Data moves between devices by JAX's collectives and lax.ppermute only.
A program may use at most 128 MiB of HBM per device.

v0:
```python
import jax
import jax.numpy as jnp
from jax import lax
from jax.sharding import PartitionSpec as P


def contract_last(left, right):
    return lax.dot_general(
        left, right, (((1,), (1,)), ((), ())), preferred_element_type=jnp.float32
    )


def contract_first(left, right):
    return lax.dot_general(
        left, right, (((0,), (0,)), ((), ())), preferred_element_type=jnp.float32
    )


def rounded(value):
    return lax.optimization_barrier(value.astype(jnp.bfloat16)).astype(jnp.float32)


def expert_forward(expert_rows, gate_mat, up_mat, down_mat):
    pre_gate = contract_last(expert_rows, gate_mat)
    pre_up = contract_last(expert_rows, up_mat)
    gate_sigmoid = jax.nn.sigmoid(pre_gate)
    hidden = (pre_gate * gate_sigmoid * pre_up).astype(jnp.bfloat16)
    outputs = contract_last(hidden, down_mat).astype(jnp.bfloat16)
    return (pre_gate, pre_up, gate_sigmoid, hidden, outputs)


def body(tokens, expert_ids, gate_weights, cotangent, w_gate, w_up, w_down):
    tok_rows, top_count = expert_ids.shape
    model_width = tokens.shape[1]
    experts = lax.axis_size("expert")
    capacity = min(tok_rows, 2 * tok_rows * top_count // experts)
    slot_count = tok_rows * top_count
    buffer_rows = experts * capacity
    flat_ids = expert_ids.reshape(slot_count)
    onehot = (flat_ids[:, None] == jnp.arange(experts, dtype=jnp.int32)[None, :]).astype(jnp.int32)
    slot_rank = jnp.sum((jnp.cumsum(onehot, axis=0) - 1) * onehot, axis=1)
    position = flat_ids * capacity + slot_rank
    placing = (jnp.arange(buffer_rows, dtype=jnp.int32)[:, None] == position[None, :]).astype(
        jnp.bfloat16
    )
    token_map = placing.reshape(buffer_rows, tok_rows, top_count).sum(axis=2)
    x_send = jnp.dot(token_map, tokens, preferred_element_type=jnp.float32).astype(jnp.bfloat16)
    x_send = x_send.reshape(experts, capacity, model_width)
    cot_send = jnp.dot(token_map, cotangent, preferred_element_type=jnp.float32).astype(
        jnp.bfloat16
    )
    cot_send = cot_send.reshape(experts, capacity, model_width)
    gate_send = jnp.dot(
        placing, gate_weights.reshape(slot_count), preferred_element_type=jnp.float32
    )
    gate_send = gate_send.astype(jnp.bfloat16).reshape(experts, capacity)
    gate_mat = w_gate[0]
    up_mat = w_up[0]
    down_mat = w_down[0]
    x_recv = lax.all_to_all(x_send, "expert", split_axis=0, concat_axis=0, tiled=True)
    expert_rows = x_recv.reshape(buffer_rows, model_width)
    pre_gate, pre_up, gate_sigmoid, hidden, outputs = expert_forward(
        expert_rows, gate_mat, up_mat, down_mat
    )
    cot_recv, gate_recv = (
        lax.all_to_all(cot_send, "expert", split_axis=0, concat_axis=0, tiled=True),
        lax.all_to_all(gate_send, "expert", split_axis=0, concat_axis=0, tiled=True),
    )
    cot_rows = cot_recv.reshape(buffer_rows, model_width)
    gate_rows = gate_recv.reshape(buffer_rows).astype(jnp.float32)
    scaled = (gate_rows[:, None] * cot_rows.astype(jnp.float32)).astype(jnp.bfloat16)
    d_hidden = jnp.dot(scaled, down_mat, preferred_element_type=jnp.float32)
    d_pre_gate = (
        d_hidden * pre_up * gate_sigmoid * (1.0 + pre_gate * (1.0 - gate_sigmoid))
    ).astype(jnp.bfloat16)
    d_pre_up = (d_hidden * pre_gate * gate_sigmoid).astype(jnp.bfloat16)
    slot_grad = (
        jnp.dot(d_pre_gate, gate_mat, preferred_element_type=jnp.float32)
        + jnp.dot(d_pre_up, up_mat, preferred_element_type=jnp.float32)
    ).astype(jnp.bfloat16)
    pieces = []
    for operand, partner in ((d_pre_gate, expert_rows), (d_pre_up, expert_rows), (hidden, scaled)):
        pieces.append(rounded(contract_first(operand, partner)))
    summed = lax.psum_scatter(
        jnp.concatenate(pieces, axis=1).astype(jnp.bfloat16), "dp", scatter_dimension=0, tiled=True
    ).astype(jnp.float32)
    grad_gate = summed[:, :model_width].astype(jnp.bfloat16)[None]
    grad_up = summed[:, model_width : 2 * model_width].astype(jnp.bfloat16)[None]
    grad_down_t = summed[:, 2 * model_width :].astype(jnp.bfloat16)[None]
    slot_back = slot_grad.reshape(experts, capacity, model_width)
    out_send = outputs.reshape(experts, capacity, model_width)
    grad_back, out_back = (
        lax.all_to_all(slot_back, "expert", split_axis=0, concat_axis=0, tiled=True),
        lax.all_to_all(out_send, "expert", split_axis=0, concat_axis=0, tiled=True),
    )
    picked = out_back.reshape(buffer_rows, model_width)[position].astype(jnp.float32)
    picked = picked.reshape(tok_rows, top_count, model_width)
    gate_grad = jnp.sum(picked * cotangent.astype(jnp.float32)[:, None, :], axis=2).astype(
        jnp.bfloat16
    )
    gathered = grad_back.reshape(buffer_rows, model_width)[position].astype(jnp.float32)
    token_grad = gathered.reshape(tok_rows, top_count, model_width).sum(axis=1).astype(jnp.bfloat16)
    return (token_grad, gate_grad, grad_gate, grad_up, grad_down_t)


def solution(mesh):
    return jax.shard_map(
        body,
        mesh=mesh,
        in_specs=(
            P(("expert", "dp"), None),
            P(("expert", "dp"), None),
            P(("expert", "dp"), None),
            P(("expert", "dp"), None),
            P("expert", None, None),
            P("expert", None, None),
            P("expert", None, None),
        ),
        out_specs=(
            P(("expert", "dp"), None),
            P(("expert", "dp"), None),
            P("expert", "dp", None),
            P("expert", "dp", None),
            P("expert", "dp", None),
        ),
        check_vma=False,
    )
```

profile of v0, /device:TPU:13, one launch (start us, length us, event | category | flops | bytes accessed | tf_op | source)
XLA Modules:
  0.0 286.1 jit_solution(716277059071720648)
XLA Ops:
  7.2 0.9 copy.31
  9.1 0.8 copy.34
  10.3 0.7 all_to_all.24
  11.0 6.6 %all-to-all-start = ((bf16[16,1,32]{2,1,0:T(2,128)(2,1)}), bf16[16,1,32]{2,1,0:T(2,128)(2,1)S(1)}, u32[]{:S(2)}, u32[]{:S(2)}) async-start(bf16[16,1,32]{2,1,0:T(2,128)(2,1)} %all_to_all.24), calls=%async_computation | async-start | bytes 16384 | tf_op jit(solution)/shard_map/all_to_all | solution.py:67
  17.9 2.9 %convolution_convert_fusion.3 = bf16[512,2048]{1,0:T(8,128)(2,1)} fusion(bf16[512,32]{0,1:T(8,128)(2,1)S(1)} %fusion.21, bf16[32,2048]{1,0:T(8,128)(2,1)} %param.7), kind=kOutput, calls=%fused_computation.23 | convolution fusion | flops 68157440 | bytes 2260992 | tf_op jit(solution)/shard_map/dot_general | solution.py:47
  21.3 7.0 %all-to-all-start.2 = ((bf16[16,32,2048]{2,1,0:T(8,128)(2,1)}), bf16[16,32,2048]{2,1,0:T(8,128)(2,1)}, u32[]{:S(2)}, u32[]{:S(2)}) async-start(bf16[16,32,2048]{2,1,0:T(8,128)(2,1)} %bitcast.81), calls=%async_computation.2 | async-start | bytes 4194304 | tf_op jit(solution)/shard_map/all_to_all | solution.py:60
  28.3 2.1 convolution_convert_fusion.4
  30.4 45.5 %all-to-all-done.2 = bf16[16,32,2048]{2,1,0:T(8,128)(2,1)} async-done(((bf16[16,32,2048]{2,1,0:T(8,128)(2,1)}), bf16[16,32,2048]{2,1,0:T(8,128)(2,1)}, u32[]{:S(2)}, u32[]{:S(2)}) %all-to-all-start.2) | async-done | bytes 2097184 | tf_op jit(solution)/shard_map/all_to_all | solution.py:60
  75.8 4.9 %all-to-all-start.1 = ((bf16[16,32,2048]{2,1,0:T(8,128)(2,1)}), bf16[16,32,2048]{2,1,0:T(8,128)(2,1)}, u32[]{:S(2)}, u32[]{:S(2)}) async-start(bf16[16,32,2048]{2,1,0:T(8,128)(2,1)} %bitcast.80), calls=%async_computation.1 | async-start | bytes 4194304 | tf_op jit(solution)/shard_map/all_to_all | solution.py:66
  81.1 5.5 %fusion.3 = f32[512,768]{1,0:T(8,128)} fusion(bf16[512,2048]{1,0:T(8,128)(2,1)} %bitcast.7, bf16[1,768,2048]{2,1,0:T(8,128)(2,1)} %param.11), kind=kOutput, calls=%fused_computation.12 | convolution fusion | flops 1610612736 | bytes 6815744 | tf_op jit(solution)/shard_map/dot_general | solution.py:8
  86.6 41.7 %all-to-all-done.1 = bf16[16,32,2048]{2,1,0:T(8,128)(2,1)} async-done(((bf16[16,32,2048]{2,1,0:T(8,128)(2,1)}), bf16[16,32,2048]{2,1,0:T(8,128)(2,1)}, u32[]{:S(2)}, u32[]{:S(2)}) %all-to-all-start.1) | async-done | bytes 2097184 | tf_op jit(solution)/shard_map/all_to_all | solution.py:66
  128.2 2.1 multiply_convert_fusion
  130.8 1.8 fusion.11
  132.6 4.0 %multiply_convert_fusion.1 = (bf16[512,768]{1,0:T(8,128)(2,1)S(1)}, bf16[512,768]{1,0:T(8,128)(2,1)S(1)}, bf16[512,768]{1,0:T(8,128)(2,1)S(1)}) fusion(f32[512,768]{1,0:T(8,128)S(1)} %copy-done.8, f32[512,768]{1,0:T(8,128)S(1)} %fusion.11, bf16[512,2048]{1,0:T(8,128)(2,1)} %bitcast.7, bf16[1,768,2048]{2,1,0:T(8,128)(2,1)S(1)} %copy-done), kind=kOutput, calls=%fused_computation.30 | convolution fusion | flops 1616904192 | bytes 10747904 | tf_op jit(solution)/shard_map/dot_general | solution.py:8
  136.6 2.8 fusion
  139.5 1.8 convolution_convert_fusion
  141.3 3.4 %convolution_convert_fusion.1 = bf16[768,2048]{1,0:T(8,128)(2,1)S(1)} fusion(bf16[512,768]{1,0:T(8,128)(2,1)S(1)} %get-tuple-element.25, bf16[512,2048]{1,0:T(8,128)(2,1)} %bitcast.7), kind=kOutput, calls=%fused_computation.8 | convolution fusion | flops 1612185600 | bytes 6029312 | tf_op jit(solution)/shard_map/dot_general | solution.py:14
  144.8 3.4 %convolution_convert_fusion.2 = bf16[768,2048]{1,0:T(8,128)(2,1)S(1)} fusion(bf16[512,768]{1,0:T(8,128)(2,1)S(1)} %get-tuple-element.24, bf16[512,2048]{1,0:T(8,128)(2,1)} %bitcast.7), kind=kOutput, calls=%fused_computation.9 | convolution fusion | flops 1612185600 | bytes 6029312 | tf_op jit(solution)/shard_map/dot_general | solution.py:14
  148.2 4.3 %pad_maximum_fusion = bf16[768,6144]{1,0:T(8,128)(2,1)} fusion(bf16[768,2048]{1,0:T(8,128)(2,1)S(1)} %convolution_convert_fusion, bf16[768,2048]{1,0:T(8,128)(2,1)S(1)} %convolution_convert_fusion.1, bf16[768,2048]{1,0:T(8,128)(2,1)S(1)} %convolution_convert_fusion.2), kind=kLoop, calls=%fused_computation.2 | loop fusion | flops 28311552 | bytes 18874368 | tf_op jit(solution)/shard_map/concatenate | solution.py:85
  152.5 4.0 %fusion.1 = f32[512,2048]{1,0:T(8,128)S(1)} fusion(bf16[512,768]{1,0:T(8,128)(2,1)} %copy-done.6, bf16[1,768,2048]{2,1,0:T(8,128)(2,1)} %param.11), kind=kOutput, calls=%fused_computation.10 | convolution fusion | flops 1610612736 | bytes 8126464 | tf_op jit(solution)/shard_map/dot_general | solution.py:78
  156.5 3.2 %add_convert_fusion = bf16[512,2048]{1,0:T(8,128)(2,1)} fusion(f32[512,2048]{1,0:T(8,128)S(1)} %fusion.1, bf16[512,768]{1,0:T(8,128)(2,1)S(1)} %copy-done.5, bf16[1,768,2048]{2,1,0:T(8,128)(2,1)S(1)} %copy-done), kind=kOutput, calls=%fused_computation.5 | convolution fusion | flops 1612709888 | bytes 10223616 | tf_op jit(solution)/shard_map/dot_general | solution.py:79
  159.7 4.9 %all-to-all-start.3 = ((bf16[16,32,2048]{2,1,0:T(8,128)(2,1)}), bf16[16,32,2048]{2,1,0:T(8,128)(2,1)}, u32[]{:S(2)}, u32[]{:S(2)}) async-start(bf16[16,32,2048]{2,1,0:T(8,128)(2,1)} %bitcast.83), calls=%async_computation.3 | async-start | bytes 4194304 | tf_op jit(solution)/shard_map/all_to_all | solution.py:93
  164.6 5.3 %fusion.13 = bf16[512,2048]{1,0:T(8,128)(2,1)} fusion(bf16[512,768]{1,0:T(8,128)(2,1)} %copy-done.7, bf16[1,2048,768]{2,1,0:T(8,128)(2,1)} %param.13), kind=kOutput, calls=%fused_computation.22 | convolution fusion | flops 1611661312 | bytes 6029312 | tf_op jit(solution)/shard_map/dot_general | solution.py:8
  169.9 42.5 %all-to-all-done.3 = bf16[16,32,2048]{2,1,0:T(8,128)(2,1)} async-done(((bf16[16,32,2048]{2,1,0:T(8,128)(2,1)}), bf16[16,32,2048]{2,1,0:T(8,128)(2,1)}, u32[]{:S(2)}, u32[]{:S(2)}) %all-to-all-start.3) | async-done | bytes 2097184 | tf_op jit(solution)/shard_map/all_to_all | solution.py:93
  212.5 4.6 %all-to-all-start.4 = ((bf16[16,32,2048]{2,1,0:T(8,128)(2,1)}), bf16[16,32,2048]{2,1,0:T(8,128)(2,1)}, u32[]{:S(2)}, u32[]{:S(2)}) async-start(bf16[16,32,2048]{2,1,0:T(8,128)(2,1)} %bitcast.82), calls=%async_computation.4 | async-start | bytes 4194304 | tf_op jit(solution)/shard_map/all_to_all | solution.py:94
  217.2 0.7 compare_select_fusion
  217.9 5.4 %gather_fusion = bf16[256,2048]{1,0:T(8,128)(2,1)} fusion(bf16[512,2048]{1,0:T(8,128)(2,1)} %bitcast.11, s32[1024]{0:T(1024)S(1)} %pad_clamp_fusion), kind=kCustom, calls=%fused_computation | custom fusion | bytes 2098176 | tf_op jit(solution)/shard_map/gather | solution.py:101
  223.2 41.4 %all-to-all-done.4 = bf16[16,32,2048]{2,1,0:T(8,128)(2,1)} async-done(((bf16[16,32,2048]{2,1,0:T(8,128)(2,1)}), bf16[16,32,2048]{2,1,0:T(8,128)(2,1)}, u32[]{:S(2)}, u32[]{:S(2)}) %all-to-all-start.4) | async-done | bytes 2097184 | tf_op jit(solution)/shard_map/all_to_all | solution.py:94
  264.6 5.2 %gather_fusion.1 = bf16[256,2048]{1,0:T(8,128)(2,1)} fusion(bf16[512,2048]{1,0:T(8,128)(2,1)} %bitcast.16, s32[1024]{0:T(1024)S(1)} %pad_clamp_fusion), kind=kCustom, calls=%fused_computation.1 | custom fusion | bytes 2098176 | tf_op jit(solution)/shard_map/gather | solution.py:96
  269.8 1.5 fusion.18
  272.0 2.6 bitcast_reduce_fusion
  274.6 4.7 %slice_bitcast_fusion = (bf16[1,384,2048]{2,1,0:T(8,128)(2,1)}, bf16[1,384,2048]{2,1,0:T(8,128)(2,1)}, bf16[1,384,2048]{2,1,0:T(8,128)(2,1)}) fusion(bf16[384,6144]{1,0:T(8,128)(2,1)} %reduce-scatter.2.cloned.1.call-done), kind=kLoop, calls=%fused_computation.27 | loop fusion | bytes 9437184 | tf_op jit(solution)/shard_map/broadcast_in_dim | solution.py:89
  (44 shorter events, 3.7 us)
Async XLA Ops:
  7.2 125.4 %copy-start = (bf16[1,768,2048]{2,1,0:T(8,128)(2,1)S(1)}, bf16[1,768,2048]{2,1,0:T(8,128)(2,1)}, u32[]{:S(2)}) copy-start(bf16[1,768,2048]{2,1,0:T(8,128)(2,1)} %param.12) | copy-start | bytes 9437188
  10.1 11.2 %copy-start.2 = (s32[256]{0:T(256)}, s32[256]{0:T(256)S(1)}, u32[]{:S(2)}) copy-start(s32[256]{0:T(256)S(1)} %fusion.24) | copy-start | bytes 3076
  11.0 10.3 %all-to-all-start = ((bf16[16,1,32]{2,1,0:T(2,128)(2,1)}), bf16[16,1,32]{2,1,0:T(2,128)(2,1)S(1)}, u32[]{:S(2)}, u32[]{:S(2)}) async-start(bf16[16,1,32]{2,1,0:T(2,128)(2,1)} %all_to_all.24), calls=%async_computation | async-start | bytes 16384 | tf_op jit(solution)/shard_map/all_to_all | solution.py:67
  21.3 7.0 %copy-start.1 = (bf16[32,2048]{1,0:T(8,128)(2,1)S(1)}, bf16[32,2048]{1,0:T(8,128)(2,1)}, u32[]{:S(2)}) copy-start(bf16[32,2048]{1,0:T(8,128)(2,1)} %param.10) | copy-start | bytes 393220
  21.3 54.6 %all-to-all-start.2 = ((bf16[16,32,2048]{2,1,0:T(8,128)(2,1)}), bf16[16,32,2048]{2,1,0:T(8,128)(2,1)}, u32[]{:S(2)}, u32[]{:S(2)}) async-start(bf16[16,32,2048]{2,1,0:T(8,128)(2,1)} %bitcast.81), calls=%async_computation.2 | async-start | bytes 4194304 | tf_op jit(solution)/shard_map/all_to_all | solution.py:60
  75.8 52.4 %all-to-all-start.1 = ((bf16[16,32,2048]{2,1,0:T(8,128)(2,1)}), bf16[16,32,2048]{2,1,0:T(8,128)(2,1)}, u32[]{:S(2)}, u32[]{:S(2)}) async-start(bf16[16,32,2048]{2,1,0:T(8,128)(2,1)} %bitcast.80), calls=%async_computation.1 | async-start | bytes 4194304 | tf_op jit(solution)/shard_map/all_to_all | solution.py:66
  80.7 193.8 %reduce-scatter.2.cloned.1.call-start = ((), (), s32[]{:S(2)}) async-start(), calls=%async_computation.6 | async-start | bytes 14155776 | tf_op jit(solution)/shard_map/reduce_scatter | solution.py:84
  128.2 2.5 copy-start.3
  130.8 1.8 copy-start.8
  136.6 2.9 %copy-start.7 = (bf16[512,768]{1,0:T(8,128)(2,1)}, bf16[512,768]{1,0:T(8,128)(2,1)S(1)}, u32[]{:S(2)}) copy-start(bf16[512,768]{1,0:T(8,128)(2,1)S(1)} %get-tuple-element.23) | copy-start | bytes 2359300
  136.6 4.7 %copy-start.4 = (bf16[512,768]{1,0:T(8,128)(2,1)}, bf16[512,768]{1,0:T(8,128)(2,1)S(1)}, u32[]{:S(2)}) copy-start(bf16[512,768]{1,0:T(8,128)(2,1)S(1)} %get-tuple-element.25) | copy-start | bytes 2359300
  136.6 8.1 %copy-start.6 = (bf16[512,768]{1,0:T(8,128)(2,1)}, bf16[512,768]{1,0:T(8,128)(2,1)S(1)}, u32[]{:S(2)}) copy-start(bf16[512,768]{1,0:T(8,128)(2,1)S(1)} %get-tuple-element.24) | copy-start | bytes 2359300
  152.5 4.0 %copy-start.5 = (bf16[512,768]{1,0:T(8,128)(2,1)S(1)}, bf16[512,768]{1,0:T(8,128)(2,1)}, u32[]{:S(2)}) copy-start(bf16[512,768]{1,0:T(8,128)(2,1)} %copy-done.4) | copy-start | bytes 2359300
  159.7 52.7 %all-to-all-start.3 = ((bf16[16,32,2048]{2,1,0:T(8,128)(2,1)}), bf16[16,32,2048]{2,1,0:T(8,128)(2,1)}, u32[]{:S(2)}, u32[]{:S(2)}) async-start(bf16[16,32,2048]{2,1,0:T(8,128)(2,1)} %bitcast.83), calls=%async_computation.3 | async-start | bytes 4194304 | tf_op jit(solution)/shard_map/all_to_all | solution.py:93
  212.5 52.1 %all-to-all-start.4 = ((bf16[16,32,2048]{2,1,0:T(8,128)(2,1)}), bf16[16,32,2048]{2,1,0:T(8,128)(2,1)}, u32[]{:S(2)}, u32[]{:S(2)}) async-start(bf16[16,32,2048]{2,1,0:T(8,128)(2,1)} %bitcast.82), calls=%async_computation.4 | async-start | bytes 4194304 | tf_op jit(solution)/shard_map/all_to_all | solution.py:94
Sparse Core Ops, SparseCore 0:
  152.6 110.0 reduce-scatter.1
where the time goes:
time: 287 us; the launch traced here: 286 us
  waiting for transfers between devices  172 us (60%)
  matrix products  37.6 us (13%)
  starting transfers between devices  28.2 us (10%)
  local copies, waits for them, and re-layouts  19.4 us (7%)
  other arithmetic  15.1 us (5%)
  between operations  14.2 us (5%)
    all_to_all x1, waiting for transfers between devices, body(): lax.all_to_all(x_send, 'expert', split_axis=0, concat_axis=0, tiled=True)  45.5 us
    all_to_all x1, waiting for transfers between devices, body(): lax.all_to_all(slot_back, 'expert', split_axis=0, concat_axis=0, tiled=True)  42.5 us
    all_to_all x1, waiting for transfers between devices, body(): lax.all_to_all(cot_send, 'expert', split_axis=0, concat_axis=0, tiled=True)  41.7 us
    all_to_all x1, waiting for transfers between devices, body(): lax.all_to_all(out_send, 'expert', split_axis=0, concat_axis=0, tiled=True)  41.4 us
    dot_general x3, matrix products, contract_last(): lax.dot_general(left, right, (((1,), (1,)), ((), ())), preferred_element_...  14.8 us
    dot_general x3, matrix products, contract_first(): lax.dot_general(left, right, (((0,), (0,)), ((), ())), preferred_element_...  8.69 us
    all_to_all x1, starting transfers between devices, body(): lax.all_to_all(x_send, 'expert', split_axis=0, concat_axis=0, tiled=True)  7.02 us
    all_to_all x1, starting transfers between devices, body(): lax.all_to_all(gate_send, 'expert', split_axis=0, concat_axis=0, tiled=True)  6.55 us
  transfers between devices with their start and end apart: 6, of which 5 were waited for; matrix products, arithmetic and copies ran while one was open for 14% of the time, Pallas kernels for 0%

commit v1 on v0

--- a/solution.py
+++ b/solution.py
@@ -2,6 +2,8 @@
 import jax.numpy as jnp
 from jax import lax
 from jax.sharding import PartitionSpec as P
+
+BOTH = ("expert", "dp")
 
 
 def contract_last(left, right):
@@ -29,7 +31,7 @@
     return (pre_gate, pre_up, gate_sigmoid, hidden, outputs)
 
 
-def body(tokens, expert_ids, gate_weights, cotangent, w_gate, w_up, w_down):
+def routed_body(tokens, expert_ids, gate_weights, cotangent, w_gate, w_up, w_down):
     tok_rows, top_count = expert_ids.shape
     model_width = tokens.shape[1]
     experts = lax.axis_size("expert")
@@ -103,6 +105,118 @@
     return (token_grad, gate_grad, grad_gate, grad_up, grad_down_t)
 
 
+def stages_of(count, groups):
+    core = groups
+    bits = [1 << b for b in range(count.bit_length() - 1)]
+    bits.remove(core)
+    last = [bits[0], bits[1]]
+    first = bits[:1:-1]
+    steps = [[i ^ b for i in range(count)] for b in first]
+    steps.append([i ^ (last[1] if i & core else last[0]) for i in range(count)])
+    steps.append([i ^ (last[0] if i & core else last[1]) for i in range(count)])
+    return steps, [i ^ core for i in range(count)]
+
+
+def swap(value, partners):
+    return lax.ppermute(value, BOTH, list(enumerate(partners)))
+
+
+def gathered(value, steps):
+    for partners in steps:
+        value = jnp.concatenate([value, swap(value, partners)], axis=0)
+    return value
+
+
+def added(left, right):
+    return (left.astype(jnp.float32) + right.astype(jnp.float32)).astype(jnp.bfloat16)
+
+
+def scattered(value, steps):
+    for partners in steps[::-1]:
+        half = value.shape[0] // 2
+        value = added(value[:half], swap(value[half:], partners))
+    return value
+
+
+def dense_body(tokens, expert_ids, gate_weights, cotangent, w_gate, w_up, w_down):
+    model_width = tokens.shape[1]
+    experts = lax.axis_size("expert")
+    groups = lax.axis_size("dp")
+    mine = lax.axis_index("expert")
+    part = lax.axis_index("dp")
+    hidden_units = w_gate.shape[1] // groups
+    steps, core_swap = stages_of(experts * groups, groups)
+    lanes = -(-experts // 128) * 128
+    named = expert_ids[:, :, None] == jnp.arange(lanes, dtype=jnp.int32)[None, None, :]
+    gate_table = jnp.sum(
+        jnp.where(named, gate_weights.astype(jnp.float32)[:, :, None], 0.0), axis=1
+    ).astype(jnp.bfloat16)
+    x_own = gathered(jnp.concatenate([tokens, gate_table], axis=1), steps)
+    x_other = swap(x_own, core_swap)
+    cot_own = gathered(cotangent, steps)
+    cot_other = swap(cot_own, core_swap)
+    gate_mat = lax.dynamic_slice_in_dim(w_gate[0], part * hidden_units, hidden_units, 0)
+    up_mat = lax.dynamic_slice_in_dim(w_up[0], part * hidden_units, hidden_units, 0)
+    down_mat = lax.dynamic_slice_in_dim(w_down[0], part * hidden_units, hidden_units, 1)
+    column = jnp.arange(lanes, dtype=jnp.int32)[None, :] == mine
+    kept = []
+    for x_rows, cot_rows in ((x_own, cot_own), (x_other, cot_other)):
+        x_part = x_rows[:, :model_width]
+        gate_rows = jnp.sum(
+            jnp.where(column, x_rows[:, model_width:].astype(jnp.float32), 0.0),
+            axis=1,
+            keepdims=True,
+        )
+        pre_gate = contract_last(x_part, gate_mat)
+        pre_up = contract_last(x_part, up_mat)
+        gate_sigmoid = jax.nn.sigmoid(pre_gate)
+        hidden = pre_gate * gate_sigmoid * pre_up
+        raw = jnp.dot(cot_rows, down_mat, preferred_element_type=jnp.float32)
+        score = jnp.sum(hidden * raw, axis=1, keepdims=True)
+        d_hidden = gate_rows * raw
+        d_pre_gate = (
+            d_hidden * pre_up * gate_sigmoid * (1.0 + pre_gate * (1.0 - gate_sigmoid))
+        ).astype(jnp.bfloat16)
+        d_pre_up = (d_hidden * pre_gate * gate_sigmoid).astype(jnp.bfloat16)
+        slot_grad = (
+            jnp.dot(d_pre_gate, gate_mat, preferred_element_type=jnp.float32)
+            + jnp.dot(d_pre_up, up_mat, preferred_element_type=jnp.float32)
+        ).astype(jnp.bfloat16)
+        scores = jnp.where(column, score, 0.0).astype(jnp.bfloat16)
+        kept.append(
+            (
+                jnp.concatenate([slot_grad, scores], axis=1),
+                d_pre_gate,
+                d_pre_up,
+                (gate_rows * hidden).astype(jnp.bfloat16),
+            )
+        )
+    partial = added(kept[0][0], swap(kept[1][0], core_swap))
+    result = scattered(partial, steps)
+    token_grad = result[:, :model_width]
+    gate_grad = jnp.sum(
+        jnp.where(named, result[:, model_width:].astype(jnp.float32)[:, None, :], 0.0), axis=2
+    ).astype(jnp.bfloat16)
+    grads = []
+    for place, (own, other) in (
+        (1, (x_own, x_other)),
+        (2, (x_own, x_other)),
+        (3, (cot_own, cot_other)),
+    ):
+        total = contract_first(kept[0][place], own[:, :model_width]) + contract_first(
+            kept[1][place], other[:, :model_width]
+        )
+        grads.append(total.astype(jnp.bfloat16)[None])
+    return (token_grad, gate_grad, *grads)
+
+
+def body(tokens, expert_ids, *rest):
+    tok_rows, top_count = expert_ids.shape
+    if 2 * tok_rows * top_count // lax.axis_size("expert") < tok_rows:
+        return routed_body(tokens, expert_ids, *rest)
+    return dense_body(tokens, expert_ids, *rest)
+
+
 def solution(mesh):
     return jax.shard_map(
         body,

time: 287 us -> 137 us (0.48)
  the two profiles are of different devices: /device:TPU:13 before, /device:TPU:0 now
where the time goes in v1:
time: 137 us
  waiting for transfers between devices  50.9 us (37%)
  matrix products  41.1 us (30%)
  starting transfers between devices  26.3 us (19%)
  local copies, waits for them, and re-layouts  10.7 us (8%)
  other arithmetic  6.57 us (5%)
    ppermute x15, waiting for transfers between devices, swap(): return lax.ppermute(value, BOTH, list(enumerate(partners)))  50.9 us
    ppermute x15, starting transfers between devices, swap(): return lax.ppermute(value, BOTH, list(enumerate(partners)))  26.3 us
    dot_general x6, matrix products, contract_first(): lax.dot_general(left, right, (((0,), (0,)), ((), ())), preferred_element_...  19 us
    dot_general x4, matrix products, contract_last(): lax.dot_general(left, right, (((1,), (1,)), ((), ())), preferred_element_...  10.7 us
    unnamed x21, local copies, waits for them, and re-layouts  6.85 us
    dot_general x2, matrix products, dense_body(): raw = jnp.dot(cot_rows, down_mat, preferred_element_type=jnp.float32)  5.94 us
    dot_general x2, matrix products, dense_body(): jnp.dot(d_pre_up, up_mat, preferred_element_type=jnp.float32)  2.9 us
  transfers between devices with their start and end apart: 15, of which 11 were waited for; matrix products, arithmetic and copies ran while one was open for 31% of the time, Pallas kernels for 0%

profile of v1, /device:TPU:0, one launch (start us, length us, event | category | flops | bytes accessed | tf_op | source)
XLA Modules:
  0.0 136.5 jit_solution(4246847849728515275)
XLA Ops:
  2.6 1.6 %pad_maximum_fusion.7 = (bf16[32,2176]{1,0:T(8,128)(2,1)S(1)}, bf16[512,2176]{1,0:T(8,128)(2,1)}) fusion(bf16[32,128]{1,0:T(8,128)(2,1)S(1)} %select_reduce_fusion.3, bf16[32,2048]{1,0:T(8,128)(2,1)} %param.7), kind=kLoop, calls=%fused_computation.77 | loop fusion | flops 278527 | bytes 417792 | tf_op jit(solution)/shard_map/concatenate | solution.py:154
  4.2 4.0 %collective-permute-start = (bf16[32,2176]{1,0:T(8,128)(2,1)S(1)}, bf16[32,2176]{1,0:T(8,128)(2,1)S(1)}, u32[]{:S(2)}, u32[]{:S(2)}) collective-permute-start(bf16[32,2176]{1,0:T(8,128)(2,1)S(1)} %get-tuple-element.18), channel_id=1, source_target_pairs={{0,16},{1,17},{2,18},{3,19},{4,20},{5,21},{6,22},{7,23},{8,24},{9,... | collective-permute-start | bytes 417800 | tf_op jit(solution)/shard_map/ppermute | solution.py:121
  8.2 6.7 %collective-permute-done = bf16[32,2176]{1,0:T(8,128)(2,1)S(1)} collective-permute-done((bf16[32,2176]{1,0:T(8,128)(2,1)S(1)}, bf16[32,2176]{1,0:T(8,128)(2,1)S(1)}, u32[]{:S(2)}, u32[]{:S(2)}) %collective-permute-start) | collective-permute-done | bytes 139296 | tf_op jit(solution)/shard_map/ppermute | solution.py:121
  16.6 3.4 %collective-permute-start.4 = (bf16[32,2048]{1,0:T(8,128)(2,1)}, bf16[32,2048]{1,0:T(8,128)(2,1)S(1)}, u32[]{:S(2)}, u32[]{:S(2)}) collective-permute-start(bf16[32,2048]{1,0:T(8,128)(2,1)} %param.10), channel_id=1, source_target_pairs={{0,16},{1,17},{2,18},{3,19},{4,20},{5,21},{6,22},{7,23},{8,24},{9,... | collective-permute-start | bytes 393224 | tf_op jit(solution)/shard_map/ppermute | solution.py:121
  20.0 6.5 %collective-permute-done.1 = bf16[64,2176]{1,0:T(8,128)(2,1)S(1)} collective-permute-done((bf16[64,2176]{1,0:T(8,128)(2,1)S(1)}, bf16[64,2176]{1,0:T(8,128)(2,1)S(1)}, u32[]{:S(2)}, u32[]{:S(2)}) %collective-permute-start.1) | collective-permute-done | bytes 278560 | tf_op jit(solution)/shard_map/ppermute | solution.py:121
  30.4 5.3 %collective-permute-done.5 = bf16[64,2048]{1,0:T(8,128)(2,1)S(1)} collective-permute-done((bf16[64,2048]{1,0:T(8,128)(2,1)S(1)}, bf16[64,2048]{1,0:T(8,128)(2,1)S(1)}, u32[]{:S(2)}, u32[]{:S(2)}) %collective-permute-start.5) | collective-permute-done | bytes 262176 | tf_op jit(solution)/shard_map/ppermute | solution.py:121
  35.7 1.6 %collective-permute-start.6 = (bf16[128,2048]{1,0:T(8,128)(2,1)S(1)}, bf16[128,2048]{1,0:T(8,128)(2,1)S(1)}, u32[]{:S(2)}, u32[]{:S(2)}) collective-permute-start(bf16[128,2048]{1,0:T(8,128)(2,1)S(1)} %pad_maximum_fusion.4), channel_id=1, source_target_pairs={{0,1},{1,0},{2,6},{3,7},{4,5},{5,4},{6,2},{7,3},{8,9},{9,8},{10,14... | collective-permute-start | bytes 1572872 | tf_op jit(solution)/shard_map/ppermute | solution.py:121
  37.4 1.6 %collective-permute-start.3 = (bf16[256,2176]{1,0:T(8,128)(2,1)S(1)}, bf16[256,2176]{1,0:T(8,128)(2,1)S(1)}, u32[]{:S(2)}, u32[]{:S(2)}) collective-permute-start(bf16[256,2176]{1,0:T(8,128)(2,1)S(1)} %pad_maximum_fusion.1), channel_id=1, source_target_pairs={{0,4},{1,5},{2,3},{3,2},{4,0},{5,1},{6,7},{7,6},{8,12},{9,13},{10,... | collective-permute-start | bytes 3342344 | tf_op jit(solution)/shard_map/ppermute | solution.py:121
  40.4 10.2 %collective-permute-done.6 = bf16[128,2048]{1,0:T(8,128)(2,1)S(1)} collective-permute-done((bf16[128,2048]{1,0:T(8,128)(2,1)S(1)}, bf16[128,2048]{1,0:T(8,128)(2,1)S(1)}, u32[]{:S(2)}, u32[]{:S(2)}) %collective-permute-start.6) | collective-permute-done | bytes 524320 | tf_op jit(solution)/shard_map/ppermute | solution.py:121
  50.7 1.6 %collective-permute-start.7 = (bf16[256,2048]{1,0:T(8,128)(2,1)S(1)}, bf16[256,2048]{1,0:T(8,128)(2,1)S(1)}, u32[]{:S(2)}, u32[]{:S(2)}) collective-permute-start(bf16[256,2048]{1,0:T(8,128)(2,1)S(1)} %pad_maximum_fusion.2), channel_id=1, source_target_pairs={{0,4},{1,5},{2,3},{3,2},{4,0},{5,1},{6,7},{7,6},{8,12},{9,13},{10,... | collective-permute-start | bytes 3145736 | tf_op jit(solution)/shard_map/ppermute | solution.py:121
  54.9 2.1 %collective-permute-start.8 = (bf16[512,2176]{1,0:T(8,128)(2,1)}, bf16[512,2176]{1,0:T(8,128)(2,1)}, u32[]{:S(2)}, u32[]{:S(2)}) collective-permute-start(bf16[512,2176]{1,0:T(8,128)(2,1)} %constant_dynamic-update-slice_fusion), channel_id=1, source_target_pairs={{0,2},{1,3},{2,0},{3,1},{4,6},{5,7},{6,4},{7,5},{8,10},{9,11},{10,... | collective-permute-start | bytes 6684680 | tf_op jit(solution)/shard_map/ppermute | solution.py:121
  59.2 6.4 %collective-permute-done.7 = bf16[256,2048]{1,0:T(8,128)(2,1)S(1)} collective-permute-done((bf16[256,2048]{1,0:T(8,128)(2,1)S(1)}, bf16[256,2048]{1,0:T(8,128)(2,1)S(1)}, u32[]{:S(2)}, u32[]{:S(2)}) %collective-permute-start.7) | collective-permute-done | bytes 1048608 | tf_op jit(solution)/shard_map/ppermute | solution.py:121
  67.9 2.8 %fusion.9 = f32[512,384]{0,1:T(8,128)S(1)} fusion(bf16[512,2176]{1,0:T(8,128)(2,1)} %constant_dynamic-update-slice_fusion, bf16[1,768,2048]{2,1,0:T(8,128)(2,1)S(1)} %copy-done, s32[]{:T(128)S(6)} %select_n.29), kind=kOutput, calls=%fused_computation.17 | convolution fusion | flops 805306368 | bytes 4456452 | tf_op jit(solution)/shard_map/dot_general | solution.py:10
  70.7 2.6 %fusion.15 = f32[512,384]{0,1:T(8,128)S(1)} fusion(bf16[512,2176]{1,0:T(8,128)(2,1)} %constant_dynamic-update-slice_fusion, bf16[1,768,2048]{2,1,0:T(8,128)(2,1)S(1)} %copy-done.2, s32[]{:T(128)S(6)} %select_n.29), kind=kOutput, calls=%fused_computation.23 | convolution fusion | flops 805306368 | bytes 4456452 | tf_op jit(solution)/shard_map/dot_general | solution.py:10
  74.4 2.6 %fusion.5 = f32[512,384]{0,1:T(8,128)S(1)} fusion(bf16[512,2176]{1,0:T(8,128)(2,1)} %collective-permute-done.8, bf16[1,768,2048]{2,1,0:T(8,128)(2,1)S(1)} %copy-done, s32[]{:T(128)S(6)} %select_n.29), kind=kOutput, calls=%fused_computation.13 | convolution fusion | flops 805306368 | bytes 4456452 | tf_op jit(solution)/shard_map/dot_general | solution.py:10
  77.0 2.8 %fusion.12 = f32[512,384]{0,1:T(8,128)S(1)} fusion(bf16[512,2176]{1,0:T(8,128)(2,1)} %collective-permute-done.8, bf16[1,768,2048]{2,1,0:T(8,128)(2,1)S(1)} %copy-done.2, s32[]{:T(128)S(6)} %select_n.29), kind=kOutput, calls=%fused_computation.20 | convolution fusion | flops 805306368 | bytes 4456452 | tf_op jit(solution)/shard_map/dot_general | solution.py:10
  79.8 3.0 %multiply_convert_fusion.3 = (bf16[512,384]{0,1:T(8,128)(2,1)S(1)}, bf16[512]{0:T(512)(128)(2,1)S(1)}, bf16[512,384]{0,1:T(8,128)(2,1)S(1)}) fusion(f32[512,384]{0,1:T(8,128)S(1)} %fusion.5, f32[512,384]{0,1:T(8,128)S(1)} %fusion.12, f32[512]{0:T(512)S(1)} %get-tuple-element.11, bf16[512,2048]{1,0:T(8,128)(2,1)} %collective-permute-done.9, ...), kind=kOutput, calls=%fused_computation.57 | convolution fusion | flops 808844800 | bytes 6032388 | tf_op jit(solution)/shard_map/dot_general | solution.py:174
  84.1 3.0 %multiply_convert_fusion.5 = (bf16[512,384]{0,1:T(8,128)(2,1)S(1)}, bf16[512]{0:T(512)(128)(2,1)S(1)}, bf16[512,384]{0,1:T(8,128)(2,1)S(1)}) fusion(f32[512,384]{0,1:T(8,128)S(1)} %fusion.9, f32[512,384]{0,1:T(8,128)S(1)} %fusion.15, f32[512]{0:T(512)S(1)} %get-tuple-element.10, bf16[512,2048]{1,0:T(8,128)(2,1)} %constant_dynamic-update-slice_fusion.5, ...), kind=kOutput, calls=%fused_computation.62 | convolution fusion | flops 808844800 | bytes 6032388 | tf_op jit(solution)/shard_map/dot_general | solution.py:174
  90.2 1.6 %add_convert_fusion.2 = bf16[512,2048]{1,0:T(8,128)(2,1)S(1)} fusion(f32[512,2048]{1,0:T(8,128)S(1)} %fusion.7, bf16[512,384]{0,1:T(8,128)(2,1)S(1)} %get-tuple-element.16, bf16[1,768,2048]{2,1,0:T(8,128)(2,1)S(1)} %copy-done.2, s32[]{:T(128)S(6)} %select_n.29), kind=kOutput, calls=%fused_computation.2 | convolution fusion | flops 807403520 | bytes 8257540 | tf_op jit(solution)/shard_map/dot_general | solution.py:183
  91.7 1.5 %collective-permute-done.10 = bf16[512,2176]{1,0:T(8,128)(2,1)S(1)} collective-permute-done((bf16[512,2176]{1,0:T(8,128)(2,1)S(1)}, bf16[512,2176]{1,0:T(8,128)(2,1)S(1)}, u32[]{:S(2)}, u32[]{:S(2)}) %collective-permute-start.10) | collective-permute-done | bytes 2228256 | tf_op jit(solution)/shard_map/ppermute | solution.py:121
  94.4 2.6 %fusion.25 = f32[384,2048]{1,0:T(8,128)S(1)} fusion(bf16[512,384]{0,1:T(8,128)(2,1)S(1)} %get-tuple-element.14, bf16[512,2176]{1,0:T(8,128)(2,1)} %collective-permute-done.8), kind=kOutput, calls=%fused_computation.33 | convolution fusion | flops 805306368 | bytes 5636096 | tf_op jit(solution)/shard_map/dot_general | solution.py:16
  97.0 3.7 %fusion = bf16[1,384,2048]{2,1,0:T(8,128)(2,1)} fusion(f32[384,2048]{1,0:T(8,128)S(1)} %fusion.25, bf16[512,384]{0,1:T(8,128)(2,1)S(1)} %get-tuple-element.12, bf16[512,2176]{1,0:T(8,128)(2,1)} %constant_dynamic-update-slice_fusion), kind=kOutput, calls=%fused_computation.6 | convolution fusion | flops 806879232 | bytes 7208960 | tf_op jit(solution)/shard_map/dot_general | solution.py:16
  100.7 8.7 %collective-permute-done.11 = bf16[256,2176]{1,0:T(8,128)(2,1)S(1)} collective-permute-done((bf16[256,2176]{1,0:T(8,128)(2,1)S(1)}, bf16[256,2176]{1,0:T(8,128)(2,1)S(1)}, u32[]{:S(2)}, u32[]{:S(2)}) %collective-permute-start.11) | collective-permute-done | bytes 1114144 | tf_op jit(solution)/shard_map/ppermute | solution.py:121
  109.7 1.8 %collective-permute-start.12 = (bf16[128,2176]{1,0:T(8,128)(2,1)S(1)}, bf16[128,2176]{1,0:T(8,128)(2,1)S(1)}, u32[]{:S(2)}, u32[]{:S(2)}) collective-permute-start(bf16[128,2176]{1,0:T(8,128)(2,1)S(1)} %slice.67), channel_id=1, source_target_pairs={{0,1},{1,0},{2,6},{3,7},{4,5},{5,4},{6,2},{7,3},{8,9},{9,8},{10,14... | collective-permute-start | bytes 1671176 | tf_op jit(solution)/shard_map/ppermute | solution.py:121
  111.5 2.6 %fusion.41 = f32[384,2048]{1,0:T(8,128)S(1)} fusion(bf16[512,2048]{1,0:T(8,128)(2,1)} %collective-permute-done.9, f32[512]{0:T(512)S(1)} %get-tuple-element.11, f32[512,384]{0,1:T(8,128)S(1)} %fusion.12, f32[512,384]{0,1:T(8,128)S(1)} %fusion.5), kind=kOutput, calls=%fused_computation.67 | convolution fusion | flops 806682624 | bytes 6817792 | tf_op jit(solution)/shard_map/dot_general | solution.py:16
  114.2 3.8 %fusion.2 = bf16[1,384,2048]{2,1,0:T(8,128)(2,1)} fusion(f32[384,2048]{1,0:T(8,128)S(1)} %fusion.41, bf16[512,2048]{1,0:T(8,128)(2,1)} %constant_dynamic-update-slice_fusion.5, f32[512]{0:T(512)S(1)} %get-tuple-element.10, f32[512,384]{0,1:T(8,128)S(1)} %fusion.15, f32[512,384]{0,1:T(8,128)S(1)} %fusion.9), kind=kOutput, calls=%fused_computation.8 | convolution fusion | flops 808255488 | bytes 8390656 | tf_op jit(solution)/shard_map/dot_general | solution.py:16
  117.9 1.4 collective-permute-done.12
  119.5 2.0 %collective-permute-start.13 = (bf16[64,2176]{1,0:T(8,128)(2,1)S(1)}, bf16[64,2176]{1,0:T(8,128)(2,1)S(1)}, u32[]{:S(2)}, u32[]{:S(2)}) collective-permute-start(bf16[64,2176]{1,0:T(8,128)(2,1)S(1)} %slice.69), channel_id=1, source_target_pairs={{0,8},{1,9},{2,10},{3,11},{4,12},{5,13},{6,14},{7,15},{8,0},{9,1},... | collective-permute-start | bytes 835592 | tf_op jit(solution)/shard_map/ppermute | solution.py:121
  121.5 2.6 %fusion.23 = f32[384,2048]{1,0:T(8,128)S(1)} fusion(bf16[512,384]{0,1:T(8,128)(2,1)S(1)} %get-tuple-element.17, bf16[512,2176]{1,0:T(8,128)(2,1)} %collective-permute-done.8), kind=kOutput, calls=%fused_computation.31 | convolution fusion | flops 805306368 | bytes 5636096 | tf_op jit(solution)/shard_map/dot_general | solution.py:16
  124.1 2.7 %collective-permute-done.13 = bf16[64,2176]{1,0:T(8,128)(2,1)S(1)} collective-permute-done((bf16[64,2176]{1,0:T(8,128)(2,1)S(1)}, bf16[64,2176]{1,0:T(8,128)(2,1)S(1)}, u32[]{:S(2)}, u32[]{:S(2)}) %collective-permute-start.13) | collective-permute-done | bytes 278560 | tf_op jit(solution)/shard_map/ppermute | solution.py:121
  126.8 3.4 %collective-permute-start.14 = (bf16[32,2176]{1,0:T(8,128)(2,1)S(1)}, bf16[32,2176]{1,0:T(8,128)(2,1)S(1)}, u32[]{:S(2)}, u32[]{:S(2)}) collective-permute-start(bf16[32,2176]{1,0:T(8,128)(2,1)S(1)} %slice.71), channel_id=1, source_target_pairs={{0,16},{1,17},{2,18},{3,19},{4,20},{5,21},{6,22},{7,23},{8,24},{9,... | collective-permute-start | bytes 417800 | tf_op jit(solution)/shard_map/ppermute | solution.py:121
  130.3 3.7 %fusion.1 = bf16[1,384,2048]{2,1,0:T(8,128)(2,1)} fusion(f32[384,2048]{1,0:T(8,128)S(1)} %fusion.23, bf16[512,384]{0,1:T(8,128)(2,1)S(1)} %get-tuple-element.16, bf16[512,2176]{1,0:T(8,128)(2,1)} %constant_dynamic-update-slice_fusion), kind=kOutput, calls=%fused_computation.7 | convolution fusion | flops 806879232 | bytes 7208960 | tf_op jit(solution)/shard_map/dot_general | solution.py:16
  (62 shorter events, 26.0 us)
Async XLA Ops:
  0.6 67.3 %copy-start = (bf16[1,768,2048]{2,1,0:T(8,128)(2,1)S(1)}, bf16[1,768,2048]{2,1,0:T(8,128)(2,1)}, u32[]{:S(2)}) copy-start(bf16[1,768,2048]{2,1,0:T(8,128)(2,1)} %param.11) | copy-start | bytes 9437188
  0.6 36.7 %copy-start.3 = (bf16[32,2048]{1,0:T(8,128)(2,1)S(1)}, bf16[32,2048]{1,0:T(8,128)(2,1)}, u32[]{:S(2)}) copy-start(bf16[32,2048]{1,0:T(8,128)(2,1)} %param.7) | copy-start | bytes 393220
  0.7 28.2 %copy-start.4 = (bf16[32,2048]{1,0:T(8,128)(2,1)S(1)}, bf16[32,2048]{1,0:T(8,128)(2,1)}, u32[]{:S(2)}) copy-start(bf16[32,2048]{1,0:T(8,128)(2,1)} %param.10) | copy-start | bytes 393220
  4.2 10.7 %collective-permute-start = (bf16[32,2176]{1,0:T(8,128)(2,1)S(1)}, bf16[32,2176]{1,0:T(8,128)(2,1)S(1)}, u32[]{:S(2)}, u32[]{:S(2)}) collective-permute-start(bf16[32,2176]{1,0:T(8,128)(2,1)S(1)} %get-tuple-element.18), channel_id=1, source_target_pairs={{0,16},{1,17},{2,18},{3,19},{4,20},{5,21},{6,22},{7,23},{8,24},{9,... | collective-permute-start | bytes 417800 | tf_op jit(solution)/shard_map/ppermute | solution.py:121
  15.8 10.7 %collective-permute-start.1 = (bf16[64,2176]{1,0:T(8,128)(2,1)S(1)}, bf16[64,2176]{1,0:T(8,128)(2,1)S(1)}, u32[]{:S(2)}, u32[]{:S(2)}) collective-permute-start(bf16[64,2176]{1,0:T(8,128)(2,1)S(1)} %pad_maximum_fusion.5), channel_id=1, source_target_pairs={{0,8},{1,9},{2,10},{3,11},{4,12},{5,13},{6,14},{7,15},{8,0},{9,1},... | collective-permute-start | bytes 835592 | tf_op jit(solution)/shard_map/ppermute | solution.py:121
  16.6 12.2 %collective-permute-start.4 = (bf16[32,2048]{1,0:T(8,128)(2,1)}, bf16[32,2048]{1,0:T(8,128)(2,1)S(1)}, u32[]{:S(2)}, u32[]{:S(2)}) collective-permute-start(bf16[32,2048]{1,0:T(8,128)(2,1)} %param.10), channel_id=1, source_target_pairs={{0,16},{1,17},{2,18},{3,19},{4,20},{5,21},{6,22},{7,23},{8,24},{9,... | collective-permute-start | bytes 393224 | tf_op jit(solution)/shard_map/ppermute | solution.py:121
  27.5 9.8 %collective-permute-start.2 = (bf16[128,2176]{1,0:T(8,128)(2,1)S(1)}, bf16[128,2176]{1,0:T(8,128)(2,1)S(1)}, u32[]{:S(2)}, u32[]{:S(2)}) collective-permute-start(bf16[128,2176]{1,0:T(8,128)(2,1)S(1)} %pad_maximum_fusion.3), channel_id=1, source_target_pairs={{0,1},{1,0},{2,6},{3,7},{4,5},{5,4},{6,2},{7,3},{8,9},{9,8},{10,14... | collective-permute-start | bytes 1671176 | tf_op jit(solution)/shard_map/ppermute | solution.py:121
  28.9 6.8 %collective-permute-start.5 = (bf16[64,2048]{1,0:T(8,128)(2,1)S(1)}, bf16[64,2048]{1,0:T(8,128)(2,1)S(1)}, u32[]{:S(2)}, u32[]{:S(2)}) collective-permute-start(bf16[64,2048]{1,0:T(8,128)(2,1)S(1)} %pad_maximum_fusion.6), channel_id=1, source_target_pairs={{0,8},{1,9},{2,10},{3,11},{4,12},{5,13},{6,14},{7,15},{8,0},{9,1},... | collective-permute-start | bytes 786440 | tf_op jit(solution)/shard_map/ppermute | solution.py:121
  35.7 14.9 %collective-permute-start.6 = (bf16[128,2048]{1,0:T(8,128)(2,1)S(1)}, bf16[128,2048]{1,0:T(8,128)(2,1)S(1)}, u32[]{:S(2)}, u32[]{:S(2)}) collective-permute-start(bf16[128,2048]{1,0:T(8,128)(2,1)S(1)} %pad_maximum_fusion.4), channel_id=1, source_target_pairs={{0,1},{1,0},{2,6},{3,7},{4,5},{5,4},{6,2},{7,3},{8,9},{9,8},{10,14... | collective-permute-start | bytes 1572872 | tf_op jit(solution)/shard_map/ppermute | solution.py:121
  37.4 16.4 %collective-permute-start.3 = (bf16[256,2176]{1,0:T(8,128)(2,1)S(1)}, bf16[256,2176]{1,0:T(8,128)(2,1)S(1)}, u32[]{:S(2)}, u32[]{:S(2)}) collective-permute-start(bf16[256,2176]{1,0:T(8,128)(2,1)S(1)} %pad_maximum_fusion.1), channel_id=1, source_target_pairs={{0,4},{1,5},{2,3},{3,2},{4,0},{5,1},{6,7},{7,6},{8,12},{9,13},{10,... | collective-permute-start | bytes 3342344 | tf_op jit(solution)/shard_map/ppermute | solution.py:121
  50.7 14.9 %collective-permute-start.7 = (bf16[256,2048]{1,0:T(8,128)(2,1)S(1)}, bf16[256,2048]{1,0:T(8,128)(2,1)S(1)}, u32[]{:S(2)}, u32[]{:S(2)}) collective-permute-start(bf16[256,2048]{1,0:T(8,128)(2,1)S(1)} %pad_maximum_fusion.2), channel_id=1, source_target_pairs={{0,4},{1,5},{2,3},{3,2},{4,0},{5,1},{6,7},{7,6},{8,12},{9,13},{10,... | collective-permute-start | bytes 3145736 | tf_op jit(solution)/shard_map/ppermute | solution.py:121
  54.9 18.4 %collective-permute-start.8 = (bf16[512,2176]{1,0:T(8,128)(2,1)}, bf16[512,2176]{1,0:T(8,128)(2,1)}, u32[]{:S(2)}, u32[]{:S(2)}) collective-permute-start(bf16[512,2176]{1,0:T(8,128)(2,1)} %constant_dynamic-update-slice_fusion), channel_id=1, source_target_pairs={{0,2},{1,3},{2,0},{3,1},{4,6},{5,7},{6,4},{7,5},{8,10},{9,11},{10,... | collective-permute-start | bytes 6684680 | tf_op jit(solution)/shard_map/ppermute | solution.py:121
  66.7 13.1 %collective-permute-start.9 = (bf16[512,2048]{1,0:T(8,128)(2,1)}, bf16[512,2048]{1,0:T(8,128)(2,1)}, u32[]{:S(2)}, u32[]{:S(2)}) collective-permute-start(bf16[512,2048]{1,0:T(8,128)(2,1)} %constant_dynamic-update-slice_fusion.5), channel_id=1, source_target_pairs={{0,2},{1,3},{2,0},{3,1},{4,6},{5,7},{6,4},{7,5},{8,10},{9,11},{10,... | collective-permute-start | bytes 6291464 | tf_op jit(solution)/shard_map/ppermute | solution.py:121
  67.9 2.8 %copy-start.2 = (bf16[1,768,2048]{2,1,0:T(8,128)(2,1)S(1)}, bf16[1,768,2048]{2,1,0:T(8,128)(2,1)}, u32[]{:S(2)}) copy-start(bf16[1,768,2048]{2,1,0:T(8,128)(2,1)} %param.12) | copy-start | bytes 9437188
  77.0 2.8 %copy-start.5 = (bf16[1,2048,768]{2,1,0:T(8,128)(2,1)S(1)}, bf16[1,2048,768]{2,1,0:T(8,128)(2,1)}, u32[]{:S(2)}) copy-start(bf16[1,2048,768]{2,1,0:T(8,128)(2,1)} %param.13) | copy-start | bytes 9437188
  88.8 4.4 %collective-permute-start.10 = (bf16[512,2176]{1,0:T(8,128)(2,1)S(1)}, bf16[512,2176]{1,0:T(8,128)(2,1)S(1)}, u32[]{:S(2)}, u32[]{:S(2)}) collective-permute-start(bf16[512,2176]{1,0:T(8,128)(2,1)S(1)} %pad_maximum_fusion), channel_id=1, source_target_pairs={{0,2},{1,3},{2,0},{3,1},{4,6},{5,7},{6,4},{7,5},{8,10},{9,11},{10,... | collective-permute-start | bytes 6684680 | tf_op jit(solution)/shard_map/ppermute | solution.py:121
  93.8 15.6 %collective-permute-start.11 = (bf16[256,2176]{1,0:T(8,128)(2,1)S(1)}, bf16[256,2176]{1,0:T(8,128)(2,1)S(1)}, u32[]{:S(2)}, u32[]{:S(2)}) collective-permute-start(bf16[256,2176]{1,0:T(8,128)(2,1)S(1)} %slice.65), channel_id=1, source_target_pairs={{0,4},{1,5},{2,3},{3,2},{4,0},{5,1},{6,7},{7,6},{8,12},{9,13},{10,... | collective-permute-start | bytes 3342344 | tf_op jit(solution)/shard_map/ppermute | solution.py:121
  109.7 9.6 %collective-permute-start.12 = (bf16[128,2176]{1,0:T(8,128)(2,1)S(1)}, bf16[128,2176]{1,0:T(8,128)(2,1)S(1)}, u32[]{:S(2)}, u32[]{:S(2)}) collective-permute-start(bf16[128,2176]{1,0:T(8,128)(2,1)S(1)} %slice.67), channel_id=1, source_target_pairs={{0,1},{1,0},{2,6},{3,7},{4,5},{5,4},{6,2},{7,3},{8,9},{9,8},{10,14... | collective-permute-start | bytes 1671176 | tf_op jit(solution)/shard_map/ppermute | solution.py:121
  119.5 7.3 %collective-permute-start.13 = (bf16[64,2176]{1,0:T(8,128)(2,1)S(1)}, bf16[64,2176]{1,0:T(8,128)(2,1)S(1)}, u32[]{:S(2)}, u32[]{:S(2)}) collective-permute-start(bf16[64,2176]{1,0:T(8,128)(2,1)S(1)} %slice.69), channel_id=1, source_target_pairs={{0,8},{1,9},{2,10},{3,11},{4,12},{5,13},{6,14},{7,15},{8,0},{9,1},... | collective-permute-start | bytes 835592 | tf_op jit(solution)/shard_map/ppermute | solution.py:121
  126.8 9.7 %copy-start.1 = (bf16[1,768,2048]{2,1,0:T(8,128)(2,1)S(1)}, bf16[1,768,2048]{2,1,0:T(8,128)(2,1)}, u32[]{:S(2)}) copy-start(bf16[1,768,2048]{2,1,0:T(8,128)(2,1)} %param.11) | copy-start | bytes 9437188
  126.8 8.1 %collective-permute-start.14 = (bf16[32,2176]{1,0:T(8,128)(2,1)S(1)}, bf16[32,2176]{1,0:T(8,128)(2,1)S(1)}, u32[]{:S(2)}, u32[]{:S(2)}) collective-permute-start(bf16[32,2176]{1,0:T(8,128)(2,1)S(1)} %slice.71), channel_id=1, source_target_pairs={{0,16},{1,17},{2,18},{3,19},{4,20},{5,21},{6,22},{7,23},{8,24},{9,... | collective-permute-start | bytes 417800 | tf_op jit(solution)/shard_map/ppermute | solution.py:121

commit v2 on v0

--- a/solution.py
+++ b/solution.py
@@ -1,7 +1,14 @@
+import functools
+
 import jax
 import jax.numpy as jnp
 from jax import lax
+from jax.experimental import pallas as pl
+from jax.experimental.pallas import tpu as pltpu
 from jax.sharding import PartitionSpec as P
+
+TILE = 256
+BOTH = ("expert", "dp")
 
 
 def contract_last(left, right):
@@ -29,7 +36,7 @@
     return (pre_gate, pre_up, gate_sigmoid, hidden, outputs)
 
 
-def body(tokens, expert_ids, gate_weights, cotangent, w_gate, w_up, w_down):
+def routed_body(tokens, expert_ids, gate_weights, cotangent, w_gate, w_up, w_down):
     tok_rows, top_count = expert_ids.shape
     model_width = tokens.shape[1]
     experts = lax.axis_size("expert")
@@ -103,6 +110,385 @@
     return (token_grad, gate_grad, grad_gate, grad_up, grad_down_t)
 
 
+def swap(value, flip):
+    count = lax.axis_size(BOTH)
+    return lax.ppermute(value, BOTH, [(i, i ^ flip) for i in range(count)])
+
+
+def added(*terms):
+    return sum(term.astype(jnp.float32) for term in terms).astype(jnp.bfloat16)
+
+
+def tied(*values):
+    return lax.optimization_barrier(values)
+
+
+def kernel_params(flops, moved, transcendentals=0, megabytes=14):
+    return {
+        "compiler_params": pltpu.CompilerParams(vmem_limit_bytes=megabytes * 1024 * 1024),
+        "cost_estimate": pl.CostEstimate(
+            flops=flops, bytes_accessed=moved, transcendentals=transcendentals
+        ),
+    }
+
+
+IN_HBM = pl.BlockSpec(memory_space=pl.ANY)
+IN_VMEM = pl.BlockSpec(memory_space=pltpu.VMEM)
+IN_SMEM = pl.BlockSpec(memory_space=pltpu.SMEM)
+
+
+def kept(value):
+    return pltpu.with_memory_space_constraint(value, pltpu.VMEM)
+
+
+def left_out(value):
+    return pltpu.with_memory_space_constraint(value, pltpu.HBM)
+
+
+def fetched(pairs, sems):
+    copies = [pltpu.make_async_copy(src, dst, sems.at[i]) for i, (src, dst) in enumerate(pairs)]
+    for copy in copies:
+        copy.start()
+    return copies
+
+
+def placed(pieces, target):
+    pairs, first = [], 0
+    for piece in pieces:
+        pairs.append((piece, target.at[pl.ds(first, piece.shape[0])]))
+        first += piece.shape[0]
+    return pairs
+
+
+def forward_kernel(*refs):
+    pieces, weight_refs, weight_outs, sems = refs[:4], refs[4:7], refs[7:10], refs[-1]
+    rows_out, slope_out, swish_out, hidden_out = refs[10:14]
+    units = slope_out.shape[1]
+    pairs = placed(pieces, rows_out)
+    for start in range(0, units, TILE):
+        for i in range(2):
+            rows = pl.ds(start, TILE)
+            pairs.append((weight_refs[i].at[0, rows], weight_outs[i].at[rows]))
+    half = weight_outs[2].shape[0] // 2
+    for i in range(2):
+        rows = pl.ds(i * half, half)
+        pairs.append((weight_refs[2].at[0, rows], weight_outs[2].at[rows]))
+    copies = fetched(pairs, sems)
+    for copy in copies[:4]:
+        copy.wait()
+    for step, start in enumerate(range(0, units, TILE)):
+        for copy in copies[4 + 2 * step : 6 + 2 * step]:
+            copy.wait()
+        rows = rows_out[...]
+        chunk = slice(start, start + TILE)
+        pre_gate = contract_last(rows, weight_outs[0][chunk])
+        pre_up = contract_last(rows, weight_outs[1][chunk])
+        gate_sigmoid = jax.nn.sigmoid(pre_gate)
+        swish = pre_gate * gate_sigmoid
+        slope_out[:, chunk] = pre_up * gate_sigmoid * (1.0 + pre_gate * (1.0 - gate_sigmoid))
+        swish_out[:, chunk] = swish
+        hidden_out[:, chunk] = swish * pre_up
+    for copy in copies[-2:]:
+        copy.wait()
+
+
+def forward(pieces, weights):
+    _, units, width = weights[0].shape
+    rows = sum(piece.shape[0] for piece in pieces)
+    outs = [pltpu.VMEM((rows, units), jnp.float32)] * 3
+    for shape in ((rows, width), (width, units), (units, width), (units, width)):
+        outs.insert(0, pltpu.VMEM(shape, jnp.bfloat16))
+    return pl.pallas_call(
+        forward_kernel,
+        in_specs=[IN_HBM] * 7,
+        out_specs=[IN_VMEM] * 7,
+        out_shape=outs,
+        scratch_shapes=[pltpu.SemaphoreType.DMA((6 + 2 * (units // TILE),))],
+        **kernel_params(4 * rows * units * width, 2 * rows * width, rows * units),
+    )(*[left_out(value) for value in (*pieces, *weights)])
+
+
+def backward_kernel(
+    which,
+    place_ref,
+    own_ref,
+    other_ref,
+    slope_ref,
+    swish_ref,
+    hidden_ref,
+    gate_ref,
+    up_ref,
+    down_ref,
+    _,
+    own_out,
+    other_out,
+    rows_out,
+    lefts_out,
+    token_out,
+    sems,
+):
+    width, units = down_ref.shape
+    half = own_ref.shape[0]
+    lanes = own_ref.shape[1] - width
+    copies = fetched(placed((own_ref, other_ref), rows_out), sems)
+    token_out[...] = jnp.zeros_like(token_out)
+    for copy in copies:
+        copy.wait()
+    saved = pl.ds(which * 2 * half, 2 * half)
+    column = lax.broadcasted_iota(jnp.int32, (2 * half, lanes), 1) == place_ref[0]
+    table = rows_out[:, width:].astype(jnp.float32)
+    gates = jnp.sum(jnp.where(column, table, 0.0), axis=1, keepdims=True)
+    score = jnp.zeros((2 * half, 1), jnp.float32)
+    for start in range(0, units, TILE):
+        chunk = slice(start, start + TILE)
+        raw = jnp.dot(
+            rows_out[:, :width], down_ref[:, chunk], preferred_element_type=jnp.float32
+        )
+        hidden = hidden_ref[saved, chunk]
+        score += jnp.sum(hidden * raw, axis=1, keepdims=True)
+        d_hidden = gates * raw
+        lefts_out[:, chunk] = (d_hidden * slope_ref[saved, chunk]).astype(jnp.bfloat16)
+        lefts_out[:, units + start : units + start + TILE] = (
+            d_hidden * swish_ref[saved, chunk]
+        ).astype(jnp.bfloat16)
+        lefts_out[:, 2 * units + start : 2 * units + start + TILE] = (gates * hidden).astype(
+            jnp.bfloat16
+        )
+    scores = jnp.where(column, score, 0.0).astype(jnp.bfloat16)
+    own_out[:, width:] = scores[:half]
+    other_out[:, width:] = scores[half:]
+    for start in range(0, width, 2 * TILE):
+        chunk = slice(start, start + 2 * TILE)
+        total = (
+            jnp.dot(lefts_out[:, :units], gate_ref[:, chunk], preferred_element_type=jnp.float32)
+            + jnp.dot(
+                lefts_out[:, units : 2 * units],
+                up_ref[:, chunk],
+                preferred_element_type=jnp.float32,
+            )
+        ).astype(jnp.bfloat16)
+        own_out[:, chunk] = total[:half]
+        other_out[:, chunk] = total[half:]
+
+
+def backward(place, own, other, saved, which, weights, after):
+    units, width = weights[0].shape
+    half, packed = own.shape
+    rows = 2 * half
+    return pl.pallas_call(
+        functools.partial(backward_kernel, which),
+        in_specs=[IN_SMEM] + [IN_HBM] * 2 + [IN_VMEM] * 6 + [IN_HBM],
+        out_specs=[IN_VMEM] * 5,
+        out_shape=[
+            jax.ShapeDtypeStruct((half, packed), jnp.bfloat16),
+            jax.ShapeDtypeStruct((half, packed), jnp.bfloat16),
+            pltpu.VMEM((rows, packed), jnp.bfloat16),
+            pltpu.VMEM((rows, 3 * units), jnp.bfloat16),
+            jax.ShapeDtypeStruct((8, 128), jnp.float32),
+        ],
+        scratch_shapes=[pltpu.SemaphoreType.DMA((2,))],
+        **kernel_params(0, 0),
+    )(place, own, other, *[kept(value) for value in (*saved, *weights)], after)
+
+
+def own_gradient_kernel(place_ref, column_ref, near_ref, x_ref, column_cot, near_cot, *refs):
+    outs, token_out, lefts = refs[:3], refs[3], refs[4]
+    share, tile = outs[0].shape
+    units = column_ref.shape[1] // 3
+
+    @pl.when(pl.program_id(0) == 0)
+    def _():
+        token_out[...] = jnp.zeros_like(token_out)
+        start = pl.multiple_of(place_ref[1] * share, 128)
+        for i in range(3):
+            lefts[i] = jnp.concatenate(
+                [ref[:, pl.ds(start + i * units, share)] for ref in (column_ref, near_ref)], axis=0
+            ).T
+
+    chunk = pl.ds(pl.multiple_of(pl.program_id(0) * tile, tile), tile)
+    cot_rows = jnp.concatenate([column_cot[:, chunk], near_cot[:, chunk]], axis=0)
+    for i, rows in enumerate((x_ref[:, chunk], x_ref[:, chunk], cot_rows)):
+        outs[i][...] = jnp.dot(lefts[i], rows, preferred_element_type=jnp.float32).astype(
+            jnp.bfloat16
+        )
+
+
+def own_gradients(place, lefts, x_rows, cot_rows, share):
+    rows, width = x_rows.shape
+    tile = 2 * TILE
+    return pl.pallas_call(
+        own_gradient_kernel,
+        grid=(width // tile,),
+        in_specs=[IN_SMEM] + [IN_VMEM] * 5,
+        out_specs=[pl.BlockSpec((share, tile), lambda i: (0, i))] * 3
+        + [pl.BlockSpec((8, 128), lambda i: (0, 0))],
+        out_shape=[jax.ShapeDtypeStruct((share, width), jnp.bfloat16)] * 3
+        + [jax.ShapeDtypeStruct((8, 128), jnp.float32)],
+        scratch_shapes=[pltpu.VMEM((3, share, rows), jnp.bfloat16)],
+        **kernel_params(6 * rows * share * width, 6 * share * width),
+    )(place, *[kept(value) for value in (*lefts, x_rows, *cot_rows)])
+
+
+def whole_gradient_kernel(place_ref, *refs):
+    x_refs, cot_refs, weight_refs, own_refs = refs[:6], refs[6:14], refs[14:17], refs[17:20]
+    outs, (rows, cot, gate_ref, up_ref, down_ref, lefts, sems) = refs[21:24], refs[24:]
+    share, tile = outs[0].shape[1:]
+    width = rows.shape[1]
+
+    @pl.when(pl.program_id(0) == 0)
+    def _():
+        own = pl.ds(pl.multiple_of(place_ref[1] * share, 128), share)
+        copies = fetched(
+            placed(x_refs, rows)
+            + [(weight_refs[0].at[0, own], gate_ref), (weight_refs[1].at[0, own], up_ref)]
+            + placed(cot_refs, cot)
+            + [(weight_refs[2].at[0, :, own], down_ref)],
+            sems,
+        )
+        for copy in copies[:8]:
+            copy.wait()
+        pre_gate = contract_last(gate_ref[...], rows[...])
+        pre_up = contract_last(up_ref[...], rows[...])
+        gate_sigmoid = jax.nn.sigmoid(pre_gate)
+        swish = pre_gate * gate_sigmoid
+        for copy in copies[8:]:
+            copy.wait()
+        table = cot[:, width:]
+        pick = (lax.broadcasted_iota(jnp.int32, (16, table.shape[1]), 1) == place_ref[0]).astype(
+            jnp.bfloat16
+        )
+        gates = contract_last(pick, table)[:1]
+        raw = jnp.dot(cot[:, :width], down_ref[...], preferred_element_type=jnp.float32).T
+        d_hidden = gates * raw
+        lefts[0] = (
+            d_hidden * pre_up * gate_sigmoid * (1.0 + pre_gate * (1.0 - gate_sigmoid))
+        ).astype(jnp.bfloat16)
+        lefts[1] = (d_hidden * swish).astype(jnp.bfloat16)
+        lefts[2] = (gates * (swish * pre_up)).astype(jnp.bfloat16)
+
+    first = pl.multiple_of(pl.program_id(0) * tile, tile)
+    for i in range(3):
+        right = rows if i < 2 else cot
+        away = jnp.dot(lefts[i], right[:, pl.ds(first, tile)], preferred_element_type=jnp.float32)
+        outs[i][0] = (own_refs[i][...].astype(jnp.float32) + away).astype(jnp.bfloat16)
+
+
+def whole_gradients(place, x_rows, cot_rows, weights, own, after):
+    share, width = own[0].shape
+    tile = 2 * TILE
+    rows = sum(piece.shape[0] for piece in x_rows)
+    half = pltpu.VMEM((share, width), jnp.bfloat16)
+    return pl.pallas_call(
+        whole_gradient_kernel,
+        grid=(width // tile,),
+        in_specs=[IN_SMEM]
+        + [IN_HBM] * 17
+        + [pl.BlockSpec((share, tile), lambda i: (0, i))] * 3
+        + [IN_HBM],
+        out_specs=[pl.BlockSpec((1, share, tile), lambda i: (0, 0, i))] * 3,
+        out_shape=[jax.ShapeDtypeStruct((1, share, width), jnp.bfloat16)] * 3,
+        scratch_shapes=[
+            pltpu.VMEM((rows, width), jnp.bfloat16),
+            pltpu.VMEM((rows, cot_rows[0].shape[1]), jnp.bfloat16),
+            half,
+            half,
+            pltpu.VMEM((width, share), jnp.bfloat16),
+            pltpu.VMEM((3, share, rows), jnp.bfloat16),
+            pltpu.SemaphoreType.DMA((17,)),
+        ],
+        **kernel_params(
+            12 * rows * share * width, 4 * rows * width + 12 * share * width, rows * share, 32
+        ),
+    )(place, *[left_out(value) for value in (*x_rows, *cot_rows, *weights, *own)], after)
+
+
+def dense_body(tokens, expert_ids, gate_weights, cotangent, w_gate, w_up, w_down):
+    model_width = tokens.shape[1]
+    experts = lax.axis_size("expert")
+    groups = lax.axis_size("dp")
+    share = w_gate.shape[1] // groups
+    place = jnp.stack([lax.axis_index("expert"), lax.axis_index("dp")]).astype(jnp.int32)
+    group, core, near, low, high = 1, 2, 4, 8, 16
+    lanes = -(-experts // 128) * 128
+    named = expert_ids[:, :, None] == jnp.arange(lanes, dtype=jnp.int32)[None, None, :]
+    gate_table = jnp.sum(
+        jnp.where(named, gate_weights.astype(jnp.float32)[:, :, None], 0.0), axis=1
+    ).astype(jnp.bfloat16)
+
+    def column_of(value):
+        return [swap(value, high), swap(value, low | high), swap(value, low)]
+
+    weights = (w_gate, w_up, w_down)
+    packed = jnp.concatenate([cotangent, gate_table], axis=1)
+    x_mine_away, cot_mine_away = swap(tokens, group), swap(packed, group)
+    packed, x_mine_away, cot_mine_away, *x_far = tied(
+        packed, x_mine_away, cot_mine_away, *column_of(tokens)
+    )
+    x_far = jnp.concatenate(x_far, axis=0)
+    x_column = jnp.concatenate([tokens, x_far], axis=0)
+    x_near = swap(x_column, near)
+    x_far_away, x_near_away = swap(x_far, group), swap(x_near, group)
+    *cot_far, x_far_away = tied(*column_of(packed), x_far_away)
+    x_far_other = swap(x_far_away, core)
+    cot_column = jnp.concatenate([packed, *cot_far], axis=0)
+    cot_first_away = swap(cot_far[0], group)
+    cot_near = swap(cot_column, near)
+    *kept_weights, x_rows, slope, swish, hidden = forward(
+        [x_column, swap(x_column, core), x_near, swap(x_near, core)], weights
+    )
+    saved = (slope, swish, hidden)
+    own_part, other_part, column_cot, column_lefts, token = backward(
+        place, cot_column, swap(cot_column, core), saved, 0, kept_weights, place
+    )
+    column_partial = added(own_part, swap(other_part, core))
+    cot_near, token, x_near_away, x_far_other = tied(cot_near, token, x_near_away, x_far_other)
+    x_near_other = swap(x_near_away, core)
+    x_mine_other, cot_mine_other = swap(x_mine_away, core), swap(cot_mine_away, core)
+    cot_second_away = swap(jnp.concatenate(cot_far[1:], axis=0), group)
+    cot_near_away = swap(cot_near, group)
+    own_part, other_part, near_cot, near_lefts, _ = backward(
+        place, cot_near, swap(cot_near, core), saved, 1, kept_weights, token
+    )
+    other_part, cot_second_away, x_near_other, x_mine_other, cot_mine_other = tied(
+        other_part, cot_second_away, x_near_other, x_mine_other, cot_mine_other
+    )
+    cot_second_other = swap(cot_second_away, core)
+    near_partial = added(own_part, swap(other_part, core))
+    partial = added(column_partial, swap(near_partial, near))
+    *own, token = own_gradients(
+        place, [column_lefts, near_lefts], x_rows, [column_cot, near_cot], share
+    )
+    partial, cot_first_away, cot_near_away, cot_second_other, token = tied(
+        partial, cot_first_away, cot_near_away, cot_second_other, token
+    )
+    x_away = [x_mine_away, x_far_away, x_near_away, x_mine_other, x_far_other, x_near_other]
+    cot_away = [cot_mine_away, cot_first_away, cot_second_away, cot_near_away]
+    cot_away += [cot_mine_other, swap(cot_first_away, core), cot_second_other]
+    cot_away += [swap(cot_near_away, core)]
+    grads = list(whole_gradients(place, x_away, cot_away, weights, own, token))
+    block = partial.shape[0] // 4
+    parts = [
+        partial[:block],
+        swap(partial[block : 2 * block], high),
+        swap(partial[2 * block : 3 * block], low | high),
+        swap(partial[3 * block :], low),
+    ]
+    *parts, grads[0] = tied(*parts, grads[0])
+    result = added(*parts)
+    token_grad = result[:, :model_width]
+    gate_grad = jnp.sum(
+        jnp.where(named, result[:, model_width:].astype(jnp.float32)[:, None, :], 0.0), axis=2
+    ).astype(jnp.bfloat16)
+    return (token_grad, gate_grad, *grads)
+
+
+def body(tokens, expert_ids, *rest):
+    tok_rows, top_count = expert_ids.shape
+    if 2 * tok_rows * top_count // lax.axis_size("expert") < tok_rows:
+        return routed_body(tokens, expert_ids, *rest)
+    return dense_body(tokens, expert_ids, *rest)
+
+
 def solution(mesh):
     return jax.shard_map(
         body,

time: 287 us -> 103 us (0.36)
  the two profiles are of different devices: /device:TPU:13 before, /device:TPU:0 now
where the time goes in v2:
time: 103 us
  waiting for transfers between devices  31.9 us (31%)
  Pallas kernels  30.3 us (29%)
  starting transfers between devices  29 us (28%)
  local copies, waits for them, and re-layouts  8.52 us (8%)
  other arithmetic  1.81 us (2%)
    ppermute x32, waiting for transfers between devices, swap(): return lax.ppermute(value, BOTH, [(i, i ^ flip) for i in range(count)])  31.9 us
    ppermute x32, starting transfers between devices, swap(): return lax.ppermute(value, BOTH, [(i, i ^ flip) for i in range(count)])  29 us
    pallas_call x1, Pallas kernels, whole_gradients(): pl.pallas_call(whole_gradient_kernel, grid=(width // tile,), in_specs=[IN...  12.2 us
    pallas_call x2, Pallas kernels, backward(): pl.pallas_call(functools.partial(backward_kernel, which), in_specs=[IN_SM...  7.3 us
    unnamed x42, local copies, waits for them, and re-layouts  6.38 us
    pallas_call x1, Pallas kernels, forward(): pl.pallas_call(forward_kernel, in_specs=[IN_HBM] * 7, out_specs=[IN_VMEM]...  6.32 us
    pallas_call x1, Pallas kernels, own_gradients(): pl.pallas_call(own_gradient_kernel, grid=(width // tile,), in_specs=[IN_S...  4.41 us
  transfers between devices with their start and end apart: 32, of which 11 were waited for; matrix products, arithmetic and copies ran while one was open for 7% of the time, Pallas kernels for 30%

profile of v2, /device:TPU:0, one launch (start us, length us, event | category | flops | bytes accessed | tf_op | source)
XLA Modules:
  0.0 102.5 jit_solution(1158857633896134845)
XLA Ops:
  0.6 3.0 %collective-permute-start = (bf16[32,2048]{1,0:T(8,128)(2,1)}, bf16[32,2048]{1,0:T(8,128)(2,1)S(1)}, u32[]{:S(2)}, u32[]{:S(2)}) collective-permute-start(bf16[32,2048]{1,0:T(8,128)(2,1)} %param.7), channel_id=1, source_target_pairs={{0,1},{1,0},{2,3},{3,2},{4,5},{5,4},{6,7},{7,6},{8,9},{9,8},{10,11... | collective-permute-start | bytes 393224 | tf_op jit(solution)/shard_map/ppermute | solution.py:115
  3.6 2.6 %collective-permute-start.2 = (bf16[32,2048]{1,0:T(8,128)(2,1)}, bf16[32,2048]{1,0:T(8,128)(2,1)S(1)}, u32[]{:S(2)}, u32[]{:S(2)}) collective-permute-start(bf16[32,2048]{1,0:T(8,128)(2,1)} %param.7), channel_id=1, source_target_pairs={{0,16},{1,17},{2,18},{3,19},{4,20},{5,21},{6,22},{7,23},{8,24},{9,... | collective-permute-start | bytes 393224 | tf_op jit(solution)/shard_map/ppermute | solution.py:115
  6.2 1.3 %collective-permute-start.3 = (bf16[32,2048]{1,0:T(8,128)(2,1)}, bf16[32,2048]{1,0:T(8,128)(2,1)S(1)}, u32[]{:S(2)}, u32[]{:S(2)}) collective-permute-start(bf16[32,2048]{1,0:T(8,128)(2,1)} %param.7), channel_id=1, source_target_pairs={{0,24},{1,25},{2,26},{3,27},{4,28},{5,29},{6,30},{7,31},{8,16},{9,... | collective-permute-start | bytes 393224 | tf_op jit(solution)/shard_map/ppermute | solution.py:115
  7.8 0.8 copy.14
  8.6 0.8 copy.15
  9.5 0.9 pad_maximum_fusion.2
  11.0 1.6 %constant_dynamic-update-slice_fusion.7 = bf16[128,2048]{1,0:T(8,128)(2,1)} fusion(bf16[32,2048]{1,0:T(8,128)(2,1)} %param.7), kind=kLoop, calls=%fused_computation.17 | loop fusion | bytes 262144
  12.6 3.9 %collective-permute-done.2 = bf16[32,2048]{1,0:T(8,128)(2,1)S(1)} collective-permute-done((bf16[32,2048]{1,0:T(8,128)(2,1)}, bf16[32,2048]{1,0:T(8,128)(2,1)S(1)}, u32[]{:S(2)}, u32[]{:S(2)}) %collective-permute-start.2) | collective-permute-done | bytes 131104 | tf_op jit(solution)/shard_map/ppermute | solution.py:115
  16.7 4.1 %collective-permute-start.5 = (bf16[32,2176]{1,0:T(8,128)(2,1)S(1)}, bf16[32,2176]{1,0:T(8,128)(2,1)S(1)}, u32[]{:S(2)}, u32[]{:S(2)}) collective-permute-start(bf16[32,2176]{1,0:T(8,128)(2,1)S(1)} %pad_maximum_fusion.2), channel_id=1, source_target_pairs={{0,16},{1,17},{2,18},{3,19},{4,20},{5,21},{6,22},{7,23},{8,24},{9,... | collective-permute-start | bytes 417800 | tf_op jit(solution)/shard_map/ppermute | solution.py:115
  24.1 1.5 %collective-permute-start.11 = (bf16[128,2048]{1,0:T(8,128)(2,1)}, bf16[128,2048]{1,0:T(8,128)(2,1)}, u32[]{:S(2)}, u32[]{:S(2)}) collective-permute-start(bf16[128,2048]{1,0:T(8,128)(2,1)} %constant_dynamic-update-slice_fusion.4.refs_0_), channel_id=1, source_target_pairs={{0,4},{1,5},{2,6},{3,7},{4,0},{5,1},{6,2},{7,3},{8,12},{9,13},{10,... | collective-permute-start | bytes 1572872 | tf_op jit(solution)/shard_map/ppermute | solution.py:115
  25.6 5.4 %collective-permute-done.5 = bf16[32,2176]{1,0:T(8,128)(2,1)S(1)} collective-permute-done((bf16[32,2176]{1,0:T(8,128)(2,1)S(1)}, bf16[32,2176]{1,0:T(8,128)(2,1)S(1)}, u32[]{:S(2)}, u32[]{:S(2)}) %collective-permute-start.5) | collective-permute-done | bytes 139296 | tf_op jit(solution)/shard_map/ppermute | solution.py:115
  31.0 1.0 %collective-permute-done.7 = bf16[32,2176]{1,0:T(8,128)(2,1)S(1)} collective-permute-done((bf16[32,2176]{1,0:T(8,128)(2,1)S(1)}, bf16[32,2176]{1,0:T(8,128)(2,1)S(1)}, u32[]{:S(2)}, u32[]{:S(2)}) %collective-permute-start.7) | collective-permute-done | bytes 139296 | tf_op jit(solution)/shard_map/ppermute | solution.py:115
  32.1 5.3 %collective-permute-done.11.refs_2_ = bf16[128,2048]{1,0:T(8,128)(2,1)} collective-permute-done((bf16[128,2048]{1,0:T(8,128)(2,1)}, bf16[128,2048]{1,0:T(8,128)(2,1)}, u32[]{:S(2)}, u32[]{:S(2)}) %collective-permute-start.11) | collective-permute-done | bytes 524320 | tf_op jit(solution)/shard_map/ppermute | solution.py:115
  38.0 1.5 %collective-permute-start.14 = (bf16[128,2176]{1,0:T(8,128)(2,1)S(1)}, bf16[128,2176]{1,0:T(8,128)(2,1)S(1)}, u32[]{:S(2)}, u32[]{:S(2)}) collective-permute-start(bf16[128,2176]{1,0:T(8,128)(2,1)S(1)} %constant_dynamic-update-slice_fusion.own_ref), channel_id=1, source_target_pairs={{0,4},{1,5},{2,6},{3,7},{4,0},{5,1},{6,2},{7,3},{8,12},{9,13},{10,... | collective-permute-start | bytes 1671176 | tf_op jit(solution)/shard_map/ppermute | solution.py:115
  39.5 1.5 %collective-permute-start.15 = (bf16[128,2048]{1,0:T(8,128)(2,1)}, bf16[128,2048]{1,0:T(8,128)(2,1)S(1)}, u32[]{:S(2)}, u32[]{:S(2)}) collective-permute-start(bf16[128,2048]{1,0:T(8,128)(2,1)} %collective-permute-done.11.refs_2_), channel_id=1, source_target_pairs={{0,1},{1,0},{2,3},{3,2},{4,5},{5,4},{6,7},{7,6},{8,9},{9,8},{10,11... | collective-permute-start | bytes 1572872 | tf_op jit(solution)/shard_map/ppermute | solution.py:115
  41.1 6.3 %shard_map.110 = (bf16[768,2048]{1,0:T(8,128)(2,1)S(1)}, bf16[768,2048]{1,0:T(8,128)(2,1)S(1)}, bf16[2048,768]{1,0:T(8,128)(2,1)S(1)}, bf16[512,2048]{1,0:T(8,12...) custom-call(bf16[128,2048]{1,0:T(8,128)(2,1)} %constant_dynamic-update-slice_fusion.4.refs_0_, ...), custom_call_target="tpu_custom_call" | custom-call | flops 3221225472 | bytes 2097152 | tf_op jit(solution)/shard_map/pallas_call | solution.py:201
  47.4 3.7 %shard_map.111 = (bf16[128,2176]{1,0:T(8,128)(2,1)S(1)}, bf16[128,2176]{1,0:T(8,128)(2,1)S(1)}, bf16[256,2176]{1,0:T(8,128)(2,1)S(1)}, bf16[256,2304]{1,0:T(8,128)(2,1)S(1)}, f32[8,128]{1,0:T(8,128)S(1)}) custom-call(s32[2]{0:T(128)S(1)} %pad_add_fusion.place_ref._, bf16[128,2176]{1,0:T(8,128)(2,1)S(1)} %constant_dynamic-update-slice_fusion.own_ref, ...), custom_call_target="tpu_custom_call" | custom-call | tf_op jit(solution)/shard_map/pallas_call | solution.py:278
  51.2 1.4 %collective-permute-done.14.own_ref = bf16[128,2176]{1,0:T(8,128)(2,1)S(1)} collective-permute-done((bf16[128,2176]{1,0:T(8,128)(2,1)S(1)}, bf16[128,2176]{1,0:T(8,128)(2,1)S(1)}, u32[]{:S(2)}, u32[]{:S(2)}) %collective-permute-start.14) | collective-permute-done | bytes 557088 | tf_op jit(solution)/shard_map/ppermute | solution.py:115
  52.6 0.7 collective-permute-done.15.refs_2_
  53.9 1.6 %collective-permute-start.18 = (bf16[64,2176]{1,0:T(8,128)(2,1)S(1)}, bf16[64,2176]{1,0:T(8,128)(2,1)S(1)}, u32[]{:S(2)}, u32[]{:S(2)}) collective-permute-start(bf16[64,2176]{1,0:T(8,128)(2,1)S(1)} %pad_maximum_fusion.1), channel_id=1, source_target_pairs={{0,1},{1,0},{2,3},{3,2},{4,5},{5,4},{6,7},{7,6},{8,9},{9,8},{10,11... | collective-permute-start | bytes 835592 | tf_op jit(solution)/shard_map/ppermute | solution.py:115
  56.0 3.6 %shard_map.112 = (bf16[128,2176]{1,0:T(8,128)(2,1)S(1)}, bf16[128,2176]{1,0:T(8,128)(2,1)S(1)}, bf16[256,2176]{1,0:T(8,128)(2,1)S(1)}, bf16[256,2304]{1,0:T(8,128)(2,1)S(1)}, f32[8,128]{1,0:T(8,128)}) custom-call(s32[2]{0:T(128)S(1)} %pad_add_fusion.place_ref._, bf16[128,2176]{1,0:T(8,128)(2,1)S(1)} %collective-permute-done.14.own_ref, ...), custom_call_target="tpu_custom_call" | custom-call | tf_op jit(solution)/shard_map/pallas_call | solution.py:278
  59.6 2.9 %collective-permute-done.18.refs_8_ = bf16[64,2176]{1,0:T(8,128)(2,1)S(1)} collective-permute-done((bf16[64,2176]{1,0:T(8,128)(2,1)S(1)}, bf16[64,2176]{1,0:T(8,128)(2,1)S(1)}, u32[]{:S(2)}, u32[]{:S(2)}) %collective-permute-start.18) | collective-permute-done | bytes 278560 | tf_op jit(solution)/shard_map/ppermute | solution.py:115
  63.1 1.4 %collective-permute-done.22 = bf16[128,2176]{1,0:T(8,128)(2,1)S(1)} collective-permute-done((bf16[128,2176]{1,0:T(8,128)(2,1)S(1)}, bf16[128,2176]{1,0:T(8,128)(2,1)S(1)}, u32[]{:S(2)}, u32[]{:S(2)}) %collective-permute-start.22) | collective-permute-done | bytes 557088 | tf_op jit(solution)/shard_map/ppermute | solution.py:115
  64.7 0.9 collective-permute-start.23
  65.6 1.5 %collective-permute-start.24 = (bf16[32,2176]{1,0:T(8,128)(2,1)S(1)}, bf16[32,2176]{1,0:T(8,128)(2,1)S(1)}, u32[]{:S(2)}, u32[]{:S(2)}) collective-permute-start(bf16[32,2176]{1,0:T(8,128)(2,1)S(1)} %collective-permute-done.5), channel_id=1, source_target_pairs={{0,1},{1,0},{2,3},{3,2},{4,5},{5,4},{6,7},{7,6},{8,9},{9,8},{10,11... | collective-permute-start | bytes 417800 | tf_op jit(solution)/shard_map/ppermute | solution.py:115
  67.6 4.4 %shard_map.113 = (bf16[384,2048]{1,0:T(8,128)(2,1)S(1)}, bf16[384,2048]{1,0:T(8,128)(2,1)S(1)}, bf16[384,2048]{1,0:T(8,128)(2,1)S(1)}, f32[8,128]{1,0:T(8,128)S(1)}) custom-call(s32[2]{0:T(128)S(1)} %pad_add_fusion.place_ref._, bf16[256,2304]{1,0:T(8,128)(2,1)S(1)} %get-tuple-element.83.column_ref, bf16[256,2304]{1,0:T(8,128)(2,1)S(1)} %get-tuple-element.84.near_ref, ...), custom_call_target="tpu_custom_call" | custom-call | flops 2415919104 | bytes 4718592 | tf_op jit(solution)/shard_map/pallas_call | solution.py:319
  72.1 1.1 %copy-done.2 = bf16[384,2048]{1,0:T(8,128)(2,1)} copy-done((bf16[384,2048]{1,0:T(8,128)(2,1)}, bf16[384,2048]{1,0:T(8,128)(2,1)S(1)}, u32[]{:S(2)}) %copy-start.2) | copy-done | bytes 1572888
  73.2 6.2 %collective-permute-done.23 = bf16[128,2176]{1,0:T(8,128)(2,1)S(1)} collective-permute-done((bf16[128,2176]{1,0:T(8,128)(2,1)S(1)}, bf16[128,2176]{1,0:T(8,128)(2,1)S(1)}, u32[]{:S(2)}, u32[]{:S(2)}) %collective-permute-start.23) | collective-permute-done | bytes 557088 | tf_op jit(solution)/shard_map/ppermute | solution.py:115
  79.7 3.3 %collective-permute-done.25.refs_9_ = bf16[128,2176]{1,0:T(8,128)(2,1)S(1)} collective-permute-done((bf16[128,2176]{1,0:T(8,128)(2,1)S(1)}, bf16[128,2176]{1,0:T(8,128)(2,1)S(1)}, u32[]{:S(2)}, u32[]{:S(2)}) %collective-permute-start.25) | collective-permute-done | bytes 557088 | tf_op jit(solution)/shard_map/ppermute | solution.py:115
  83.6 3.5 %collective-permute-start.27 = (bf16[32,2176]{1,0:T(8,128)(2,1)S(1)}, bf16[32,2176]{1,0:T(8,128)(2,1)S(1)}, u32[]{:S(2)}, u32[]{:S(2)}) collective-permute-start(bf16[32,2176]{1,0:T(8,128)(2,1)S(1)} %get-tuple-element.116), channel_id=1, source_target_pairs={{0,16},{1,17},{2,18},{3,19},{4,20},{5,21},{6,22},{7,23},{8,24},{9,... | collective-permute-start | bytes 417800 | tf_op jit(solution)/shard_map/ppermute | solution.py:115
  88.6 12.2 %shard_map.114 = (bf16[1,384,2048]{2,1,0:T(8,128)(2,1)}, bf16[1,384,2048]{2,1,0:T(8,128)(2,1)}, bf16[1,384,2048]{2,1,0:T(8,128)(2,1)}) custom-call(s32[2]{0:T(128)S(1)} %pad_add_fusion.place_ref._, bf16[32,2048]{1,0:T(8,128)(2,1)} %copy-done.15, bf16[96,2048]{1,0:T(8,128)(2,1)} %copy-done.7, bf16[128,2048]{1,0:T(8,128)(2,1)} %copy-done.5, ...), custom_call_target="tpu_custom_call" | custom-call | flops 4831838208 | bytes 13631488 | tf_op jit(solution)/shard_map/pallas_call | solution.py:381
  101.0 0.7 slice.24
  (94 shorter events, 10.7 us)
Async XLA Ops:
  0.6 11.9 %collective-permute-start = (bf16[32,2048]{1,0:T(8,128)(2,1)}, bf16[32,2048]{1,0:T(8,128)(2,1)S(1)}, u32[]{:S(2)}, u32[]{:S(2)}) collective-permute-start(bf16[32,2048]{1,0:T(8,128)(2,1)} %param.7), channel_id=1, source_target_pairs={{0,1},{1,0},{2,3},{3,2},{4,5},{5,4},{6,7},{7,6},{8,9},{9,8},{10,11... | collective-permute-start | bytes 393224 | tf_op jit(solution)/shard_map/ppermute | solution.py:115
  3.6 12.9 %collective-permute-start.2 = (bf16[32,2048]{1,0:T(8,128)(2,1)}, bf16[32,2048]{1,0:T(8,128)(2,1)S(1)}, u32[]{:S(2)}, u32[]{:S(2)}) collective-permute-start(bf16[32,2048]{1,0:T(8,128)(2,1)} %param.7), channel_id=1, source_target_pairs={{0,16},{1,17},{2,18},{3,19},{4,20},{5,21},{6,22},{7,23},{8,24},{9,... | collective-permute-start | bytes 393224 | tf_op jit(solution)/shard_map/ppermute | solution.py:115
  6.2 10.3 %collective-permute-start.3 = (bf16[32,2048]{1,0:T(8,128)(2,1)}, bf16[32,2048]{1,0:T(8,128)(2,1)S(1)}, u32[]{:S(2)}, u32[]{:S(2)}) collective-permute-start(bf16[32,2048]{1,0:T(8,128)(2,1)} %param.7), channel_id=1, source_target_pairs={{0,24},{1,25},{2,26},{3,27},{4,28},{5,29},{6,30},{7,31},{8,16},{9,... | collective-permute-start | bytes 393224 | tf_op jit(solution)/shard_map/ppermute | solution.py:115
  7.6 9.1 %collective-permute-start.4 = (bf16[32,2048]{1,0:T(8,128)(2,1)}, bf16[32,2048]{1,0:T(8,128)(2,1)S(1)}, u32[]{:S(2)}, u32[]{:S(2)}) collective-permute-start(bf16[32,2048]{1,0:T(8,128)(2,1)} %param.7), channel_id=1, source_target_pairs={{0,8},{1,9},{2,10},{3,11},{4,12},{5,13},{6,14},{7,15},{8,0},{9,1},... | collective-permute-start | bytes 393224 | tf_op jit(solution)/shard_map/ppermute | solution.py:115
  10.4 6.3 %collective-permute-start.1 = (bf16[32,2176]{1,0:T(8,128)(2,1)S(1)}, bf16[32,2176]{1,0:T(8,128)(2,1)S(1)}, u32[]{:S(2)}, u32[]{:S(2)}) collective-permute-start(bf16[32,2176]{1,0:T(8,128)(2,1)S(1)} %pad_maximum_fusion.2), channel_id=1, source_target_pairs={{0,1},{1,0},{2,3},{3,2},{4,5},{5,4},{6,7},{7,6},{8,9},{9,8},{10,11... | collective-permute-start | bytes 417800 | tf_op jit(solution)/shard_map/ppermute | solution.py:115
  16.7 14.3 %collective-permute-start.5 = (bf16[32,2176]{1,0:T(8,128)(2,1)S(1)}, bf16[32,2176]{1,0:T(8,128)(2,1)S(1)}, u32[]{:S(2)}, u32[]{:S(2)}) collective-permute-start(bf16[32,2176]{1,0:T(8,128)(2,1)S(1)} %pad_maximum_fusion.2), channel_id=1, source_target_pairs={{0,16},{1,17},{2,18},{3,19},{4,20},{5,21},{6,22},{7,23},{8,24},{9,... | collective-permute-start | bytes 417800 | tf_op jit(solution)/shard_map/ppermute | solution.py:115
  20.8 10.2 %collective-permute-start.6 = (bf16[32,2176]{1,0:T(8,128)(2,1)S(1)}, bf16[32,2176]{1,0:T(8,128)(2,1)S(1)}, u32[]{:S(2)}, u32[]{:S(2)}) collective-permute-start(bf16[32,2176]{1,0:T(8,128)(2,1)S(1)} %pad_maximum_fusion.2), channel_id=1, source_target_pairs={{0,24},{1,25},{2,26},{3,27},{4,28},{5,29},{6,30},{7,31},{8,16},{9,... | collective-permute-start | bytes 417800 | tf_op jit(solution)/shard_map/ppermute | solution.py:115
  21.3 10.7 %collective-permute-start.7 = (bf16[32,2176]{1,0:T(8,128)(2,1)S(1)}, bf16[32,2176]{1,0:T(8,128)(2,1)S(1)}, u32[]{:S(2)}, u32[]{:S(2)}) collective-permute-start(bf16[32,2176]{1,0:T(8,128)(2,1)S(1)} %pad_maximum_fusion.2), channel_id=1, source_target_pairs={{0,8},{1,9},{2,10},{3,11},{4,12},{5,13},{6,14},{7,15},{8,0},{9,1},... | collective-permute-start | bytes 417800 | tf_op jit(solution)/shard_map/ppermute | solution.py:115
  21.5 10.5 %collective-permute-start.8 = (bf16[96,2048]{1,0:T(8,128)(2,1)S(1)}, bf16[96,2048]{1,0:T(8,128)(2,1)S(1)}, u32[]{:S(2)}, u32[]{:S(2)}) collective-permute-start(bf16[96,2048]{1,0:T(8,128)(2,1)S(1)} %pad_maximum_fusion), channel_id=1, source_target_pairs={{0,1},{1,0},{2,3},{3,2},{4,5},{5,4},{6,7},{7,6},{8,9},{9,8},{10,11... | collective-permute-start | bytes 1179656 | tf_op jit(solution)/shard_map/ppermute | solution.py:115
  24.1 13.3 %collective-permute-start.11 = (bf16[128,2048]{1,0:T(8,128)(2,1)}, bf16[128,2048]{1,0:T(8,128)(2,1)}, u32[]{:S(2)}, u32[]{:S(2)}) collective-permute-start(bf16[128,2048]{1,0:T(8,128)(2,1)} %constant_dynamic-update-slice_fusion.4.refs_0_), channel_id=1, source_target_pairs={{0,4},{1,5},{2,6},{3,7},{4,0},{5,1},{6,2},{7,3},{8,12},{9,13},{10,... | collective-permute-start | bytes 1572872 | tf_op jit(solution)/shard_map/ppermute | solution.py:115
  31.0 10.0 %collective-permute-start.10 = (bf16[128,2048]{1,0:T(8,128)(2,1)}, bf16[128,2048]{1,0:T(8,128)(2,1)}, u32[]{:S(2)}, u32[]{:S(2)}) collective-permute-start(bf16[128,2048]{1,0:T(8,128)(2,1)} %constant_dynamic-update-slice_fusion.4.refs_0_), channel_id=1, source_target_pairs={{0,2},{1,3},{2,0},{3,1},{4,6},{5,7},{6,4},{7,5},{8,10},{9,11},{10,... | collective-permute-start | bytes 1572872 | tf_op jit(solution)/shard_map/ppermute | solution.py:115
  37.4 3.7 %collective-permute-start.12 = (bf16[128,2048]{1,0:T(8,128)(2,1)}, bf16[128,2048]{1,0:T(8,128)(2,1)}, u32[]{:S(2)}, u32[]{:S(2)}) collective-permute-start(bf16[128,2048]{1,0:T(8,128)(2,1)} %collective-permute-done.11.refs_2_), channel_id=1, source_target_pairs={{0,2},{1,3},{2,0},{3,1},{4,6},{5,7},{6,4},{7,5},{8,10},{9,11},{10,... | collective-permute-start | bytes 1572872 | tf_op jit(solution)/shard_map/ppermute | solution.py:115
  37.4 10.0 %collective-permute-start.9 = (bf16[128,2176]{1,0:T(8,128)(2,1)S(1)}, bf16[128,2176]{1,0:T(8,128)(2,1)S(1)}, u32[]{:S(2)}, u32[]{:S(2)}) collective-permute-start(bf16[128,2176]{1,0:T(8,128)(2,1)S(1)} %constant_dynamic-update-slice_fusion.own_ref), channel_id=1, source_target_pairs={{0,2},{1,3},{2,0},{3,1},{4,6},{5,7},{6,4},{7,5},{8,10},{9,11},{10,... | collective-permute-start | bytes 1671176 | tf_op jit(solution)/shard_map/ppermute | solution.py:115
  38.0 14.6 %collective-permute-start.14 = (bf16[128,2176]{1,0:T(8,128)(2,1)S(1)}, bf16[128,2176]{1,0:T(8,128)(2,1)S(1)}, u32[]{:S(2)}, u32[]{:S(2)}) collective-permute-start(bf16[128,2176]{1,0:T(8,128)(2,1)S(1)} %constant_dynamic-update-slice_fusion.own_ref), channel_id=1, source_target_pairs={{0,4},{1,5},{2,6},{3,7},{4,0},{5,1},{6,2},{7,3},{8,12},{9,13},{10,... | collective-permute-start | bytes 1671176 | tf_op jit(solution)/shard_map/ppermute | solution.py:115
  39.5 13.8 %collective-permute-start.15 = (bf16[128,2048]{1,0:T(8,128)(2,1)}, bf16[128,2048]{1,0:T(8,128)(2,1)S(1)}, u32[]{:S(2)}, u32[]{:S(2)}) collective-permute-start(bf16[128,2048]{1,0:T(8,128)(2,1)} %collective-permute-done.11.refs_2_), channel_id=1, source_target_pairs={{0,1},{1,0},{2,3},{3,2},{4,5},{5,4},{6,7},{7,6},{8,9},{9,8},{10,11... | collective-permute-start | bytes 1572872 | tf_op jit(solution)/shard_map/ppermute | solution.py:115
  41.0 10.2 %collective-permute-start.16 = (bf16[96,2048]{1,0:T(8,128)(2,1)S(1)}, bf16[96,2048]{1,0:T(8,128)(2,1)S(1)}, u32[]{:S(2)}, u32[]{:S(2)}) collective-permute-start(bf16[96,2048]{1,0:T(8,128)(2,1)S(1)} %collective-permute-done.8.refs_1_), channel_id=1, source_target_pairs={{0,2},{1,3},{2,0},{3,1},{4,6},{5,7},{6,4},{7,5},{8,10},{9,11},{10,... | collective-permute-start | bytes 1179656 | tf_op jit(solution)/shard_map/ppermute | solution.py:115
  53.4 2.6 %collective-permute-start.17 = (bf16[128,2176]{1,0:T(8,128)(2,1)S(1)}, bf16[128,2176]{1,0:T(8,128)(2,1)S(1)}, u32[]{:S(2)}, u32[]{:S(2)}) collective-permute-start(bf16[128,2176]{1,0:T(8,128)(2,1)S(1)} %collective-permute-done.14.own_ref), channel_id=1, source_target_pairs={{0,2},{1,3},{2,0},{3,1},{4,6},{5,7},{6,4},{7,5},{8,10},{9,11},{10,... | collective-permute-start | bytes 1671176 | tf_op jit(solution)/shard_map/ppermute | solution.py:115
  53.4 9.2 %collective-permute-start.19 = (bf16[128,2048]{1,0:T(8,128)(2,1)S(1)}, bf16[128,2048]{1,0:T(8,128)(2,1)S(1)}, u32[]{:S(2)}, u32[]{:S(2)}) collective-permute-start(bf16[128,2048]{1,0:T(8,128)(2,1)S(1)} %collective-permute-done.15.refs_2_), channel_id=1, source_target_pairs={{0,2},{1,3},{2,0},{3,1},{4,6},{5,7},{6,4},{7,5},{8,10},{9,11},{10,... | collective-permute-start | bytes 1572872 | tf_op jit(solution)/shard_map/ppermute | solution.py:115
  53.9 8.6 %collective-permute-start.18 = (bf16[64,2176]{1,0:T(8,128)(2,1)S(1)}, bf16[64,2176]{1,0:T(8,128)(2,1)S(1)}, u32[]{:S(2)}, u32[]{:S(2)}) collective-permute-start(bf16[64,2176]{1,0:T(8,128)(2,1)S(1)} %pad_maximum_fusion.1), channel_id=1, source_target_pairs={{0,1},{1,0},{2,3},{3,2},{4,5},{5,4},{6,7},{7,6},{8,9},{9,8},{10,11... | collective-permute-start | bytes 835592 | tf_op jit(solution)/shard_map/ppermute | solution.py:115
  55.5 4.1 %collective-permute-start.21 = (bf16[32,2176]{1,0:T(8,128)(2,1)S(1)}, bf16[32,2176]{1,0:T(8,128)(2,1)S(1)}, u32[]{:S(2)}, u32[]{:S(2)}) collective-permute-start(bf16[32,2176]{1,0:T(8,128)(2,1)S(1)} %collective-permute-done.1.refs_6_), channel_id=1, source_target_pairs={{0,2},{1,3},{2,0},{3,1},{4,6},{5,7},{6,4},{7,5},{8,10},{9,11},{10,... | collective-permute-start | bytes 417800 | tf_op jit(solution)/shard_map/ppermute | solution.py:115
  55.5 4.1 %collective-permute-start.20 = (bf16[32,2048]{1,0:T(8,128)(2,1)S(1)}, bf16[32,2048]{1,0:T(8,128)(2,1)S(1)}, u32[]{:S(2)}, u32[]{:S(2)}) collective-permute-start(bf16[32,2048]{1,0:T(8,128)(2,1)S(1)} %collective-permute-done.refs_0_), channel_id=1, source_target_pairs={{0,2},{1,3},{2,0},{3,1},{4,6},{5,7},{6,4},{7,5},{8,10},{9,11},{10,... | collective-permute-start | bytes 393224 | tf_op jit(solution)/shard_map/ppermute | solution.py:115
  62.5 2.0 %collective-permute-start.22 = (bf16[128,2176]{1,0:T(8,128)(2,1)S(1)}, bf16[128,2176]{1,0:T(8,128)(2,1)S(1)}, u32[]{:S(2)}, u32[]{:S(2)}) collective-permute-start(bf16[128,2176]{1,0:T(8,128)(2,1)S(1)} %get-tuple-element.81), channel_id=1, source_target_pairs={{0,2},{1,3},{2,0},{3,1},{4,6},{5,7},{6,4},{7,5},{8,10},{9,11},{10,... | collective-permute-start | bytes 1671176 | tf_op jit(solution)/shard_map/ppermute | solution.py:115
  62.6 10.6 %collective-permute-start.13 = (bf16[128,2176]{1,0:T(8,128)(2,1)S(1)}, bf16[128,2176]{1,0:T(8,128)(2,1)S(1)}, u32[]{:S(2)}, u32[]{:S(2)}) collective-permute-start(bf16[128,2176]{1,0:T(8,128)(2,1)S(1)} %get-tuple-element.71), channel_id=1, source_target_pairs={{0,2},{1,3},{2,0},{3,1},{4,6},{5,7},{6,4},{7,5},{8,10},{9,11},{10,... | collective-permute-start | bytes 1671176 | tf_op jit(solution)/shard_map/ppermute | solution.py:115
  64.7 14.7 %collective-permute-start.23 = (bf16[128,2176]{1,0:T(8,128)(2,1)S(1)}, bf16[128,2176]{1,0:T(8,128)(2,1)S(1)}, u32[]{:S(2)}, u32[]{:S(2)}) collective-permute-start(bf16[128,2176]{1,0:T(8,128)(2,1)S(1)} %add_convert_fusion.1), channel_id=1, source_target_pairs={{0,4},{1,5},{2,6},{3,7},{4,0},{5,1},{6,2},{7,3},{8,12},{9,13},{10,... | collective-permute-start | bytes 1671176 | tf_op jit(solution)/shard_map/ppermute | solution.py:115
  65.6 14.0 %collective-permute-start.24 = (bf16[32,2176]{1,0:T(8,128)(2,1)S(1)}, bf16[32,2176]{1,0:T(8,128)(2,1)S(1)}, u32[]{:S(2)}, u32[]{:S(2)}) collective-permute-start(bf16[32,2176]{1,0:T(8,128)(2,1)S(1)} %collective-permute-done.5), channel_id=1, source_target_pairs={{0,1},{1,0},{2,3},{3,2},{4,5},{5,4},{6,7},{7,6},{8,9},{9,8},{10,11... | collective-permute-start | bytes 417800 | tf_op jit(solution)/shard_map/ppermute | solution.py:115
  67.1 15.9 %collective-permute-start.25 = (bf16[128,2176]{1,0:T(8,128)(2,1)S(1)}, bf16[128,2176]{1,0:T(8,128)(2,1)S(1)}, u32[]{:S(2)}, u32[]{:S(2)}) collective-permute-start(bf16[128,2176]{1,0:T(8,128)(2,1)S(1)} %collective-permute-done.14.own_ref), channel_id=1, source_target_pairs={{0,1},{1,0},{2,3},{3,2},{4,5},{5,4},{6,7},{7,6},{8,9},{9,8},{10,11... | collective-permute-start | bytes 1671176 | tf_op jit(solution)/shard_map/ppermute | solution.py:115
  67.6 15.3 %collective-permute-start.26 = (bf16[64,2176]{1,0:T(8,128)(2,1)S(1)}, bf16[64,2176]{1,0:T(8,128)(2,1)S(1)}, u32[]{:S(2)}, u32[]{:S(2)}) collective-permute-start(bf16[64,2176]{1,0:T(8,128)(2,1)S(1)} %collective-permute-done.18.refs_8_), channel_id=1, source_target_pairs={{0,2},{1,3},{2,0},{3,1},{4,6},{5,7},{6,4},{7,5},{8,10},{9,11},{10,... | collective-permute-start | bytes 835592 | tf_op jit(solution)/shard_map/ppermute | solution.py:115
  83.0 4.8 %collective-permute-start.31 = (bf16[128,2176]{1,0:T(8,128)(2,1)S(1)}, bf16[128,2176]{1,0:T(8,128)(2,1)S(1)}, u32[]{:S(2)}, u32[]{:S(2)}) collective-permute-start(bf16[128,2176]{1,0:T(8,128)(2,1)S(1)} %collective-permute-done.25.refs_9_), channel_id=1, source_target_pairs={{0,2},{1,3},{2,0},{3,1},{4,6},{5,7},{6,4},{7,5},{8,10},{9,11},{10,... | collective-permute-start | bytes 1671176 | tf_op jit(solution)/shard_map/ppermute | solution.py:115
  83.0 4.7 %collective-permute-start.30 = (bf16[32,2176]{1,0:T(8,128)(2,1)S(1)}, bf16[32,2176]{1,0:T(8,128)(2,1)S(1)}, u32[]{:S(2)}, u32[]{:S(2)}) collective-permute-start(bf16[32,2176]{1,0:T(8,128)(2,1)S(1)} %collective-permute-done.24.refs_7_), channel_id=1, source_target_pairs={{0,2},{1,3},{2,0},{3,1},{4,6},{5,7},{6,4},{7,5},{8,10},{9,11},{10,... | collective-permute-start | bytes 417800 | tf_op jit(solution)/shard_map/ppermute | solution.py:115
  83.6 17.3 %collective-permute-start.27 = (bf16[32,2176]{1,0:T(8,128)(2,1)S(1)}, bf16[32,2176]{1,0:T(8,128)(2,1)S(1)}, u32[]{:S(2)}, u32[]{:S(2)}) collective-permute-start(bf16[32,2176]{1,0:T(8,128)(2,1)S(1)} %get-tuple-element.116), channel_id=1, source_target_pairs={{0,16},{1,17},{2,18},{3,19},{4,20},{5,21},{6,22},{7,23},{8,24},{9,... | collective-permute-start | bytes 417800 | tf_op jit(solution)/shard_map/ppermute | solution.py:115
  87.1 13.8 %collective-permute-start.28 = (bf16[32,2176]{1,0:T(8,128)(2,1)S(1)}, bf16[32,2176]{1,0:T(8,128)(2,1)S(1)}, u32[]{:S(2)}, u32[]{:S(2)}) collective-permute-start(bf16[32,2176]{1,0:T(8,128)(2,1)S(1)} %get-tuple-element.115), channel_id=1, source_target_pairs={{0,24},{1,25},{2,26},{3,27},{4,28},{5,29},{6,30},{7,31},{8,16},{9,... | collective-permute-start | bytes 417800 | tf_op jit(solution)/shard_map/ppermute | solution.py:115
  87.7 13.2 %collective-permute-start.29 = (bf16[32,2176]{1,0:T(8,128)(2,1)S(1)}, bf16[32,2176]{1,0:T(8,128)(2,1)S(1)}, u32[]{:S(2)}, u32[]{:S(2)}) collective-permute-start(bf16[32,2176]{1,0:T(8,128)(2,1)S(1)} %get-tuple-element.114), channel_id=1, source_target_pairs={{0,8},{1,9},{2,10},{3,11},{4,12},{5,13},{6,14},{7,15},{8,0},{9,1},... | collective-permute-start | bytes 417800 | tf_op jit(solution)/shard_map/ppermute | solution.py:115
  (17 other events, 196.8 us)

commit v3 on v2

--- a/solution.py
+++ b/solution.py
@@ -329,9 +329,53 @@
     )(place, *[kept(value) for value in (*lefts, x_rows, *cot_rows)])
 
 
+def away_forward_kernel(place_ref, *refs):
+    x_refs, weight_refs = refs[:4], refs[4:6]
+    slope_out, swish_out, hidden_out, token_out, rows, gate_ref, up_ref, sems = refs[7:]
+    share = gate_ref.shape[0]
+    own = pl.ds(pl.multiple_of(place_ref[1] * share, 128), share)
+    copies = fetched(
+        placed(x_refs, rows)
+        + [(weight_refs[0].at[0, own], gate_ref), (weight_refs[1].at[0, own], up_ref)],
+        sems,
+    )
+    token_out[...] = jnp.zeros_like(token_out)
+    for copy in copies[:5]:
+        copy.wait()
+    pre_gate = contract_last(gate_ref[...], rows[...])
+    copies[5].wait()
+    pre_up = contract_last(up_ref[...], rows[...])
+    gate_sigmoid = jax.nn.sigmoid(pre_gate)
+    swish = pre_gate * gate_sigmoid
+    slope_out[...] = pre_up * gate_sigmoid * (1.0 + pre_gate * (1.0 - gate_sigmoid))
+    swish_out[...] = swish
+    hidden_out[...] = swish * pre_up
+
+
+def away_forward(place, x_rows, weights, share, after):
+    width = x_rows[0].shape[1]
+    rows = sum(piece.shape[0] for piece in x_rows)
+    half = pltpu.VMEM((share, width), jnp.bfloat16)
+    return pl.pallas_call(
+        away_forward_kernel,
+        in_specs=[IN_SMEM] + [IN_HBM] * 7,
+        out_specs=[IN_VMEM] * 4,
+        out_shape=[jax.ShapeDtypeStruct((share, rows), jnp.float32)] * 3
+        + [jax.ShapeDtypeStruct((8, 128), jnp.float32)],
+        scratch_shapes=[
+            pltpu.VMEM((rows, width), jnp.bfloat16),
+            half,
+            half,
+            pltpu.SemaphoreType.DMA((6,)),
+        ],
+        **kernel_params(4 * rows * share * width, 2 * rows * width, rows * share, 20),
+    )(place, *[left_out(value) for value in (*x_rows, *weights)], after)
+
+
 def whole_gradient_kernel(place_ref, *refs):
-    x_refs, cot_refs, weight_refs, own_refs = refs[:6], refs[6:14], refs[14:17], refs[17:20]
-    outs, (rows, cot, gate_ref, up_ref, down_ref, lefts, sems) = refs[21:24], refs[24:]
+    cot_refs, down_ref, saved_refs, x_refs = refs[:4], refs[4], refs[5:8], refs[8:12]
+    own_refs, outs = refs[12:15], refs[16:19]
+    rows, cot, down, slope, swish, hidden, lefts, sems = refs[19:]
     share, tile = outs[0].shape[1:]
     width = rows.shape[1]
 
@@ -339,32 +383,28 @@
     def _():
         own = pl.ds(pl.multiple_of(place_ref[1] * share, 128), share)
         copies = fetched(
-            placed(x_refs, rows)
-            + [(weight_refs[0].at[0, own], gate_ref), (weight_refs[1].at[0, own], up_ref)]
-            + placed(cot_refs, cot)
-            + [(weight_refs[2].at[0, :, own], down_ref)],
+            placed(cot_refs, cot)
+            + [(down_ref.at[0, :, own], down)]
+            + list(zip(saved_refs, (slope, swish, hidden)))
+            + placed(x_refs, rows),
             sems,
         )
-        for copy in copies[:8]:
-            copy.wait()
-        pre_gate = contract_last(gate_ref[...], rows[...])
-        pre_up = contract_last(up_ref[...], rows[...])
-        gate_sigmoid = jax.nn.sigmoid(pre_gate)
-        swish = pre_gate * gate_sigmoid
-        for copy in copies[8:]:
+        for copy in copies[:5]:
             copy.wait()
         table = cot[:, width:]
         pick = (lax.broadcasted_iota(jnp.int32, (16, table.shape[1]), 1) == place_ref[0]).astype(
             jnp.bfloat16
         )
         gates = contract_last(pick, table)[:1]
-        raw = jnp.dot(cot[:, :width], down_ref[...], preferred_element_type=jnp.float32).T
+        raw = jnp.dot(cot[:, :width], down[...], preferred_element_type=jnp.float32).T
         d_hidden = gates * raw
-        lefts[0] = (
-            d_hidden * pre_up * gate_sigmoid * (1.0 + pre_gate * (1.0 - gate_sigmoid))
-        ).astype(jnp.bfloat16)
-        lefts[1] = (d_hidden * swish).astype(jnp.bfloat16)
-        lefts[2] = (gates * (swish * pre_up)).astype(jnp.bfloat16)
+        for copy in copies[5:8]:
+            copy.wait()
+        lefts[0] = (d_hidden * slope[...]).astype(jnp.bfloat16)
+        lefts[1] = (d_hidden * swish[...]).astype(jnp.bfloat16)
+        lefts[2] = (gates * hidden[...]).astype(jnp.bfloat16)
+        for copy in copies[8:]:
+            copy.wait()
 
     first = pl.multiple_of(pl.program_id(0) * tile, tile)
     for i in range(3):
@@ -373,16 +413,16 @@
         outs[i][0] = (own_refs[i][...].astype(jnp.float32) + away).astype(jnp.bfloat16)
 
 
-def whole_gradients(place, x_rows, cot_rows, weights, own, after):
+def whole_gradients(place, cot_rows, w_down, saved, x_rows, own, after):
     share, width = own[0].shape
     tile = 2 * TILE
     rows = sum(piece.shape[0] for piece in x_rows)
-    half = pltpu.VMEM((share, width), jnp.bfloat16)
+    half = pltpu.VMEM((share, rows), jnp.float32)
     return pl.pallas_call(
         whole_gradient_kernel,
         grid=(width // tile,),
         in_specs=[IN_SMEM]
-        + [IN_HBM] * 17
+        + [IN_HBM] * 12
         + [pl.BlockSpec((share, tile), lambda i: (0, i))] * 3
         + [IN_HBM],
         out_specs=[pl.BlockSpec((1, share, tile), lambda i: (0, 0, i))] * 3,
@@ -390,16 +430,24 @@
         scratch_shapes=[
             pltpu.VMEM((rows, width), jnp.bfloat16),
             pltpu.VMEM((rows, cot_rows[0].shape[1]), jnp.bfloat16),
+            pltpu.VMEM((width, share), jnp.bfloat16),
             half,
             half,
-            pltpu.VMEM((width, share), jnp.bfloat16),
+            half,
             pltpu.VMEM((3, share, rows), jnp.bfloat16),
-            pltpu.SemaphoreType.DMA((17,)),
+            pltpu.SemaphoreType.DMA((12,)),
         ],
         **kernel_params(
-            12 * rows * share * width, 4 * rows * width + 12 * share * width, rows * share, 32
+            8 * rows * share * width, 4 * rows * width + 12 * share * width, rows * share, 32
         ),
-    )(place, *[left_out(value) for value in (*x_rows, *cot_rows, *weights, *own)], after)
+    )(
+        place,
+        *[left_out(value) for value in (*cot_rows, w_down)],
+        *saved,
+        *[left_out(value) for value in x_rows],
+        *own,
+        after,
+    )
 
 
 def dense_body(tokens, expert_ids, gate_weights, cotangent, w_gate, w_up, w_down):
@@ -420,18 +468,15 @@
 
     weights = (w_gate, w_up, w_down)
     packed = jnp.concatenate([cotangent, gate_table], axis=1)
-    x_mine_away, cot_mine_away = swap(tokens, group), swap(packed, group)
-    packed, x_mine_away, cot_mine_away, *x_far = tied(
-        packed, x_mine_away, cot_mine_away, *column_of(tokens)
-    )
-    x_far = jnp.concatenate(x_far, axis=0)
-    x_column = jnp.concatenate([tokens, x_far], axis=0)
+    cot_mine_away = swap(packed, group)
+    packed, cot_mine_away, *x_far = tied(packed, cot_mine_away, *column_of(tokens))
+    x_column = jnp.concatenate([tokens, *x_far], axis=0)
     x_near = swap(x_column, near)
-    x_far_away, x_near_away = swap(x_far, group), swap(x_near, group)
-    *cot_far, x_far_away = tied(*column_of(packed), x_far_away)
-    x_far_other = swap(x_far_away, core)
+    x_column_away = swap(x_column, group)
+    *cot_far, x_near, x_column_away = tied(*column_of(packed), x_near, x_column_away)
+    x_near_away = swap(x_near, group)
     cot_column = jnp.concatenate([packed, *cot_far], axis=0)
-    cot_first_away = swap(cot_far[0], group)
+    cot_far_away = column_of(cot_mine_away)
     cot_near = swap(cot_column, near)
     *kept_weights, x_rows, slope, swish, hidden = forward(
         [x_column, swap(x_column, core), x_near, swap(x_near, core)], weights
@@ -440,32 +485,30 @@
     own_part, other_part, column_cot, column_lefts, token = backward(
         place, cot_column, swap(cot_column, core), saved, 0, kept_weights, place
     )
-    column_partial = added(own_part, swap(other_part, core))
-    cot_near, token, x_near_away, x_far_other = tied(cot_near, token, x_near_away, x_far_other)
+    column_own, column_given = own_part, swap(other_part, core)
+    x_column_other = swap(x_column_away, core)
+    cot_near, token, x_near_away, x_column_other = tied(
+        cot_near, token, x_near_away, x_column_other
+    )
     x_near_other = swap(x_near_away, core)
-    x_mine_other, cot_mine_other = swap(x_mine_away, core), swap(cot_mine_away, core)
-    cot_second_away = swap(jnp.concatenate(cot_far[1:], axis=0), group)
     cot_near_away = swap(cot_near, group)
     own_part, other_part, near_cot, near_lefts, _ = backward(
         place, cot_near, swap(cot_near, core), saved, 1, kept_weights, token
     )
-    other_part, cot_second_away, x_near_other, x_mine_other, cot_mine_other = tied(
-        other_part, cot_second_away, x_near_other, x_mine_other, cot_mine_other
-    )
-    cot_second_other = swap(cot_second_away, core)
+    other_part, x_near_other, column_given = tied(other_part, x_near_other, column_given)
     near_partial = added(own_part, swap(other_part, core))
-    partial = added(column_partial, swap(near_partial, near))
+    partial = added(column_own, column_given, swap(near_partial, near))
     *own, token = own_gradients(
         place, [column_lefts, near_lefts], x_rows, [column_cot, near_cot], share
     )
-    partial, cot_first_away, cot_near_away, cot_second_other, token = tied(
-        partial, cot_first_away, cot_near_away, cot_second_other, token
-    )
-    x_away = [x_mine_away, x_far_away, x_near_away, x_mine_other, x_far_other, x_near_other]
-    cot_away = [cot_mine_away, cot_first_away, cot_second_away, cot_near_away]
-    cot_away += [cot_mine_other, swap(cot_first_away, core), cot_second_other]
-    cot_away += [swap(cot_near_away, core)]
-    grads = list(whole_gradients(place, x_away, cot_away, weights, own, token))
+    x_away = [x_column_away, x_near_away, x_column_other, x_near_other]
+    *away_saved, token = away_forward(place, x_away, weights[:2], share, token)
+    partial, token, cot_near_away, *cot_far_away = tied(
+        partial, token, cot_near_away, *cot_far_away
+    )
+    cot_away = [jnp.concatenate([cot_mine_away, *cot_far_away], axis=0), cot_near_away]
+    cot_away += [swap(value, core) for value in cot_away]
+    grads = list(whole_gradients(place, cot_away, w_down, away_saved, x_away, own, token))
     block = partial.shape[0] // 4
     parts = [
         partial[:block],

time: 103 us -> 91.2 us (0.89)
  waiting for transfers between devices: 31.9 us -> 22.4 us
  local copies, waits for them, and re-layouts: 8.52 us -> 5.76 us
  Pallas kernels: 30.3 us -> 31.6 us
    ppermute x32 -> x29, waiting for transfers between devices: 31.9 us -> 22.4 us  [swap(): return lax.ppermute(value, BOTH, [(i, i ^ flip) for i in range(count)])]
    pallas_call x0 -> x1, Pallas kernels: none -> 4.8 us  [away_forward(): pl.pallas_call(away_forward_kernel, in_specs=[IN_SMEM] + [IN_HBM] * 7, ou...]
    pallas_call x1, Pallas kernels: 12.2 us -> 8.73 us  [whole_gradients(): pl.pallas_call(whole_gradient_kernel, grid=(width // tile,), in_specs=[IN...]
    unnamed x42 -> x31, local copies, waits for them, and re-layouts: 6.38 us -> 4.25 us
    ppermute x32 -> x29, starting transfers between devices: 29 us -> 28.6 us  [swap(): return lax.ppermute(value, BOTH, [(i, i ^ flip) for i in range(count)])]
  transfers between devices with their start and end apart: 32 -> 29, of which waited for: 11 -> 9; matrix products, arithmetic and copies ran while one was open for 7% -> 4% of each run, Pallas kernels for 30% -> 35%
where the time goes in v3:
time: 91.2 us; the launch traced here: 91 us
  Pallas kernels  31.6 us (35%)
  starting transfers between devices  28.6 us (31%)
  waiting for transfers between devices  22.4 us (25%)
  local copies, waits for them, and re-layouts  5.76 us (6%)
  other arithmetic  1.75 us (2%)
  between operations  0.96 us (1%)
    ppermute x29, starting transfers between devices, swap(): return lax.ppermute(value, BOTH, [(i, i ^ flip) for i in range(count)])  28.6 us
    ppermute x29, waiting for transfers between devices, swap(): return lax.ppermute(value, BOTH, [(i, i ^ flip) for i in range(count)])  22.4 us
    pallas_call x1, Pallas kernels, whole_gradients(): pl.pallas_call(whole_gradient_kernel, grid=(width // tile,), in_specs=[IN...  8.73 us
    pallas_call x2, Pallas kernels, backward(): pl.pallas_call(functools.partial(backward_kernel, which), in_specs=[IN_SM...  7.29 us
    pallas_call x1, Pallas kernels, forward(): pl.pallas_call(forward_kernel, in_specs=[IN_HBM] * 7, out_specs=[IN_VMEM]...  6.32 us
    pallas_call x1, Pallas kernels, away_forward(): pl.pallas_call(away_forward_kernel, in_specs=[IN_SMEM] + [IN_HBM] * 7, ou...  4.8 us
    pallas_call x1, Pallas kernels, own_gradients(): pl.pallas_call(own_gradient_kernel, grid=(width // tile,), in_specs=[IN_S...  4.41 us
    unnamed x31, local copies, waits for them, and re-layouts  4.25 us
  transfers between devices with their start and end apart: 29, of which 9 were waited for; matrix products, arithmetic and copies ran while one was open for 4% of the time, Pallas kernels for 35%

profile of v3, /device:TPU:0, one launch (start us, length us, event | category | flops | bytes accessed | tf_op | source)
XLA Modules:
  0.0 91.0 jit_solution(17175412646041774145)
XLA Ops:
  0.6 4.1 %collective-permute-start.1 = (bf16[32,2048]{1,0:T(8,128)(2,1)}, bf16[32,2048]{1,0:T(8,128)(2,1)S(1)}, u32[]{:S(2)}, u32[]{:S(2)}) collective-permute-start(bf16[32,2048]{1,0:T(8,128)(2,1)} %param.7), channel_id=1, source_target_pairs={{0,16},{1,17},{2,18},{3,19},{4,20},{5,21},{6,22},{7,23},{8,24},{9,... | collective-permute-start | bytes 393224 | tf_op jit(solution)/shard_map/ppermute | solution.py:115
  4.7 1.3 %collective-permute-start.2 = (bf16[32,2048]{1,0:T(8,128)(2,1)}, bf16[32,2048]{1,0:T(8,128)(2,1)S(1)}, u32[]{:S(2)}, u32[]{:S(2)}) collective-permute-start(bf16[32,2048]{1,0:T(8,128)(2,1)} %param.7), channel_id=1, source_target_pairs={{0,24},{1,25},{2,26},{3,27},{4,28},{5,29},{6,30},{7,31},{8,16},{9,... | collective-permute-start | bytes 393224 | tf_op jit(solution)/shard_map/ppermute | solution.py:115
  6.3 0.8 copy.14
  7.1 0.8 copy.15
  8.0 0.9 %pad_maximum_fusion = bf16[32,2176]{1,0:T(8,128)(2,1)S(1)} fusion(bf16[32,128]{1,0:T(8,128)(2,1)S(1)} %select_reduce_fusion.1, bf16[32,2048]{1,0:T(8,128)(2,1)} %param.10), kind=kLoop, calls=%fused_computation.3 | loop fusion | flops 278528 | bytes 278528 | tf_op jit(solution)/shard_map/concatenate | solution.py:470
  8.9 1.6 %collective-permute-start = (bf16[32,2176]{1,0:T(8,128)(2,1)S(1)}, bf16[32,2176]{1,0:T(8,128)(2,1)S(1)}, u32[]{:S(2)}, u32[]{:S(2)}) collective-permute-start(bf16[32,2176]{1,0:T(8,128)(2,1)S(1)} %pad_maximum_fusion), channel_id=1, source_target_pairs={{0,1},{1,0},{2,3},{3,2},{4,5},{5,4},{6,7},{7,6},{8,9},{9,8},{10,11... | collective-permute-start | bytes 417800 | tf_op jit(solution)/shard_map/ppermute | solution.py:115
  10.5 0.9 %constant_dynamic-update-slice_fusion.3 = bf16[128,2048]{1,0:T(8,128)(2,1)S(1)} fusion(bf16[32,2048]{1,0:T(8,128)(2,1)} %param.7), kind=kLoop, calls=%fused_computation.10 | loop fusion | bytes 262144
  11.4 3.6 %collective-permute-done.1 = bf16[32,2048]{1,0:T(8,128)(2,1)S(1)} collective-permute-done((bf16[32,2048]{1,0:T(8,128)(2,1)}, bf16[32,2048]{1,0:T(8,128)(2,1)S(1)}, u32[]{:S(2)}, u32[]{:S(2)}) %collective-permute-start.1) | collective-permute-done | bytes 131104 | tf_op jit(solution)/shard_map/ppermute | solution.py:115
  15.5 1.6 %collective-permute-start.7 = (bf16[128,2048]{1,0:T(8,128)(2,1)S(1)}, bf16[128,2048]{1,0:T(8,128)(2,1)}, u32[]{:S(2)}, u32[]{:S(2)}) collective-permute-start(bf16[128,2048]{1,0:T(8,128)(2,1)S(1)} %constant_dynamic-update-slice_fusion.refs_0_), channel_id=1, source_target_pairs={{0,4},{1,5},{2,6},{3,7},{4,0},{5,1},{6,2},{7,3},{8,12},{9,13},{10,... | collective-permute-start | bytes 1572872 | tf_op jit(solution)/shard_map/ppermute | solution.py:115
  17.2 1.5 %collective-permute-start.8 = (bf16[128,2048]{1,0:T(8,128)(2,1)S(1)}, bf16[128,2048]{1,0:T(8,128)(2,1)S(1)}, u32[]{:S(2)}, u32[]{:S(2)}) collective-permute-start(bf16[128,2048]{1,0:T(8,128)(2,1)S(1)} %constant_dynamic-update-slice_fusion.refs_0_), channel_id=1, source_target_pairs={{0,1},{1,0},{2,3},{3,2},{4,5},{5,4},{6,7},{7,6},{8,9},{9,8},{10,11... | collective-permute-start | bytes 1572872 | tf_op jit(solution)/shard_map/ppermute | solution.py:115
  18.6 4.1 %collective-permute-start.4 = (bf16[32,2176]{1,0:T(8,128)(2,1)S(1)}, bf16[32,2176]{1,0:T(8,128)(2,1)S(1)}, u32[]{:S(2)}, u32[]{:S(2)}) collective-permute-start(bf16[32,2176]{1,0:T(8,128)(2,1)S(1)} %pad_maximum_fusion), channel_id=1, source_target_pairs={{0,16},{1,17},{2,18},{3,19},{4,20},{5,21},{6,22},{7,23},{8,24},{9,... | collective-permute-start | bytes 417800 | tf_op jit(solution)/shard_map/ppermute | solution.py:115
  23.3 9.1 %collective-permute-done.4 = bf16[32,2176]{1,0:T(8,128)(2,1)S(1)} collective-permute-done((bf16[32,2176]{1,0:T(8,128)(2,1)S(1)}, bf16[32,2176]{1,0:T(8,128)(2,1)S(1)}, u32[]{:S(2)}, u32[]{:S(2)}) %collective-permute-start.4) | collective-permute-done | bytes 139296 | tf_op jit(solution)/shard_map/ppermute | solution.py:115
  32.4 1.0 %collective-permute-done.6 = bf16[32,2176]{1,0:T(8,128)(2,1)S(1)} collective-permute-done((bf16[32,2176]{1,0:T(8,128)(2,1)S(1)}, bf16[32,2176]{1,0:T(8,128)(2,1)S(1)}, u32[]{:S(2)}, u32[]{:S(2)}) %collective-permute-start.6) | collective-permute-done | bytes 139296 | tf_op jit(solution)/shard_map/ppermute | solution.py:115
  35.2 0.8 copy-done.9
  36.1 6.3 %shard_map.110 = (bf16[768,2048]{1,0:T(8,128)(2,1)S(1)}, bf16[768,2048]{1,0:T(8,128)(2,1)S(1)}, bf16[2048,768]{1,0:T(8,128)(2,1)S(1)}, bf16[512,2048]{1,0:T(8,12...) custom-call(bf16[128,2048]{1,0:T(8,128)(2,1)} %copy-done.8, ...), custom_call_target="tpu_custom_call" | custom-call | flops 3221225472 | bytes 2097152 | tf_op jit(solution)/shard_map/pallas_call | solution.py:201
  42.4 3.7 %shard_map.111 = (bf16[128,2176]{1,0:T(8,128)(2,1)S(1)}, bf16[128,2176]{1,0:T(8,128)(2,1)S(1)}, bf16[256,2176]{1,0:T(8,128)(2,1)S(1)}, bf16[256,2304]{1,0:T(8,128)(2,1)S(1)}, f32[8,128]{1,0:T(8,128)S(1)}) custom-call(s32[2]{0:T(128)S(1)} %pad_add_fusion.place_ref._, bf16[128,2176]{1,0:T(8,128)(2,1)S(1)} %constant_dynamic-update-slice_fusion.4.own_ref, ...), custom_call_target="tpu_custom_call" | custom-call | tf_op jit(solution)/shard_map/pallas_call | solution.py:278
  46.2 2.3 %collective-permute-done.13.refs_1_.refs_9_ = bf16[128,2048]{1,0:T(8,128)(2,1)S(1)} collective-permute-done((bf16[128,2048]{1,0:T(8,128)(2,1)}, bf16[128,2048]{1,0:T(8,128)(2,1)S(1)}, u32[]{:S(2)}, u32[]{:S(2)}) %collective-permute-start.13) | collective-permute-done | bytes 524320 | tf_op jit(solution)/shard_map/ppermute | solution.py:115
  49.3 1.4 %collective-permute-done.15.other_ref = bf16[128,2176]{1,0:T(8,128)(2,1)S(1)} collective-permute-done((bf16[128,2176]{1,0:T(8,128)(2,1)S(1)}, bf16[128,2176]{1,0:T(8,128)(2,1)S(1)}, u32[]{:S(2)}, u32[]{:S(2)}) %collective-permute-start.15) | collective-permute-done | bytes 557088 | tf_op jit(solution)/shard_map/ppermute | solution.py:115
  50.7 3.6 %shard_map.112 = (bf16[128,2176]{1,0:T(8,128)(2,1)S(1)}, bf16[128,2176]{1,0:T(8,128)(2,1)S(1)}, bf16[256,2176]{1,0:T(8,128)(2,1)S(1)}, bf16[256,2304]{1,0:T(8,128)(2,1)S(1)}, f32[8,128]{1,0:T(8,128)}) custom-call(s32[2]{0:T(128)S(1)} %pad_add_fusion.place_ref._, bf16[128,2176]{1,0:T(8,128)(2,1)S(1)} %collective-permute-done.12.own_ref, ...), custom_call_target="tpu_custom_call" | custom-call | tf_op jit(solution)/shard_map/pallas_call | solution.py:278
  54.6 1.8 %collective-permute-start.21 = (bf16[32,2176]{1,0:T(8,128)(2,1)S(1)}, bf16[32,2176]{1,0:T(8,128)(2,1)S(1)}, u32[]{:S(2)}, u32[]{:S(2)}) collective-permute-start(bf16[32,2176]{1,0:T(8,128)(2,1)S(1)} %collective-permute-done), channel_id=1, source_target_pairs={{0,16},{1,17},{2,18},{3,19},{4,20},{5,21},{6,22},{7,23},{8,24},{9,... | collective-permute-start | bytes 417800 | tf_op jit(solution)/shard_map/ppermute | solution.py:115
  56.3 2.7 %collective-permute-start.22 = (bf16[32,2176]{1,0:T(8,128)(2,1)S(1)}, bf16[32,2176]{1,0:T(8,128)(2,1)S(1)}, u32[]{:S(2)}, u32[]{:S(2)}) collective-permute-start(bf16[32,2176]{1,0:T(8,128)(2,1)S(1)} %collective-permute-done), channel_id=1, source_target_pairs={{0,24},{1,25},{2,26},{3,27},{4,28},{5,29},{6,30},{7,31},{8,16},{9,... | collective-permute-start | bytes 417800 | tf_op jit(solution)/shard_map/ppermute | solution.py:115
  59.2 1.4 %collective-permute-start.19 = (bf16[128,2176]{1,0:T(8,128)(2,1)S(1)}, bf16[128,2176]{1,0:T(8,128)(2,1)S(1)}, u32[]{:S(2)}, u32[]{:S(2)}) collective-permute-start(bf16[128,2176]{1,0:T(8,128)(2,1)S(1)} %add_convert_fusion.1), channel_id=1, source_target_pairs={{0,4},{1,5},{2,6},{3,7},{4,0},{5,1},{6,2},{7,3},{8,12},{9,13},{10,... | collective-permute-start | bytes 1671176 | tf_op jit(solution)/shard_map/ppermute | solution.py:115
  61.2 4.4 %shard_map.113 = (bf16[384,2048]{1,0:T(8,128)(2,1)S(1)}, bf16[384,2048]{1,0:T(8,128)(2,1)S(1)}, bf16[384,2048]{1,0:T(8,128)(2,1)S(1)}, f32[8,128]{1,0:T(8,128)S(1)}) custom-call(s32[2]{0:T(128)S(1)} %pad_add_fusion.place_ref._, bf16[256,2304]{1,0:T(8,128)(2,1)S(1)} %get-tuple-element.87.column_ref, bf16[256,2304]{1,0:T(8,128)(2,1)S(1)} %get-tuple-element.88.near_ref, ...), custom_call_target="tpu_custom_call" | custom-call | flops 2415919104 | bytes 4718592 | tf_op jit(solution)/shard_map/pallas_call | solution.py:319
  65.6 4.8 %shard_map.114 = (f32[384,512]{1,0:T(8,128)S(1)}, f32[384,512]{1,0:T(8,128)S(1)}, f32[384,512]{1,0:T(8,128)S(1)}, f32[8,128]{1,0:T(8,128)S(1)}) custom-call(s32[2]{0:T(128)S(1)} %pad_add_fusion.place_ref._, bf16[128,2048]{1,0:T(8,128)(2,1)} %copy-done, bf16[128,2048]{1,0:T(8,128)(2,1)} %copy-done.1, bf16[128,2048]{1,0:T(8,128)(2,1)} %copy-done.2, ...), custom_call_target="tpu_custom_call" | custom-call | flops 1610612736 | bytes 2097152 | tf_op jit(solution)/shard_map/pallas_call | solution.py:359
  70.4 3.2 %collective-permute-done.19 = bf16[128,2176]{1,0:T(8,128)(2,1)S(1)} collective-permute-done((bf16[128,2176]{1,0:T(8,128)(2,1)S(1)}, bf16[128,2176]{1,0:T(8,128)(2,1)S(1)}, u32[]{:S(2)}, u32[]{:S(2)}) %collective-permute-start.19) | collective-permute-done | bytes 557088 | tf_op jit(solution)/shard_map/ppermute | solution.py:115
  73.8 0.9 collective-permute-done.20.refs_1_
  75.4 1.4 %collective-permute-start.24 = (bf16[32,2176]{1,0:T(8,128)(2,1)S(1)}, bf16[32,2176]{1,0:T(8,128)(2,1)S(1)}, u32[]{:S(2)}, u32[]{:S(2)}) collective-permute-start(bf16[32,2176]{1,0:T(8,128)(2,1)S(1)} %get-tuple-element.122), channel_id=1, source_target_pairs={{0,16},{1,17},{2,18},{3,19},{4,20},{5,21},{6,22},{7,23},{8,24},{9,... | collective-permute-start | bytes 417800 | tf_op jit(solution)/shard_map/ppermute | solution.py:115
  76.9 2.7 %collective-permute-start.25 = (bf16[32,2176]{1,0:T(8,128)(2,1)S(1)}, bf16[32,2176]{1,0:T(8,128)(2,1)S(1)}, u32[]{:S(2)}, u32[]{:S(2)}) collective-permute-start(bf16[32,2176]{1,0:T(8,128)(2,1)S(1)} %get-tuple-element.121), channel_id=1, source_target_pairs={{0,24},{1,25},{2,26},{3,27},{4,28},{5,29},{6,30},{7,31},{8,16},{9,... | collective-permute-start | bytes 417800 | tf_op jit(solution)/shard_map/ppermute | solution.py:115
  79.6 0.8 copy-done.6
  80.6 8.7 %shard_map.115 = (bf16[1,384,2048]{2,1,0:T(8,128)(2,1)}, bf16[1,384,2048]{2,1,0:T(8,128)(2,1)}, bf16[1,384,2048]{2,1,0:T(8,128)(2,1)}) custom-call(s32[2]{0:T(128)S(1)} %pad_add_fusion.place_ref._, bf16[128,2176]{1,0:T(8,128)(2,1)} %copy-done.4, bf16[128,2176]{1,0:T(8,128)(2,1)} %copy-done.5, bf16[128,2176]{1,0:T(8,128)(2,1)} %copy-done.6, ...), custom_call_target="tpu_custom_call" | custom-call | flops 3221225472 | bytes 13631488 | tf_op jit(solution)/shard_map/pallas_call | solution.py:421
  89.5 0.7 slice.24
  90.3 0.7 copy.16
  (77 shorter events, 6.5 us)
Async XLA Ops:
  0.6 14.3 %collective-permute-start.1 = (bf16[32,2048]{1,0:T(8,128)(2,1)}, bf16[32,2048]{1,0:T(8,128)(2,1)S(1)}, u32[]{:S(2)}, u32[]{:S(2)}) collective-permute-start(bf16[32,2048]{1,0:T(8,128)(2,1)} %param.7), channel_id=1, source_target_pairs={{0,16},{1,17},{2,18},{3,19},{4,20},{5,21},{6,22},{7,23},{8,24},{9,... | collective-permute-start | bytes 393224 | tf_op jit(solution)/shard_map/ppermute | solution.py:115
  4.7 10.2 %collective-permute-start.2 = (bf16[32,2048]{1,0:T(8,128)(2,1)}, bf16[32,2048]{1,0:T(8,128)(2,1)S(1)}, u32[]{:S(2)}, u32[]{:S(2)}) collective-permute-start(bf16[32,2048]{1,0:T(8,128)(2,1)} %param.7), channel_id=1, source_target_pairs={{0,24},{1,25},{2,26},{3,27},{4,28},{5,29},{6,30},{7,31},{8,16},{9,... | collective-permute-start | bytes 393224 | tf_op jit(solution)/shard_map/ppermute | solution.py:115
  6.1 9.4 %collective-permute-start.3 = (bf16[32,2048]{1,0:T(8,128)(2,1)}, bf16[32,2048]{1,0:T(8,128)(2,1)S(1)}, u32[]{:S(2)}, u32[]{:S(2)}) collective-permute-start(bf16[32,2048]{1,0:T(8,128)(2,1)} %param.7), channel_id=1, source_target_pairs={{0,8},{1,9},{2,10},{3,11},{4,12},{5,13},{6,14},{7,15},{8,0},{9,1},... | collective-permute-start | bytes 393224 | tf_op jit(solution)/shard_map/ppermute | solution.py:115
  8.9 6.5 %collective-permute-start = (bf16[32,2176]{1,0:T(8,128)(2,1)S(1)}, bf16[32,2176]{1,0:T(8,128)(2,1)S(1)}, u32[]{:S(2)}, u32[]{:S(2)}) collective-permute-start(bf16[32,2176]{1,0:T(8,128)(2,1)S(1)} %pad_maximum_fusion), channel_id=1, source_target_pairs={{0,1},{1,0},{2,3},{3,2},{4,5},{5,4},{6,7},{7,6},{8,9},{9,8},{10,11... | collective-permute-start | bytes 417800 | tf_op jit(solution)/shard_map/ppermute | solution.py:115
  15.5 19.7 %copy-start.8 = (bf16[128,2048]{1,0:T(8,128)(2,1)}, bf16[128,2048]{1,0:T(8,128)(2,1)S(1)}, u32[]{:S(2)}) copy-start(bf16[128,2048]{1,0:T(8,128)(2,1)S(1)} %constant_dynamic-update-slice_fusion.refs_0_) | copy-start | bytes 1572868
  15.5 17.9 %collective-permute-start.7 = (bf16[128,2048]{1,0:T(8,128)(2,1)S(1)}, bf16[128,2048]{1,0:T(8,128)(2,1)}, u32[]{:S(2)}, u32[]{:S(2)}) collective-permute-start(bf16[128,2048]{1,0:T(8,128)(2,1)S(1)} %constant_dynamic-update-slice_fusion.refs_0_), channel_id=1, source_target_pairs={{0,4},{1,5},{2,6},{3,7},{4,0},{5,1},{6,2},{7,3},{8,12},{9,13},{10,... | collective-permute-start | bytes 1572872 | tf_op jit(solution)/shard_map/ppermute | solution.py:115
  17.2 16.3 %collective-permute-start.8 = (bf16[128,2048]{1,0:T(8,128)(2,1)S(1)}, bf16[128,2048]{1,0:T(8,128)(2,1)S(1)}, u32[]{:S(2)}, u32[]{:S(2)}) collective-permute-start(bf16[128,2048]{1,0:T(8,128)(2,1)S(1)} %constant_dynamic-update-slice_fusion.refs_0_), channel_id=1, source_target_pairs={{0,1},{1,0},{2,3},{3,2},{4,5},{5,4},{6,7},{7,6},{8,9},{9,8},{10,11... | collective-permute-start | bytes 1572872 | tf_op jit(solution)/shard_map/ppermute | solution.py:115
  18.6 13.8 %collective-permute-start.4 = (bf16[32,2176]{1,0:T(8,128)(2,1)S(1)}, bf16[32,2176]{1,0:T(8,128)(2,1)S(1)}, u32[]{:S(2)}, u32[]{:S(2)}) collective-permute-start(bf16[32,2176]{1,0:T(8,128)(2,1)S(1)} %pad_maximum_fusion), channel_id=1, source_target_pairs={{0,16},{1,17},{2,18},{3,19},{4,20},{5,21},{6,22},{7,23},{8,24},{9,... | collective-permute-start | bytes 417800 | tf_op jit(solution)/shard_map/ppermute | solution.py:115
  22.7 9.7 %collective-permute-start.5 = (bf16[32,2176]{1,0:T(8,128)(2,1)S(1)}, bf16[32,2176]{1,0:T(8,128)(2,1)S(1)}, u32[]{:S(2)}, u32[]{:S(2)}) collective-permute-start(bf16[32,2176]{1,0:T(8,128)(2,1)S(1)} %pad_maximum_fusion), channel_id=1, source_target_pairs={{0,24},{1,25},{2,26},{3,27},{4,28},{5,29},{6,30},{7,31},{8,16},{9,... | collective-permute-start | bytes 417800 | tf_op jit(solution)/shard_map/ppermute | solution.py:115
  23.2 10.2 %collective-permute-start.6 = (bf16[32,2176]{1,0:T(8,128)(2,1)S(1)}, bf16[32,2176]{1,0:T(8,128)(2,1)S(1)}, u32[]{:S(2)}, u32[]{:S(2)}) collective-permute-start(bf16[32,2176]{1,0:T(8,128)(2,1)S(1)} %pad_maximum_fusion), channel_id=1, source_target_pairs={{0,8},{1,9},{2,10},{3,11},{4,12},{5,13},{6,14},{7,15},{8,0},{9,1},... | collective-permute-start | bytes 417800 | tf_op jit(solution)/shard_map/ppermute | solution.py:115
  32.4 2.8 %collective-permute-start.10 = (bf16[128,2048]{1,0:T(8,128)(2,1)S(1)}, bf16[128,2048]{1,0:T(8,128)(2,1)S(1)}, u32[]{:S(2)}, u32[]{:S(2)}) collective-permute-start(bf16[128,2048]{1,0:T(8,128)(2,1)S(1)} %constant_dynamic-update-slice_fusion.refs_0_), channel_id=1, source_target_pairs={{0,2},{1,3},{2,0},{3,1},{4,6},{5,7},{6,4},{7,5},{8,10},{9,11},{10,... | collective-permute-start | bytes 1572872 | tf_op jit(solution)/shard_map/ppermute | solution.py:115
  33.5 9.0 %copy-start = (bf16[128,2048]{1,0:T(8,128)(2,1)}, bf16[128,2048]{1,0:T(8,128)(2,1)S(1)}, u32[]{:S(2)}) copy-start(bf16[128,2048]{1,0:T(8,128)(2,1)S(1)} %collective-permute-done.8.refs_0_.refs_8_) | copy-start | bytes 1572868
  33.5 2.6 %collective-permute-start.11 = (bf16[128,2048]{1,0:T(8,128)(2,1)}, bf16[128,2048]{1,0:T(8,128)(2,1)}, u32[]{:S(2)}, u32[]{:S(2)}) collective-permute-start(bf16[128,2048]{1,0:T(8,128)(2,1)} %collective-permute-done.7.refs_2_), channel_id=1, source_target_pairs={{0,2},{1,3},{2,0},{3,1},{4,6},{5,7},{6,4},{7,5},{8,10},{9,11},{10,... | collective-permute-start | bytes 1572872 | tf_op jit(solution)/shard_map/ppermute | solution.py:115
  33.6 8.8 %collective-permute-start.9 = (bf16[128,2176]{1,0:T(8,128)(2,1)S(1)}, bf16[128,2176]{1,0:T(8,128)(2,1)S(1)}, u32[]{:S(2)}, u32[]{:S(2)}) collective-permute-start(bf16[128,2176]{1,0:T(8,128)(2,1)S(1)} %constant_dynamic-update-slice_fusion.4.own_ref), channel_id=1, source_target_pairs={{0,2},{1,3},{2,0},{3,1},{4,6},{5,7},{6,4},{7,5},{8,10},{9,11},{10,... | collective-permute-start | bytes 1671176 | tf_op jit(solution)/shard_map/ppermute | solution.py:115
  34.2 14.6 %collective-permute-start.12 = (bf16[128,2176]{1,0:T(8,128)(2,1)S(1)}, bf16[128,2176]{1,0:T(8,128)(2,1)S(1)}, u32[]{:S(2)}, u32[]{:S(2)}) collective-permute-start(bf16[128,2176]{1,0:T(8,128)(2,1)S(1)} %constant_dynamic-update-slice_fusion.4.own_ref), channel_id=1, source_target_pairs={{0,4},{1,5},{2,6},{3,7},{4,0},{5,1},{6,2},{7,3},{8,12},{9,13},{10,... | collective-permute-start | bytes 1671176 | tf_op jit(solution)/shard_map/ppermute | solution.py:115
  34.7 13.8 %collective-permute-start.13 = (bf16[128,2048]{1,0:T(8,128)(2,1)}, bf16[128,2048]{1,0:T(8,128)(2,1)S(1)}, u32[]{:S(2)}, u32[]{:S(2)}) collective-permute-start(bf16[128,2048]{1,0:T(8,128)(2,1)} %collective-permute-done.7.refs_2_), channel_id=1, source_target_pairs={{0,1},{1,0},{2,3},{3,2},{4,5},{5,4},{6,7},{7,6},{8,9},{9,8},{10,11... | collective-permute-start | bytes 1572872 | tf_op jit(solution)/shard_map/ppermute | solution.py:115
  36.0 12.5 %collective-permute-start.14 = (bf16[128,2048]{1,0:T(8,128)(2,1)S(1)}, bf16[128,2048]{1,0:T(8,128)(2,1)S(1)}, u32[]{:S(2)}, u32[]{:S(2)}) collective-permute-start(bf16[128,2048]{1,0:T(8,128)(2,1)S(1)} %collective-permute-done.8.refs_0_.refs_8_), channel_id=1, source_target_pairs={{0,2},{1,3},{2,0},{3,1},{4,6},{5,7},{6,4},{7,5},{8,10},{9,11},{10,... | collective-permute-start | bytes 1572872 | tf_op jit(solution)/shard_map/ppermute | solution.py:115
  48.8 2.0 %collective-permute-start.15 = (bf16[128,2176]{1,0:T(8,128)(2,1)S(1)}, bf16[128,2176]{1,0:T(8,128)(2,1)S(1)}, u32[]{:S(2)}, u32[]{:S(2)}) collective-permute-start(bf16[128,2176]{1,0:T(8,128)(2,1)S(1)} %collective-permute-done.12.own_ref), channel_id=1, source_target_pairs={{0,2},{1,3},{2,0},{3,1},{4,6},{5,7},{6,4},{7,5},{8,10},{9,11},{10,... | collective-permute-start | bytes 1671176 | tf_op jit(solution)/shard_map/ppermute | solution.py:115
  48.8 5.6 %collective-permute-start.17 = (bf16[128,2176]{1,0:T(8,128)(2,1)S(1)}, bf16[128,2176]{1,0:T(8,128)(2,1)S(1)}, u32[]{:S(2)}, u32[]{:S(2)}) collective-permute-start(bf16[128,2176]{1,0:T(8,128)(2,1)S(1)} %get-tuple-element.81), channel_id=1, source_target_pairs={{0,2},{1,3},{2,0},{3,1},{4,6},{5,7},{6,4},{7,5},{8,10},{9,11},{10,... | collective-permute-start | bytes 1671176 | tf_op jit(solution)/shard_map/ppermute | solution.py:115
  49.3 5.0 %collective-permute-start.16 = (bf16[128,2048]{1,0:T(8,128)(2,1)S(1)}, bf16[128,2048]{1,0:T(8,128)(2,1)S(1)}, u32[]{:S(2)}, u32[]{:S(2)}) collective-permute-start(bf16[128,2048]{1,0:T(8,128)(2,1)S(1)} %collective-permute-done.13.refs_1_.refs_9_), channel_id=1, source_target_pairs={{0,2},{1,3},{2,0},{3,1},{4,6},{5,7},{6,4},{7,5},{8,10},{9,11},{10,... | collective-permute-start | bytes 1572872 | tf_op jit(solution)/shard_map/ppermute | solution.py:115
  54.3 11.3 %copy-start.3 = (bf16[128,2048]{1,0:T(8,128)(2,1)}, bf16[128,2048]{1,0:T(8,128)(2,1)S(1)}, u32[]{:S(2)}) copy-start(bf16[128,2048]{1,0:T(8,128)(2,1)S(1)} %collective-permute-done.16.refs_3_.refs_11_) | copy-start | bytes 1572868
  54.4 4.7 %collective-permute-start.18 = (bf16[128,2176]{1,0:T(8,128)(2,1)S(1)}, bf16[128,2176]{1,0:T(8,128)(2,1)S(1)}, u32[]{:S(2)}, u32[]{:S(2)}) collective-permute-start(bf16[128,2176]{1,0:T(8,128)(2,1)S(1)} %get-tuple-element.84), channel_id=1, source_target_pairs={{0,2},{1,3},{2,0},{3,1},{4,6},{5,7},{6,4},{7,5},{8,10},{9,11},{10,... | collective-permute-start | bytes 1671176 | tf_op jit(solution)/shard_map/ppermute | solution.py:115
  54.6 19.2 %collective-permute-start.21 = (bf16[32,2176]{1,0:T(8,128)(2,1)S(1)}, bf16[32,2176]{1,0:T(8,128)(2,1)S(1)}, u32[]{:S(2)}, u32[]{:S(2)}) collective-permute-start(bf16[32,2176]{1,0:T(8,128)(2,1)S(1)} %collective-permute-done), channel_id=1, source_target_pairs={{0,16},{1,17},{2,18},{3,19},{4,20},{5,21},{6,22},{7,23},{8,24},{9,... | collective-permute-start | bytes 417800 | tf_op jit(solution)/shard_map/ppermute | solution.py:115
  56.3 17.5 %collective-permute-start.22 = (bf16[32,2176]{1,0:T(8,128)(2,1)S(1)}, bf16[32,2176]{1,0:T(8,128)(2,1)S(1)}, u32[]{:S(2)}, u32[]{:S(2)}) collective-permute-start(bf16[32,2176]{1,0:T(8,128)(2,1)S(1)} %collective-permute-done), channel_id=1, source_target_pairs={{0,24},{1,25},{2,26},{3,27},{4,28},{5,29},{6,30},{7,31},{8,16},{9,... | collective-permute-start | bytes 417800 | tf_op jit(solution)/shard_map/ppermute | solution.py:115
  59.1 14.8 %collective-permute-start.23 = (bf16[32,2176]{1,0:T(8,128)(2,1)S(1)}, bf16[32,2176]{1,0:T(8,128)(2,1)S(1)}, u32[]{:S(2)}, u32[]{:S(2)}) collective-permute-start(bf16[32,2176]{1,0:T(8,128)(2,1)S(1)} %collective-permute-done), channel_id=1, source_target_pairs={{0,8},{1,9},{2,10},{3,11},{4,12},{5,13},{6,14},{7,15},{8,0},{9,1},... | collective-permute-start | bytes 417800 | tf_op jit(solution)/shard_map/ppermute | solution.py:115
  59.2 14.4 %collective-permute-start.19 = (bf16[128,2176]{1,0:T(8,128)(2,1)S(1)}, bf16[128,2176]{1,0:T(8,128)(2,1)S(1)}, u32[]{:S(2)}, u32[]{:S(2)}) collective-permute-start(bf16[128,2176]{1,0:T(8,128)(2,1)S(1)} %add_convert_fusion.1), channel_id=1, source_target_pairs={{0,4},{1,5},{2,6},{3,7},{4,0},{5,1},{6,2},{7,3},{8,12},{9,13},{10,... | collective-permute-start | bytes 1671176 | tf_op jit(solution)/shard_map/ppermute | solution.py:115
  60.6 14.1 %collective-permute-start.20 = (bf16[128,2176]{1,0:T(8,128)(2,1)S(1)}, bf16[128,2176]{1,0:T(8,128)(2,1)S(1)}, u32[]{:S(2)}, u32[]{:S(2)}) collective-permute-start(bf16[128,2176]{1,0:T(8,128)(2,1)S(1)} %collective-permute-done.12.own_ref), channel_id=1, source_target_pairs={{0,1},{1,0},{2,3},{3,2},{4,5},{5,4},{6,7},{7,6},{8,9},{9,8},{10,11... | collective-permute-start | bytes 1671176 | tf_op jit(solution)/shard_map/ppermute | solution.py:115
  74.8 4.8 %collective-permute-start.27 = (bf16[128,2176]{1,0:T(8,128)(2,1)S(1)}, bf16[128,2176]{1,0:T(8,128)(2,1)S(1)}, u32[]{:S(2)}, u32[]{:S(2)}) collective-permute-start(bf16[128,2176]{1,0:T(8,128)(2,1)S(1)} %constant_dynamic-update-slice_fusion.8.refs_0_), channel_id=1, source_target_pairs={{0,2},{1,3},{2,0},{3,1},{4,6},{5,7},{6,4},{7,5},{8,10},{9,11},{10,... | collective-permute-start | bytes 1671176 | tf_op jit(solution)/shard_map/ppermute | solution.py:115
  74.9 4.7 %collective-permute-start.28 = (bf16[128,2176]{1,0:T(8,128)(2,1)S(1)}, bf16[128,2176]{1,0:T(8,128)(2,1)S(1)}, u32[]{:S(2)}, u32[]{:S(2)}) collective-permute-start(bf16[128,2176]{1,0:T(8,128)(2,1)S(1)} %collective-permute-done.20.refs_1_), channel_id=1, source_target_pairs={{0,2},{1,3},{2,0},{3,1},{4,6},{5,7},{6,4},{7,5},{8,10},{9,11},{10,... | collective-permute-start | bytes 1671176 | tf_op jit(solution)/shard_map/ppermute | solution.py:115
  75.4 13.9 %collective-permute-start.24 = (bf16[32,2176]{1,0:T(8,128)(2,1)S(1)}, bf16[32,2176]{1,0:T(8,128)(2,1)S(1)}, u32[]{:S(2)}, u32[]{:S(2)}) collective-permute-start(bf16[32,2176]{1,0:T(8,128)(2,1)S(1)} %get-tuple-element.122), channel_id=1, source_target_pairs={{0,16},{1,17},{2,18},{3,19},{4,20},{5,21},{6,22},{7,23},{8,24},{9,... | collective-permute-start | bytes 417800 | tf_op jit(solution)/shard_map/ppermute | solution.py:115
  76.9 12.5 %collective-permute-start.25 = (bf16[32,2176]{1,0:T(8,128)(2,1)S(1)}, bf16[32,2176]{1,0:T(8,128)(2,1)S(1)}, u32[]{:S(2)}, u32[]{:S(2)}) collective-permute-start(bf16[32,2176]{1,0:T(8,128)(2,1)S(1)} %get-tuple-element.121), channel_id=1, source_target_pairs={{0,24},{1,25},{2,26},{3,27},{4,28},{5,29},{6,30},{7,31},{8,16},{9,... | collective-permute-start | bytes 417800 | tf_op jit(solution)/shard_map/ppermute | solution.py:115
  79.6 9.8 %collective-permute-start.26 = (bf16[32,2176]{1,0:T(8,128)(2,1)S(1)}, bf16[32,2176]{1,0:T(8,128)(2,1)S(1)}, u32[]{:S(2)}, u32[]{:S(2)}) collective-permute-start(bf16[32,2176]{1,0:T(8,128)(2,1)S(1)} %get-tuple-element.120), channel_id=1, source_target_pairs={{0,8},{1,9},{2,10},{3,11},{4,12},{5,13},{6,14},{7,15},{8,0},{9,1},... | collective-permute-start | bytes 417800 | tf_op jit(solution)/shard_map/ppermute | solution.py:115
  (7 other events, 23.9 us)

commit v4 on v3

--- a/solution.py
+++ b/solution.py
@@ -158,6 +158,15 @@
         pairs.append((piece, target.at[pl.ds(first, piece.shape[0])]))
         first += piece.shape[0]
     return pairs
+
+
+def as_cotangents(x_refs):
+    views = []
+    for column, near in (x_refs[:2], x_refs[2:]):
+        block = column.shape[0] // 4
+        views += [column.at[pl.ds(0, 2 * block)], near.at[pl.ds(0, block)]]
+        views += [column.at[pl.ds(2 * block, 2 * block)], near.at[pl.ds(block, 3 * block)]]
+    return views
 
 
 def forward_kernel(*refs):
@@ -291,15 +300,28 @@
     )(place, own, other, *[kept(value) for value in (*saved, *weights)], after)
 
 
-def own_gradient_kernel(place_ref, column_ref, near_ref, x_ref, column_cot, near_cot, *refs):
-    outs, token_out, lefts = refs[:3], refs[3], refs[4]
+def own_gradient_kernel(place_ref, *refs):
+    column_ref, near_ref, x_ref, column_cot, near_cot = refs[:5]
+    x_refs, weight_refs = refs[5:9], refs[9:11]
+    outs, (slope_out, swish_out, hidden_out, token_out) = refs[11:14], refs[14:18]
+    lefts, rows, gate_ref, up_ref, sems = refs[18:]
     share, tile = outs[0].shape
     units = column_ref.shape[1] // 3
+    start = pl.multiple_of(place_ref[1] * share, 128)
+    own = pl.ds(start, share)
+    copies = [
+        pltpu.make_async_copy(source, target, sems.at[i])
+        for i, (source, target) in enumerate(
+            placed(as_cotangents(x_refs), rows)
+            + [(weight_refs[0].at[0, own], gate_ref), (weight_refs[1].at[0, own], up_ref)]
+        )
+    ]
 
     @pl.when(pl.program_id(0) == 0)
     def _():
+        for copy in copies:
+            copy.start()
         token_out[...] = jnp.zeros_like(token_out)
-        start = pl.multiple_of(place_ref[1] * share, 128)
         for i in range(3):
             lefts[i] = jnp.concatenate(
                 [ref[:, pl.ds(start + i * units, share)] for ref in (column_ref, near_ref)], axis=0
@@ -307,75 +329,59 @@
 
     chunk = pl.ds(pl.multiple_of(pl.program_id(0) * tile, tile), tile)
     cot_rows = jnp.concatenate([column_cot[:, chunk], near_cot[:, chunk]], axis=0)
-    for i, rows in enumerate((x_ref[:, chunk], x_ref[:, chunk], cot_rows)):
-        outs[i][...] = jnp.dot(lefts[i], rows, preferred_element_type=jnp.float32).astype(
+    for i, right in enumerate((x_ref[:, chunk], x_ref[:, chunk], cot_rows)):
+        outs[i][...] = jnp.dot(lefts[i], right, preferred_element_type=jnp.float32).astype(
             jnp.bfloat16
         )
 
-
-def own_gradients(place, lefts, x_rows, cot_rows, share):
+    @pl.when(pl.program_id(0) == pl.num_programs(0) - 1)
+    def _():
+        for copy in copies:
+            copy.wait()
+        pre_gate = contract_last(gate_ref[...], rows[...])
+        pre_up = contract_last(up_ref[...], rows[...])
+        gate_sigmoid = jax.nn.sigmoid(pre_gate)
+        swish = pre_gate * gate_sigmoid
+        slope_out[...] = (pre_up * gate_sigmoid * (1.0 + pre_gate * (1.0 - gate_sigmoid))).astype(
+            jnp.bfloat16
+        )
+        swish_out[...] = swish.astype(jnp.bfloat16)
+        hidden_out[...] = (swish * pre_up).astype(jnp.bfloat16)
+
+
+def own_gradients(place, lefts, x_rows, cot_rows, x_away, weights, share):
     rows, width = x_rows.shape
     tile = 2 * TILE
+    half = pltpu.VMEM((share, width), jnp.bfloat16)
     return pl.pallas_call(
         own_gradient_kernel,
         grid=(width // tile,),
-        in_specs=[IN_SMEM] + [IN_VMEM] * 5,
+        in_specs=[IN_SMEM] + [IN_VMEM] * 5 + [IN_HBM] * 6,
         out_specs=[pl.BlockSpec((share, tile), lambda i: (0, i))] * 3
+        + [pl.BlockSpec((share, rows), lambda i: (0, 0))] * 3
         + [pl.BlockSpec((8, 128), lambda i: (0, 0))],
         out_shape=[jax.ShapeDtypeStruct((share, width), jnp.bfloat16)] * 3
-        + [jax.ShapeDtypeStruct((8, 128), jnp.float32)],
-        scratch_shapes=[pltpu.VMEM((3, share, rows), jnp.bfloat16)],
-        **kernel_params(6 * rows * share * width, 6 * share * width),
-    )(place, *[kept(value) for value in (*lefts, x_rows, *cot_rows)])
-
-
-def away_forward_kernel(place_ref, *refs):
-    x_refs, weight_refs = refs[:4], refs[4:6]
-    slope_out, swish_out, hidden_out, token_out, rows, gate_ref, up_ref, sems = refs[7:]
-    share = gate_ref.shape[0]
-    own = pl.ds(pl.multiple_of(place_ref[1] * share, 128), share)
-    copies = fetched(
-        placed(x_refs, rows)
-        + [(weight_refs[0].at[0, own], gate_ref), (weight_refs[1].at[0, own], up_ref)],
-        sems,
-    )
-    token_out[...] = jnp.zeros_like(token_out)
-    for copy in copies[:5]:
-        copy.wait()
-    pre_gate = contract_last(gate_ref[...], rows[...])
-    copies[5].wait()
-    pre_up = contract_last(up_ref[...], rows[...])
-    gate_sigmoid = jax.nn.sigmoid(pre_gate)
-    swish = pre_gate * gate_sigmoid
-    slope_out[...] = pre_up * gate_sigmoid * (1.0 + pre_gate * (1.0 - gate_sigmoid))
-    swish_out[...] = swish
-    hidden_out[...] = swish * pre_up
-
-
-def away_forward(place, x_rows, weights, share, after):
-    width = x_rows[0].shape[1]
-    rows = sum(piece.shape[0] for piece in x_rows)
-    half = pltpu.VMEM((share, width), jnp.bfloat16)
-    return pl.pallas_call(
-        away_forward_kernel,
-        in_specs=[IN_SMEM] + [IN_HBM] * 7,
-        out_specs=[IN_VMEM] * 4,
-        out_shape=[jax.ShapeDtypeStruct((share, rows), jnp.float32)] * 3
+        + [jax.ShapeDtypeStruct((share, rows), jnp.bfloat16)] * 3
         + [jax.ShapeDtypeStruct((8, 128), jnp.float32)],
         scratch_shapes=[
+            pltpu.VMEM((3, share, rows), jnp.bfloat16),
             pltpu.VMEM((rows, width), jnp.bfloat16),
             half,
             half,
-            pltpu.SemaphoreType.DMA((6,)),
+            pltpu.SemaphoreType.DMA((10,)),
         ],
-        **kernel_params(4 * rows * share * width, 2 * rows * width, rows * share, 20),
-    )(place, *[left_out(value) for value in (*x_rows, *weights)], after)
+        **kernel_params(0, 0, 0, 24),
+    )(
+        place,
+        *[kept(value) for value in (*lefts, x_rows, *cot_rows)],
+        *[left_out(value) for value in (*x_away, *weights)],
+    )
 
 
 def whole_gradient_kernel(place_ref, *refs):
-    cot_refs, down_ref, saved_refs, x_refs = refs[:4], refs[4], refs[5:8], refs[8:12]
-    own_refs, outs = refs[12:15], refs[16:19]
-    rows, cot, down, slope, swish, hidden, lefts, sems = refs[19:]
+    cot_refs, down_ref, saved_refs, x_refs = refs[:6], refs[6], refs[7:10], refs[10:14]
+    own_refs, outs = refs[14:17], refs[18:21]
+    rows, cot, down, slope, swish, hidden, lefts, sems = refs[21:]
     share, tile = outs[0].shape[1:]
     width = rows.shape[1]
 
@@ -386,10 +392,10 @@
             placed(cot_refs, cot)
             + [(down_ref.at[0, :, own], down)]
             + list(zip(saved_refs, (slope, swish, hidden)))
-            + placed(x_refs, rows),
+            + placed(as_cotangents(x_refs), rows),
             sems,
         )
-        for copy in copies[:5]:
+        for copy in copies[:7]:
             copy.wait()
         table = cot[:, width:]
         pick = (lax.broadcasted_iota(jnp.int32, (16, table.shape[1]), 1) == place_ref[0]).astype(
@@ -398,12 +404,12 @@
         gates = contract_last(pick, table)[:1]
         raw = jnp.dot(cot[:, :width], down[...], preferred_element_type=jnp.float32).T
         d_hidden = gates * raw
-        for copy in copies[5:8]:
+        for copy in copies[7:10]:
             copy.wait()
-        lefts[0] = (d_hidden * slope[...]).astype(jnp.bfloat16)
-        lefts[1] = (d_hidden * swish[...]).astype(jnp.bfloat16)
-        lefts[2] = (gates * hidden[...]).astype(jnp.bfloat16)
-        for copy in copies[8:]:
+        for i, factor in enumerate((slope, swish)):
+            lefts[i] = (d_hidden * factor[...].astype(jnp.float32)).astype(jnp.bfloat16)
+        lefts[2] = (gates * hidden[...].astype(jnp.float32)).astype(jnp.bfloat16)
+        for copy in copies[10:]:
             copy.wait()
 
     first = pl.multiple_of(pl.program_id(0) * tile, tile)
@@ -417,12 +423,12 @@
     share, width = own[0].shape
     tile = 2 * TILE
     rows = sum(piece.shape[0] for piece in x_rows)
-    half = pltpu.VMEM((share, rows), jnp.float32)
+    half = pltpu.VMEM((share, rows), jnp.bfloat16)
     return pl.pallas_call(
         whole_gradient_kernel,
         grid=(width // tile,),
         in_specs=[IN_SMEM]
-        + [IN_HBM] * 12
+        + [IN_HBM] * 14
         + [pl.BlockSpec((share, tile), lambda i: (0, i))] * 3
         + [IN_HBM],
         out_specs=[pl.BlockSpec((1, share, tile), lambda i: (0, 0, i))] * 3,
@@ -435,7 +441,7 @@
             half,
             half,
             pltpu.VMEM((3, share, rows), jnp.bfloat16),
-            pltpu.SemaphoreType.DMA((12,)),
+            pltpu.SemaphoreType.DMA((18,)),
         ],
         **kernel_params(
             8 * rows * share * width, 4 * rows * width + 12 * share * width, rows * share, 32
@@ -458,13 +464,13 @@
     place = jnp.stack([lax.axis_index("expert"), lax.axis_index("dp")]).astype(jnp.int32)
     group, core, near, low, high = 1, 2, 4, 8, 16
     lanes = -(-experts // 128) * 128
-    named = expert_ids[:, :, None] == jnp.arange(lanes, dtype=jnp.int32)[None, None, :]
+    named = expert_ids.T[:, :, None] == jnp.arange(lanes, dtype=jnp.int32)[None, None, :]
     gate_table = jnp.sum(
-        jnp.where(named, gate_weights.astype(jnp.float32)[:, :, None], 0.0), axis=1
+        jnp.where(named, gate_weights.T.astype(jnp.float32)[:, :, None], 0.0), axis=0
     ).astype(jnp.bfloat16)
 
     def column_of(value):
-        return [swap(value, high), swap(value, low | high), swap(value, low)]
+        return [swap(value, high), swap(value, low), swap(value, low | high)]
 
     weights = (w_gate, w_up, w_down)
     packed = jnp.concatenate([cotangent, gate_table], axis=1)
@@ -476,7 +482,7 @@
     *cot_far, x_near, x_column_away = tied(*column_of(packed), x_near, x_column_away)
     x_near_away = swap(x_near, group)
     cot_column = jnp.concatenate([packed, *cot_far], axis=0)
-    cot_far_away = column_of(cot_mine_away)
+    cot_high_away = swap(cot_mine_away, high)
     cot_near = swap(cot_column, near)
     *kept_weights, x_rows, slope, swish, hidden = forward(
         [x_column, swap(x_column, core), x_near, swap(x_near, core)], weights
@@ -487,42 +493,53 @@
     )
     column_own, column_given = own_part, swap(other_part, core)
     x_column_other = swap(x_column_away, core)
-    cot_near, token, x_near_away, x_column_other = tied(
-        cot_near, token, x_near_away, x_column_other
-    )
+    cot_near, token, x_near_away, x_column_other, cot_high_away = tied(
+        cot_near, token, x_near_away, x_column_other, cot_high_away
+    )
+    cot_first_away = jnp.concatenate([cot_mine_away, cot_high_away], axis=0)
+    cot_second_away, cot_first_other = swap(cot_first_away, low), swap(cot_first_away, core)
     x_near_other = swap(x_near_away, core)
-    cot_near_away = swap(cot_near, group)
+    near_mine_away = swap(cot_mine_away, near)
+    near_far_away = swap(cot_near[packed.shape[0] :], group)
     own_part, other_part, near_cot, near_lefts, _ = backward(
         place, cot_near, swap(cot_near, core), saved, 1, kept_weights, token
     )
-    other_part, x_near_other, column_given = tied(other_part, x_near_other, column_given)
-    near_partial = added(own_part, swap(other_part, core))
-    partial = added(column_own, column_given, swap(near_partial, near))
-    *own, token = own_gradients(
-        place, [column_lefts, near_lefts], x_rows, [column_cot, near_cot], share
-    )
+    other_part, x_near_other, column_given, cot_first_other, near_mine_away = tied(
+        other_part, x_near_other, column_given, cot_first_other, near_mine_away
+    )
+    near_mine_other = swap(near_mine_away, core)
+    near_sum = added(own_part, swap(other_part, core))
+    partial = added(column_own, column_given, swap(near_sum, near))
+    block = packed.shape[0]
     x_away = [x_column_away, x_near_away, x_column_other, x_near_other]
-    *away_saved, token = away_forward(place, x_away, weights[:2], share, token)
-    partial, token, cot_near_away, *cot_far_away = tied(
-        partial, token, cot_near_away, *cot_far_away
-    )
-    cot_away = [jnp.concatenate([cot_mine_away, *cot_far_away], axis=0), cot_near_away]
-    cot_away += [swap(value, core) for value in cot_away]
-    grads = list(whole_gradients(place, cot_away, w_down, away_saved, x_away, own, token))
-    block = partial.shape[0] // 4
+    *own, slope, swish, hidden, token = own_gradients(
+        place,
+        [column_lefts, near_lefts],
+        x_rows,
+        [column_cot, near_cot],
+        x_away,
+        weights[:2],
+        share,
+    )
+    cot_second_away, near_far_away, near_mine_other, partial, token = tied(
+        cot_second_away, near_far_away, near_mine_other, partial, token
+    )
+    cot_rest_away = jnp.concatenate([cot_second_away, near_far_away], axis=0)
+    cot_away = [cot_first_away, near_mine_away, cot_rest_away]
+    cot_away += [cot_first_other, near_mine_other, swap(cot_rest_away, core)]
+    saved = (slope, swish, hidden)
+    grads = list(whole_gradients(place, cot_away, w_down, saved, x_away, own, token))
     parts = [
         partial[:block],
         swap(partial[block : 2 * block], high),
-        swap(partial[2 * block : 3 * block], low | high),
-        swap(partial[3 * block :], low),
+        swap(partial[2 * block : 3 * block], low),
+        swap(partial[3 * block :], low | high),
     ]
     *parts, grads[0] = tied(*parts, grads[0])
-    result = added(*parts)
-    token_grad = result[:, :model_width]
-    gate_grad = jnp.sum(
-        jnp.where(named, result[:, model_width:].astype(jnp.float32)[:, None, :], 0.0), axis=2
-    ).astype(jnp.bfloat16)
-    return (token_grad, gate_grad, *grads)
+    token_grad = added(*[value[:, :model_width] for value in parts])
+    scores = added(*[value[:, model_width:] for value in parts]).astype(jnp.float32)
+    gate_grad = jnp.sum(jnp.where(named, scores[None], 0.0), axis=2).astype(jnp.bfloat16)
+    return (token_grad, gate_grad.T, *grads)
 
 
 def body(tokens, expert_ids, *rest):

time: 91.2 us -> 89.4 us (0.980)
  local copies, waits for them, and re-layouts: 5.76 us -> 2.08 us
  starting transfers between devices: 28.6 us -> 31.9 us
  Pallas kernels: 31.6 us -> 29 us
  other arithmetic: 1.75 us -> 4.33 us
  waiting for transfers between devices: 22.4 us -> 20.9 us
    pallas_call x1 -> x0, Pallas kernels: 4.8 us -> none  [away_forward(): pl.pallas_call(away_forward_kernel, in_specs=[IN_SMEM] + [IN_HBM] * 7, ou...]
    ppermute x29 -> x30, starting transfers between devices: 28.6 us -> 31.9 us  [swap(): return lax.ppermute(value, BOTH, [(i, i ^ flip) for i in range(count)])]
    unnamed x31 -> x38, local copies, waits for them, and re-layouts: 4.25 us -> 1.92 us
    pallas_call x1, Pallas kernels: 4.41 us -> 6.56 us  [own_gradients(): pl.pallas_call(own_gradient_kernel, grid=(width // tile,), in_specs=[IN_S...]
    ppermute x29 -> x30, waiting for transfers between devices: 22.4 us -> 20.9 us  [swap(): return lax.ppermute(value, BOTH, [(i, i ^ flip) for i in range(count)])]
    reduce_sum x2, other arithmetic: 0.33 us -> 1.59 us  [the longest x1 0.82 us: dense_body(): jnp.sum(jnp.where(named, gate_weights.T.astype(jnp.float32)[:, :, None],...]
  transfers between devices with their start and end apart: 29 -> 30, of which waited for: 9 -> 11; matrix products, arithmetic and copies ran while one was open for 4% -> 4% of each run, Pallas kernels for 35% -> 32%
where the time goes in v4:
time: 89.4 us; the launch traced here: 89.2 us
  starting transfers between devices  31.9 us (36%)
  Pallas kernels  29 us (32%)
  waiting for transfers between devices  20.9 us (23%)
  other arithmetic  4.33 us (5%)
  local copies, waits for them, and re-layouts  2.08 us (2%)
  between operations  1 us (1%)
    ppermute x30, starting transfers between devices, swap(): return lax.ppermute(value, BOTH, [(i, i ^ flip) for i in range(count)])  31.9 us
    ppermute x30, waiting for transfers between devices, swap(): return lax.ppermute(value, BOTH, [(i, i ^ flip) for i in range(count)])  20.9 us
    pallas_call x1, Pallas kernels, whole_gradients(): pl.pallas_call(whole_gradient_kernel, grid=(width // tile,), in_specs=[IN...  8.83 us
    pallas_call x2, Pallas kernels, backward(): pl.pallas_call(functools.partial(backward_kernel, which), in_specs=[IN_SM...  7.23 us
    pallas_call x1, Pallas kernels, own_gradients(): pl.pallas_call(own_gradient_kernel, grid=(width // tile,), in_specs=[IN_S...  6.56 us
    pallas_call x1, Pallas kernels, forward(): pl.pallas_call(forward_kernel, in_specs=[IN_HBM] * 7, out_specs=[IN_VMEM]...  6.33 us
    unnamed x38, local copies, waits for them, and re-layouts  1.92 us
  transfers between devices with their start and end apart: 30, of which 11 were waited for; matrix products, arithmetic and copies ran while one was open for 4% of the time, Pallas kernels for 32%

profile of v4, /device:TPU:0, one launch (start us, length us, event | category | flops | bytes accessed | tf_op | source)
XLA Modules:
  0.0 89.2 jit_solution(2271897511729125938)
XLA Ops:
  0.6 4.1 %collective-permute-start.1 = (bf16[32,2048]{1,0:T(8,128)(2,1)}, bf16[32,2048]{1,0:T(8,128)(2,1)S(1)}, u32[]{:S(2)}, u32[]{:S(2)}) collective-permute-start(bf16[32,2048]{1,0:T(8,128)(2,1)} %param.7), channel_id=1, source_target_pairs={{0,16},{1,17},{2,18},{3,19},{4,20},{5,21},{6,22},{7,23},{8,24},{9,... | collective-permute-start | bytes 393224 | tf_op jit(solution)/shard_map/ppermute | solution.py:115
  4.7 1.6 %collective-permute-start.2 = (bf16[32,2048]{1,0:T(8,128)(2,1)}, bf16[32,2048]{1,0:T(8,128)(2,1)S(1)}, u32[]{:S(2)}, u32[]{:S(2)}) collective-permute-start(bf16[32,2048]{1,0:T(8,128)(2,1)} %param.7), channel_id=1, source_target_pairs={{0,8},{1,9},{2,10},{3,11},{4,12},{5,13},{6,14},{7,15},{8,0},{9,1},... | collective-permute-start | bytes 393224 | tf_op jit(solution)/shard_map/ppermute | solution.py:115
  6.3 0.7 convert_bitcast_fusion
  7.0 0.8 select_reduce_fusion.1
  7.8 0.9 %pad_maximum_fusion = bf16[32,2176]{1,0:T(8,128)(2,1)S(1)} fusion(bf16[32,128]{1,0:T(8,128)(2,1)S(1)} %select_reduce_fusion.1, bf16[32,2048]{1,0:T(8,128)(2,1)} %param.10), kind=kLoop, calls=%fused_computation.3 | loop fusion | flops 278528 | bytes 278528 | tf_op jit(solution)/shard_map/concatenate | solution.py:476
  8.7 1.8 %collective-permute-start = (bf16[32,2176]{1,0:T(8,128)(2,1)S(1)}, bf16[32,2176]{1,0:T(8,128)(2,1)S(1)}, u32[]{:S(2)}, u32[]{:S(2)}) collective-permute-start(bf16[32,2176]{1,0:T(8,128)(2,1)S(1)} %pad_maximum_fusion), channel_id=1, source_target_pairs={{0,1},{1,0},{2,3},{3,2},{4,5},{5,4},{6,7},{7,6},{8,9},{9,8},{10,11... | collective-permute-start | bytes 417800 | tf_op jit(solution)/shard_map/ppermute | solution.py:115
  10.5 0.9 %constant_dynamic-update-slice_fusion.3 = bf16[128,2048]{1,0:T(8,128)(2,1)S(1)} fusion(bf16[32,2048]{1,0:T(8,128)(2,1)} %param.7), kind=kLoop, calls=%fused_computation.10 | loop fusion | bytes 262144
  11.4 1.5 %collective-permute-done.1 = bf16[32,2048]{1,0:T(8,128)(2,1)S(1)} collective-permute-done((bf16[32,2048]{1,0:T(8,128)(2,1)}, bf16[32,2048]{1,0:T(8,128)(2,1)S(1)}, u32[]{:S(2)}, u32[]{:S(2)}) %collective-permute-start.1) | collective-permute-done | bytes 131104 | tf_op jit(solution)/shard_map/ppermute | solution.py:115
  12.9 2.4 %collective-permute-done.3 = bf16[32,2048]{1,0:T(8,128)(2,1)S(1)} collective-permute-done((bf16[32,2048]{1,0:T(8,128)(2,1)}, bf16[32,2048]{1,0:T(8,128)(2,1)S(1)}, u32[]{:S(2)}, u32[]{:S(2)}) %collective-permute-start.3) | collective-permute-done | bytes 131104 | tf_op jit(solution)/shard_map/ppermute | solution.py:115
  15.3 1.6 %collective-permute-start.7 = (bf16[128,2048]{1,0:T(8,128)(2,1)S(1)}, bf16[128,2048]{1,0:T(8,128)(2,1)S(1)}, u32[]{:S(2)}, u32[]{:S(2)}) collective-permute-start(bf16[128,2048]{1,0:T(8,128)(2,1)S(1)} %constant_dynamic-update-slice_fusion.refs_0_), channel_id=1, source_target_pairs={{0,4},{1,5},{2,6},{3,7},{4,0},{5,1},{6,2},{7,3},{8,12},{9,13},{10,... | collective-permute-start | bytes 1572872 | tf_op jit(solution)/shard_map/ppermute | solution.py:115
  16.9 1.5 %collective-permute-start.8 = (bf16[128,2048]{1,0:T(8,128)(2,1)S(1)}, bf16[128,2048]{1,0:T(8,128)(2,1)S(1)}, u32[]{:S(2)}, u32[]{:S(2)}) collective-permute-start(bf16[128,2048]{1,0:T(8,128)(2,1)S(1)} %constant_dynamic-update-slice_fusion.refs_0_), channel_id=1, source_target_pairs={{0,1},{1,0},{2,3},{3,2},{4,5},{5,4},{6,7},{7,6},{8,9},{9,8},{10,11... | collective-permute-start | bytes 1572872 | tf_op jit(solution)/shard_map/ppermute | solution.py:115
  18.5 4.2 %collective-permute-start.4 = (bf16[32,2176]{1,0:T(8,128)(2,1)S(1)}, bf16[32,2176]{1,0:T(8,128)(2,1)S(1)}, u32[]{:S(2)}, u32[]{:S(2)}) collective-permute-start(bf16[32,2176]{1,0:T(8,128)(2,1)S(1)} %pad_maximum_fusion), channel_id=1, source_target_pairs={{0,16},{1,17},{2,18},{3,19},{4,20},{5,21},{6,22},{7,23},{8,24},{9,... | collective-permute-start | bytes 417800 | tf_op jit(solution)/shard_map/ppermute | solution.py:115
  22.7 1.5 %collective-permute-start.6 = (bf16[32,2176]{1,0:T(8,128)(2,1)S(1)}, bf16[32,2176]{1,0:T(8,128)(2,1)S(1)}, u32[]{:S(2)}, u32[]{:S(2)}) collective-permute-start(bf16[32,2176]{1,0:T(8,128)(2,1)S(1)} %pad_maximum_fusion), channel_id=1, source_target_pairs={{0,24},{1,25},{2,26},{3,27},{4,28},{5,29},{6,30},{7,31},{8,16},{9,... | collective-permute-start | bytes 417800 | tf_op jit(solution)/shard_map/ppermute | solution.py:115
  24.3 8.2 %collective-permute-done.4 = bf16[32,2176]{1,0:T(8,128)(2,1)S(1)} collective-permute-done((bf16[32,2176]{1,0:T(8,128)(2,1)S(1)}, bf16[32,2176]{1,0:T(8,128)(2,1)S(1)}, u32[]{:S(2)}, u32[]{:S(2)}) %collective-permute-start.4) | collective-permute-done | bytes 139296 | tf_op jit(solution)/shard_map/ppermute | solution.py:115
  35.1 2.4 %collective-permute-start.15 = (bf16[32,2176]{1,0:T(8,128)(2,1)S(1)}, bf16[32,2176]{1,0:T(8,128)(2,1)S(1)}, u32[]{:S(2)}, u32[]{:S(2)}) collective-permute-start(bf16[32,2176]{1,0:T(8,128)(2,1)S(1)} %collective-permute-done), channel_id=1, source_target_pairs={{0,16},{1,17},{2,18},{3,19},{4,20},{5,21},{6,22},{7,23},{8,24},{9,... | collective-permute-start | bytes 417800 | tf_op jit(solution)/shard_map/ppermute | solution.py:115
  37.5 6.3 %shard_map.110 = (bf16[768,2048]{1,0:T(8,128)(2,1)S(1)}, bf16[768,2048]{1,0:T(8,128)(2,1)S(1)}, bf16[2048,768]{1,0:T(8,128)(2,1)S(1)}, bf16[512,2048]{1,0:T(8,12...) custom-call(bf16[128,2048]{1,0:T(8,128)(2,1)} %copy-done.10, ...), custom_call_target="tpu_custom_call" | custom-call | flops 3221225472 | bytes 2097152 | tf_op jit(solution)/shard_map/pallas_call | solution.py:210
  43.9 3.7 %shard_map.111 = (bf16[128,2176]{1,0:T(8,128)(2,1)S(1)}, bf16[128,2176]{1,0:T(8,128)(2,1)S(1)}, bf16[256,2176]{1,0:T(8,128)(2,1)S(1)}, bf16[256,2304]{1,0:T(8,128)(2,1)S(1)}, f32[8,128]{1,0:T(8,128)S(1)}) custom-call(s32[2]{0:T(128)S(1)} %pad_add_fusion.place_ref._, bf16[128,2176]{1,0:T(8,128)(2,1)S(1)} %constant_dynamic-update-slice_fusion.4.own_ref, ...), custom_call_target="tpu_custom_call" | custom-call | tf_op jit(solution)/shard_map/pallas_call | solution.py:287
  49.5 1.1 %collective-permute-start.22 = (bf16[32,2176]{1,0:T(8,128)(2,1)S(1)}, bf16[32,2176]{1,0:T(8,128)(2,1)S(1)}, u32[]{:S(2)}, u32[]{:S(2)}) collective-permute-start(bf16[32,2176]{1,0:T(8,128)(2,1)S(1)} %collective-permute-done), channel_id=1, source_target_pairs={{0,4},{1,5},{2,6},{3,7},{4,0},{5,1},{6,2},{7,3},{8,12},{9,13},{10,... | collective-permute-start | bytes 417800 | tf_op jit(solution)/shard_map/ppermute | solution.py:115
  50.7 3.6 %shard_map.112 = (bf16[128,2176]{1,0:T(8,128)(2,1)S(1)}, bf16[128,2176]{1,0:T(8,128)(2,1)S(1)}, bf16[256,2176]{1,0:T(8,128)(2,1)S(1)}, bf16[256,2304]{1,0:T(8,128)(2,1)S(1)}, f32[8,128]{1,0:T(8,128)}) custom-call(s32[2]{0:T(128)S(1)} %pad_add_fusion.place_ref._, bf16[128,2176]{1,0:T(8,128)(2,1)S(1)} %collective-permute-done.9.own_ref, ...), custom_call_target="tpu_custom_call" | custom-call | tf_op jit(solution)/shard_map/pallas_call | solution.py:287
  54.2 0.9 %collective-permute-done.22.refs_1_ = bf16[32,2176]{1,0:T(8,128)(2,1)S(1)} collective-permute-done((bf16[32,2176]{1,0:T(8,128)(2,1)S(1)}, bf16[32,2176]{1,0:T(8,128)(2,1)S(1)}, u32[]{:S(2)}, u32[]{:S(2)}) %collective-permute-start.22) | collective-permute-done | bytes 139296 | tf_op jit(solution)/shard_map/ppermute | solution.py:115
  55.3 1.9 %collective-permute-done.24 = bf16[128,2176]{1,0:T(8,128)(2,1)S(1)} collective-permute-done((bf16[128,2176]{1,0:T(8,128)(2,1)S(1)}, bf16[128,2176]{1,0:T(8,128)(2,1)S(1)}, u32[]{:S(2)}, u32[]{:S(2)}) %collective-permute-start.24) | collective-permute-done | bytes 557088 | tf_op jit(solution)/shard_map/ppermute | solution.py:115
  57.4 1.2 %collective-permute-start.25 = (bf16[128,2176]{1,0:T(8,128)(2,1)S(1)}, bf16[128,2176]{1,0:T(8,128)(2,1)S(1)}, u32[]{:S(2)}, u32[]{:S(2)}) collective-permute-start(bf16[128,2176]{1,0:T(8,128)(2,1)S(1)} %add_convert_fusion.1), channel_id=1, source_target_pairs={{0,4},{1,5},{2,6},{3,7},{4,0},{5,1},{6,2},{7,3},{8,12},{9,13},{10,... | collective-permute-start | bytes 1671176 | tf_op jit(solution)/shard_map/ppermute | solution.py:115
  58.6 2.6 %collective-permute-start.16 = (bf16[64,2176]{1,0:T(8,128)(2,1)S(1)}, bf16[64,2176]{1,0:T(8,128)(2,1)S(1)}, u32[]{:S(2)}, u32[]{:S(2)}) collective-permute-start(bf16[64,2176]{1,0:T(8,128)(2,1)S(1)} %constant_dynamic-update-slice_fusion.8.refs_0_), channel_id=1, source_target_pairs={{0,8},{1,9},{2,10},{3,11},{4,12},{5,13},{6,14},{7,15},{8,0},{9,1},... | collective-permute-start | bytes 835592 | tf_op jit(solution)/shard_map/ppermute | solution.py:115
  61.7 6.6 %shard_map.113 = (bf16[384,2048]{1,0:T(8,128)(2,1)S(1)}, bf16[384,2048]{1,0:T(8,128)(2,1)S(1)}, bf16[384,2048]{1,0:T(8,128)(2,1)S(1)}, bf16[384,512]{1,0:T(8,128...) custom-call(s32[2]{0:T(128)S(1)} %pad_add_fusion.place_ref._, ...), custom_call_target="tpu_custom_call" | custom-call | tf_op jit(solution)/shard_map/pallas_call | solution.py:356
  68.3 3.8 %collective-permute-done.25 = bf16[128,2176]{1,0:T(8,128)(2,1)S(1)} collective-permute-done((bf16[128,2176]{1,0:T(8,128)(2,1)S(1)}, bf16[128,2176]{1,0:T(8,128)(2,1)S(1)}, u32[]{:S(2)}, u32[]{:S(2)}) %collective-permute-start.25) | collective-permute-done | bytes 557088 | tf_op jit(solution)/shard_map/ppermute | solution.py:115
  72.6 1.9 %collective-permute-start.26 = (bf16[32,2176]{1,0:T(8,128)(2,1)S(1)}, bf16[32,2176]{1,0:T(8,128)(2,1)S(1)}, u32[]{:S(2)}, u32[]{:S(2)}) collective-permute-start(bf16[32,2176]{1,0:T(8,128)(2,1)S(1)} %get-tuple-element.119), channel_id=1, source_target_pairs={{0,16},{1,17},{2,18},{3,19},{4,20},{5,21},{6,22},{7,23},{8,24},{9,... | collective-permute-start | bytes 417800 | tf_op jit(solution)/shard_map/ppermute | solution.py:115
  74.5 1.3 %collective-permute-start.27 = (bf16[32,2176]{1,0:T(8,128)(2,1)S(1)}, bf16[32,2176]{1,0:T(8,128)(2,1)S(1)}, u32[]{:S(2)}, u32[]{:S(2)}) collective-permute-start(bf16[32,2176]{1,0:T(8,128)(2,1)S(1)} %get-tuple-element.118), channel_id=1, source_target_pairs={{0,8},{1,9},{2,10},{3,11},{4,12},{5,13},{6,14},{7,15},{8,0},{9,1},... | collective-permute-start | bytes 417800 | tf_op jit(solution)/shard_map/ppermute | solution.py:115
  75.8 1.8 %collective-permute-start.28 = (bf16[32,2176]{1,0:T(8,128)(2,1)S(1)}, bf16[32,2176]{1,0:T(8,128)(2,1)S(1)}, u32[]{:S(2)}, u32[]{:S(2)}) collective-permute-start(bf16[32,2176]{1,0:T(8,128)(2,1)S(1)} %get-tuple-element.117), channel_id=1, source_target_pairs={{0,24},{1,25},{2,26},{3,27},{4,28},{5,29},{6,30},{7,31},{8,16},{9,... | collective-permute-start | bytes 417800 | tf_op jit(solution)/shard_map/ppermute | solution.py:115
  77.5 0.9 copy-done.5
  78.4 8.8 %shard_map.114 = (bf16[1,384,2048]{2,1,0:T(8,128)(2,1)}, bf16[1,384,2048]{2,1,0:T(8,128)(2,1)}, bf16[1,384,2048]{2,1,0:T(8,128)(2,1)}) custom-call(s32[2]{0:T(128)S(1)} %pad_add_fusion.place_ref._, bf16[64,2176]{1,0:T(8,128)(2,1)} %copy-done.6, bf16[32,2176]{1,0:T(8,128)(2,1)} %copy-done.8, bf16[160,2176]{1,0:T(8,128)(2,1)} %copy-done.4, ...), custom_call_target="tpu_custom_call" | custom-call | flops 3221225472 | bytes 13631488 | tf_op jit(solution)/shard_map/pallas_call | solution.py:427
  87.7 0.7 add_convert_fusion.2
  88.4 0.8 select_reduce_fusion
  (86 shorter events, 6.4 us)
Async XLA Ops:
  0.6 12.3 %collective-permute-start.1 = (bf16[32,2048]{1,0:T(8,128)(2,1)}, bf16[32,2048]{1,0:T(8,128)(2,1)S(1)}, u32[]{:S(2)}, u32[]{:S(2)}) collective-permute-start(bf16[32,2048]{1,0:T(8,128)(2,1)} %param.7), channel_id=1, source_target_pairs={{0,16},{1,17},{2,18},{3,19},{4,20},{5,21},{6,22},{7,23},{8,24},{9,... | collective-permute-start | bytes 393224 | tf_op jit(solution)/shard_map/ppermute | solution.py:115
  4.7 8.2 %collective-permute-start.2 = (bf16[32,2048]{1,0:T(8,128)(2,1)}, bf16[32,2048]{1,0:T(8,128)(2,1)S(1)}, u32[]{:S(2)}, u32[]{:S(2)}) collective-permute-start(bf16[32,2048]{1,0:T(8,128)(2,1)} %param.7), channel_id=1, source_target_pairs={{0,8},{1,9},{2,10},{3,11},{4,12},{5,13},{6,14},{7,15},{8,0},{9,1},... | collective-permute-start | bytes 393224 | tf_op jit(solution)/shard_map/ppermute | solution.py:115
  6.3 9.0 %collective-permute-start.3 = (bf16[32,2048]{1,0:T(8,128)(2,1)}, bf16[32,2048]{1,0:T(8,128)(2,1)S(1)}, u32[]{:S(2)}, u32[]{:S(2)}) collective-permute-start(bf16[32,2048]{1,0:T(8,128)(2,1)} %param.7), channel_id=1, source_target_pairs={{0,24},{1,25},{2,26},{3,27},{4,28},{5,29},{6,30},{7,31},{8,16},{9,... | collective-permute-start | bytes 393224 | tf_op jit(solution)/shard_map/ppermute | solution.py:115
  8.7 6.5 %collective-permute-start = (bf16[32,2176]{1,0:T(8,128)(2,1)S(1)}, bf16[32,2176]{1,0:T(8,128)(2,1)S(1)}, u32[]{:S(2)}, u32[]{:S(2)}) collective-permute-start(bf16[32,2176]{1,0:T(8,128)(2,1)S(1)} %pad_maximum_fusion), channel_id=1, source_target_pairs={{0,1},{1,0},{2,3},{3,2},{4,5},{5,4},{6,7},{7,6},{8,9},{9,8},{10,11... | collective-permute-start | bytes 417800 | tf_op jit(solution)/shard_map/ppermute | solution.py:115
  15.3 22.2 %copy-start.10 = (bf16[128,2048]{1,0:T(8,128)(2,1)}, bf16[128,2048]{1,0:T(8,128)(2,1)S(1)}, u32[]{:S(2)}) copy-start(bf16[128,2048]{1,0:T(8,128)(2,1)S(1)} %constant_dynamic-update-slice_fusion.refs_0_) | copy-start | bytes 1572868
  15.3 17.7 %collective-permute-start.7 = (bf16[128,2048]{1,0:T(8,128)(2,1)S(1)}, bf16[128,2048]{1,0:T(8,128)(2,1)S(1)}, u32[]{:S(2)}, u32[]{:S(2)}) collective-permute-start(bf16[128,2048]{1,0:T(8,128)(2,1)S(1)} %constant_dynamic-update-slice_fusion.refs_0_), channel_id=1, source_target_pairs={{0,4},{1,5},{2,6},{3,7},{4,0},{5,1},{6,2},{7,3},{8,12},{9,13},{10,... | collective-permute-start | bytes 1572872 | tf_op jit(solution)/shard_map/ppermute | solution.py:115
  16.9 16.2 %collective-permute-start.8 = (bf16[128,2048]{1,0:T(8,128)(2,1)S(1)}, bf16[128,2048]{1,0:T(8,128)(2,1)S(1)}, u32[]{:S(2)}, u32[]{:S(2)}) collective-permute-start(bf16[128,2048]{1,0:T(8,128)(2,1)S(1)} %constant_dynamic-update-slice_fusion.refs_0_), channel_id=1, source_target_pairs={{0,1},{1,0},{2,3},{3,2},{4,5},{5,4},{6,7},{7,6},{8,9},{9,8},{10,11... | collective-permute-start | bytes 1572872 | tf_op jit(solution)/shard_map/ppermute | solution.py:115
  18.5 13.9 %collective-permute-start.4 = (bf16[32,2176]{1,0:T(8,128)(2,1)S(1)}, bf16[32,2176]{1,0:T(8,128)(2,1)S(1)}, u32[]{:S(2)}, u32[]{:S(2)}) collective-permute-start(bf16[32,2176]{1,0:T(8,128)(2,1)S(1)} %pad_maximum_fusion), channel_id=1, source_target_pairs={{0,16},{1,17},{2,18},{3,19},{4,20},{5,21},{6,22},{7,23},{8,24},{9,... | collective-permute-start | bytes 417800 | tf_op jit(solution)/shard_map/ppermute | solution.py:115
  22.7 10.4 %collective-permute-start.5 = (bf16[32,2176]{1,0:T(8,128)(2,1)S(1)}, bf16[32,2176]{1,0:T(8,128)(2,1)S(1)}, u32[]{:S(2)}, u32[]{:S(2)}) collective-permute-start(bf16[32,2176]{1,0:T(8,128)(2,1)S(1)} %pad_maximum_fusion), channel_id=1, source_target_pairs={{0,8},{1,9},{2,10},{3,11},{4,12},{5,13},{6,14},{7,15},{8,0},{9,1},... | collective-permute-start | bytes 417800 | tf_op jit(solution)/shard_map/ppermute | solution.py:115
  22.7 10.4 %collective-permute-start.6 = (bf16[32,2176]{1,0:T(8,128)(2,1)S(1)}, bf16[32,2176]{1,0:T(8,128)(2,1)S(1)}, u32[]{:S(2)}, u32[]{:S(2)}) collective-permute-start(bf16[32,2176]{1,0:T(8,128)(2,1)S(1)} %pad_maximum_fusion), channel_id=1, source_target_pairs={{0,24},{1,25},{2,26},{3,27},{4,28},{5,29},{6,30},{7,31},{8,16},{9,... | collective-permute-start | bytes 417800 | tf_op jit(solution)/shard_map/ppermute | solution.py:115
  32.4 2.4 %collective-permute-start.11 = (bf16[128,2048]{1,0:T(8,128)(2,1)S(1)}, bf16[128,2048]{1,0:T(8,128)(2,1)S(1)}, u32[]{:S(2)}, u32[]{:S(2)}) collective-permute-start(bf16[128,2048]{1,0:T(8,128)(2,1)S(1)} %constant_dynamic-update-slice_fusion.refs_0_), channel_id=1, source_target_pairs={{0,2},{1,3},{2,0},{3,1},{4,6},{5,7},{6,4},{7,5},{8,10},{9,11},{10,... | collective-permute-start | bytes 1572872 | tf_op jit(solution)/shard_map/ppermute | solution.py:115
  33.1 2.0 %collective-permute-start.12 = (bf16[128,2048]{1,0:T(8,128)(2,1)S(1)}, bf16[128,2048]{1,0:T(8,128)(2,1)S(1)}, u32[]{:S(2)}, u32[]{:S(2)}) collective-permute-start(bf16[128,2048]{1,0:T(8,128)(2,1)S(1)} %collective-permute-done.7.refs_2_), channel_id=1, source_target_pairs={{0,2},{1,3},{2,0},{3,1},{4,6},{5,7},{6,4},{7,5},{8,10},{9,11},{10,... | collective-permute-start | bytes 1572872 | tf_op jit(solution)/shard_map/ppermute | solution.py:115
  33.3 10.6 %collective-permute-start.10 = (bf16[128,2176]{1,0:T(8,128)(2,1)S(1)}, bf16[128,2176]{1,0:T(8,128)(2,1)S(1)}, u32[]{:S(2)}, u32[]{:S(2)}) collective-permute-start(bf16[128,2176]{1,0:T(8,128)(2,1)S(1)} %constant_dynamic-update-slice_fusion.4.own_ref), channel_id=1, source_target_pairs={{0,2},{1,3},{2,0},{3,1},{4,6},{5,7},{6,4},{7,5},{8,10},{9,11},{10,... | collective-permute-start | bytes 1671176 | tf_op jit(solution)/shard_map/ppermute | solution.py:115
  33.8 14.6 %collective-permute-start.9 = (bf16[128,2176]{1,0:T(8,128)(2,1)S(1)}, bf16[128,2176]{1,0:T(8,128)(2,1)S(1)}, u32[]{:S(2)}, u32[]{:S(2)}) collective-permute-start(bf16[128,2176]{1,0:T(8,128)(2,1)S(1)} %constant_dynamic-update-slice_fusion.4.own_ref), channel_id=1, source_target_pairs={{0,4},{1,5},{2,6},{3,7},{4,0},{5,1},{6,2},{7,3},{8,12},{9,13},{10,... | collective-permute-start | bytes 1671176 | tf_op jit(solution)/shard_map/ppermute | solution.py:115
  34.3 13.6 %collective-permute-start.13 = (bf16[128,2048]{1,0:T(8,128)(2,1)S(1)}, bf16[128,2048]{1,0:T(8,128)(2,1)S(1)}, u32[]{:S(2)}, u32[]{:S(2)}) collective-permute-start(bf16[128,2048]{1,0:T(8,128)(2,1)S(1)} %collective-permute-done.7.refs_2_), channel_id=1, source_target_pairs={{0,1},{1,0},{2,3},{3,2},{4,5},{5,4},{6,7},{7,6},{8,9},{9,8},{10,11... | collective-permute-start | bytes 1572872 | tf_op jit(solution)/shard_map/ppermute | solution.py:115
  34.9 13.1 %collective-permute-start.14 = (bf16[128,2048]{1,0:T(8,128)(2,1)S(1)}, bf16[128,2048]{1,0:T(8,128)(2,1)S(1)}, u32[]{:S(2)}, u32[]{:S(2)}) collective-permute-start(bf16[128,2048]{1,0:T(8,128)(2,1)S(1)} %collective-permute-done.8.refs_5_.refs_10_), channel_id=1, source_target_pairs={{0,2},{1,3},{2,0},{3,1},{4,6},{5,7},{6,4},{7,5},{8,10},{9,11},{10,... | collective-permute-start | bytes 1572872 | tf_op jit(solution)/shard_map/ppermute | solution.py:115
  35.1 12.4 %collective-permute-start.15 = (bf16[32,2176]{1,0:T(8,128)(2,1)S(1)}, bf16[32,2176]{1,0:T(8,128)(2,1)S(1)}, u32[]{:S(2)}, u32[]{:S(2)}) collective-permute-start(bf16[32,2176]{1,0:T(8,128)(2,1)S(1)} %collective-permute-done), channel_id=1, source_target_pairs={{0,16},{1,17},{2,18},{3,19},{4,20},{5,21},{6,22},{7,23},{8,24},{9,... | collective-permute-start | bytes 417800 | tf_op jit(solution)/shard_map/ppermute | solution.py:115
  48.4 2.2 %collective-permute-start.18 = (bf16[128,2176]{1,0:T(8,128)(2,1)S(1)}, bf16[128,2176]{1,0:T(8,128)(2,1)S(1)}, u32[]{:S(2)}, u32[]{:S(2)}) collective-permute-start(bf16[128,2176]{1,0:T(8,128)(2,1)S(1)} %collective-permute-done.9.own_ref), channel_id=1, source_target_pairs={{0,2},{1,3},{2,0},{3,1},{4,6},{5,7},{6,4},{7,5},{8,10},{9,11},{10,... | collective-permute-start | bytes 1671176 | tf_op jit(solution)/shard_map/ppermute | solution.py:115
  48.4 6.8 %collective-permute-start.19 = (bf16[128,2048]{1,0:T(8,128)(2,1)S(1)}, bf16[128,2048]{1,0:T(8,128)(2,1)S(1)}, u32[]{:S(2)}, u32[]{:S(2)}) collective-permute-start(bf16[128,2048]{1,0:T(8,128)(2,1)S(1)} %collective-permute-done.13.refs_6_.refs_11_), channel_id=1, source_target_pairs={{0,2},{1,3},{2,0},{3,1},{4,6},{5,7},{6,4},{7,5},{8,10},{9,11},{10,... | collective-permute-start | bytes 1572872 | tf_op jit(solution)/shard_map/ppermute | solution.py:115
  48.9 6.3 %collective-permute-start.20 = (bf16[128,2176]{1,0:T(8,128)(2,1)S(1)}, bf16[128,2176]{1,0:T(8,128)(2,1)S(1)}, u32[]{:S(2)}, u32[]{:S(2)}) collective-permute-start(bf16[128,2176]{1,0:T(8,128)(2,1)S(1)} %get-tuple-element.83), channel_id=1, source_target_pairs={{0,2},{1,3},{2,0},{3,1},{4,6},{5,7},{6,4},{7,5},{8,10},{9,11},{10,... | collective-permute-start | bytes 1671176 | tf_op jit(solution)/shard_map/ppermute | solution.py:115
  49.0 6.2 %collective-permute-start.21 = (bf16[64,2176]{1,0:T(8,128)(2,1)S(1)}, bf16[64,2176]{1,0:T(8,128)(2,1)S(1)}, u32[]{:S(2)}, u32[]{:S(2)}) collective-permute-start(bf16[64,2176]{1,0:T(8,128)(2,1)S(1)} %constant_dynamic-update-slice_fusion.8.refs_0_), channel_id=1, source_target_pairs={{0,2},{1,3},{2,0},{3,1},{4,6},{5,7},{6,4},{7,5},{8,10},{9,11},{10,... | collective-permute-start | bytes 835592 | tf_op jit(solution)/shard_map/ppermute | solution.py:115
  49.5 5.7 %collective-permute-start.22 = (bf16[32,2176]{1,0:T(8,128)(2,1)S(1)}, bf16[32,2176]{1,0:T(8,128)(2,1)S(1)}, u32[]{:S(2)}, u32[]{:S(2)}) collective-permute-start(bf16[32,2176]{1,0:T(8,128)(2,1)S(1)} %collective-permute-done), channel_id=1, source_target_pairs={{0,4},{1,5},{2,6},{3,7},{4,0},{5,1},{6,2},{7,3},{8,12},{9,13},{10,... | collective-permute-start | bytes 417800 | tf_op jit(solution)/shard_map/ppermute | solution.py:115
  55.2 13.1 %copy-start.7 = (bf16[64,2176]{1,0:T(8,128)(2,1)}, bf16[64,2176]{1,0:T(8,128)(2,1)S(1)}, u32[]{:S(2)}) copy-start(bf16[64,2176]{1,0:T(8,128)(2,1)S(1)} %collective-permute-done.21.refs_3_) | copy-start | bytes 835588
  55.2 2.0 %collective-permute-start.24 = (bf16[128,2176]{1,0:T(8,128)(2,1)S(1)}, bf16[128,2176]{1,0:T(8,128)(2,1)S(1)}, u32[]{:S(2)}, u32[]{:S(2)}) collective-permute-start(bf16[128,2176]{1,0:T(8,128)(2,1)S(1)} %get-tuple-element.88), channel_id=1, source_target_pairs={{0,2},{1,3},{2,0},{3,1},{4,6},{5,7},{6,4},{7,5},{8,10},{9,11},{10,... | collective-permute-start | bytes 1671176 | tf_op jit(solution)/shard_map/ppermute | solution.py:115
  57.4 14.7 %collective-permute-start.25 = (bf16[128,2176]{1,0:T(8,128)(2,1)S(1)}, bf16[128,2176]{1,0:T(8,128)(2,1)S(1)}, u32[]{:S(2)}, u32[]{:S(2)}) collective-permute-start(bf16[128,2176]{1,0:T(8,128)(2,1)S(1)} %add_convert_fusion.1), channel_id=1, source_target_pairs={{0,4},{1,5},{2,6},{3,7},{4,0},{5,1},{6,2},{7,3},{8,12},{9,13},{10,... | collective-permute-start | bytes 1671176 | tf_op jit(solution)/shard_map/ppermute | solution.py:115
  58.6 13.7 %collective-permute-start.16 = (bf16[64,2176]{1,0:T(8,128)(2,1)S(1)}, bf16[64,2176]{1,0:T(8,128)(2,1)S(1)}, u32[]{:S(2)}, u32[]{:S(2)}) collective-permute-start(bf16[64,2176]{1,0:T(8,128)(2,1)S(1)} %constant_dynamic-update-slice_fusion.8.refs_0_), channel_id=1, source_target_pairs={{0,8},{1,9},{2,10},{3,11},{4,12},{5,13},{6,14},{7,15},{8,0},{9,1},... | collective-permute-start | bytes 835592 | tf_op jit(solution)/shard_map/ppermute | solution.py:115
  61.2 11.2 %collective-permute-start.17 = (bf16[96,2176]{1,0:T(8,128)(2,1)S(1)}, bf16[96,2176]{1,0:T(8,128)(2,1)S(1)}, u32[]{:S(2)}, u32[]{:S(2)}) collective-permute-start(bf16[96,2176]{1,0:T(8,128)(2,1)S(1)} %slice.39), channel_id=1, source_target_pairs={{0,1},{1,0},{2,3},{3,2},{4,5},{5,4},{6,7},{7,6},{8,9},{9,8},{10,11... | collective-permute-start | bytes 1253384 | tf_op jit(solution)/shard_map/ppermute | solution.py:115
  61.7 10.6 %collective-permute-start.23 = (bf16[32,2176]{1,0:T(8,128)(2,1)S(1)}, bf16[32,2176]{1,0:T(8,128)(2,1)S(1)}, u32[]{:S(2)}, u32[]{:S(2)}) collective-permute-start(bf16[32,2176]{1,0:T(8,128)(2,1)S(1)} %collective-permute-done.22.refs_1_), channel_id=1, source_target_pairs={{0,2},{1,3},{2,0},{3,1},{4,6},{5,7},{6,4},{7,5},{8,10},{9,11},{10,... | collective-permute-start | bytes 417800 | tf_op jit(solution)/shard_map/ppermute | solution.py:115
  72.5 5.1 %collective-permute-start.29 = (bf16[160,2176]{1,0:T(8,128)(2,1)S(1)}, bf16[160,2176]{1,0:T(8,128)(2,1)S(1)}, u32[]{:S(2)}, u32[]{:S(2)}) collective-permute-start(bf16[160,2176]{1,0:T(8,128)(2,1)S(1)} %constant_dynamic-update-slice_fusion.10.refs_2_), channel_id=1, source_target_pairs={{0,2},{1,3},{2,0},{3,1},{4,6},{5,7},{6,4},{7,5},{8,10},{9,11},{10,... | collective-permute-start | bytes 2088968 | tf_op jit(solution)/shard_map/ppermute | solution.py:115
  72.6 14.6 %collective-permute-start.26 = (bf16[32,2176]{1,0:T(8,128)(2,1)S(1)}, bf16[32,2176]{1,0:T(8,128)(2,1)S(1)}, u32[]{:S(2)}, u32[]{:S(2)}) collective-permute-start(bf16[32,2176]{1,0:T(8,128)(2,1)S(1)} %get-tuple-element.119), channel_id=1, source_target_pairs={{0,16},{1,17},{2,18},{3,19},{4,20},{5,21},{6,22},{7,23},{8,24},{9,... | collective-permute-start | bytes 417800 | tf_op jit(solution)/shard_map/ppermute | solution.py:115
  74.5 12.7 %collective-permute-start.27 = (bf16[32,2176]{1,0:T(8,128)(2,1)S(1)}, bf16[32,2176]{1,0:T(8,128)(2,1)S(1)}, u32[]{:S(2)}, u32[]{:S(2)}) collective-permute-start(bf16[32,2176]{1,0:T(8,128)(2,1)S(1)} %get-tuple-element.118), channel_id=1, source_target_pairs={{0,8},{1,9},{2,10},{3,11},{4,12},{5,13},{6,14},{7,15},{8,0},{9,1},... | collective-permute-start | bytes 417800 | tf_op jit(solution)/shard_map/ppermute | solution.py:115
  75.8 11.9 %collective-permute-start.28 = (bf16[32,2176]{1,0:T(8,128)(2,1)S(1)}, bf16[32,2176]{1,0:T(8,128)(2,1)S(1)}, u32[]{:S(2)}, u32[]{:S(2)}) collective-permute-start(bf16[32,2176]{1,0:T(8,128)(2,1)S(1)} %get-tuple-element.117), channel_id=1, source_target_pairs={{0,24},{1,25},{2,26},{3,27},{4,28},{5,29},{6,30},{7,31},{8,16},{9,... | collective-permute-start | bytes 417800 | tf_op jit(solution)/shard_map/ppermute | solution.py:115
  (13 other events, 83.1 us)

commit v5 on v4

--- a/solution.py
+++ b/solution.py
@@ -217,37 +217,21 @@
     )(*[left_out(value) for value in (*pieces, *weights)])
 
 
-def backward_kernel(
-    which,
-    place_ref,
-    own_ref,
-    other_ref,
-    slope_ref,
-    swish_ref,
-    hidden_ref,
-    gate_ref,
-    up_ref,
-    down_ref,
-    _,
-    own_out,
-    other_out,
-    rows_out,
-    lefts_out,
-    token_out,
-    sems,
-):
+def backward_kernel(first, count, place_ref, *refs):
+    pieces, (slope_ref, swish_ref, hidden_ref) = refs[:count], refs[count : count + 3]
+    gate_ref, up_ref, down_ref, _ = refs[count + 3 : count + 7]
+    parts_out, (rows_out, lefts_out, token_out, sems) = refs[count + 7 : -4], refs[-4:]
     width, units = down_ref.shape
-    half = own_ref.shape[0]
-    lanes = own_ref.shape[1] - width
-    copies = fetched(placed((own_ref, other_ref), rows_out), sems)
+    rows, packed = rows_out.shape
+    copies = fetched(placed(pieces, rows_out), sems)
     token_out[...] = jnp.zeros_like(token_out)
     for copy in copies:
         copy.wait()
-    saved = pl.ds(which * 2 * half, 2 * half)
-    column = lax.broadcasted_iota(jnp.int32, (2 * half, lanes), 1) == place_ref[0]
+    saved = slice(first, first + rows)
+    column = lax.broadcasted_iota(jnp.int32, (rows, packed - width), 1) == place_ref[0]
     table = rows_out[:, width:].astype(jnp.float32)
     gates = jnp.sum(jnp.where(column, table, 0.0), axis=1, keepdims=True)
-    score = jnp.zeros((2 * half, 1), jnp.float32)
+    score = jnp.zeros((rows, 1), jnp.float32)
     for start in range(0, units, TILE):
         chunk = slice(start, start + TILE)
         raw = jnp.dot(
@@ -264,8 +248,9 @@
             jnp.bfloat16
         )
     scores = jnp.where(column, score, 0.0).astype(jnp.bfloat16)
-    own_out[:, width:] = scores[:half]
-    other_out[:, width:] = scores[half:]
+    block = rows // count
+    for i, part in enumerate(parts_out):
+        part[:, width:] = scores[i * block : (i + 1) * block]
     for start in range(0, width, 2 * TILE):
         chunk = slice(start, start + 2 * TILE)
         total = (
@@ -276,37 +261,37 @@
                 preferred_element_type=jnp.float32,
             )
         ).astype(jnp.bfloat16)
-        own_out[:, chunk] = total[:half]
-        other_out[:, chunk] = total[half:]
-
-
-def backward(place, own, other, saved, which, weights, after):
+        for i, part in enumerate(parts_out):
+            part[:, chunk] = total[i * block : (i + 1) * block]
+
+
+def backward(place, pieces, saved, first, weights, after):
     units, width = weights[0].shape
-    half, packed = own.shape
-    rows = 2 * half
+    count = len(pieces)
+    block, packed = pieces[0].shape
+    rows = count * block
     return pl.pallas_call(
-        functools.partial(backward_kernel, which),
-        in_specs=[IN_SMEM] + [IN_HBM] * 2 + [IN_VMEM] * 6 + [IN_HBM],
-        out_specs=[IN_VMEM] * 5,
-        out_shape=[
-            jax.ShapeDtypeStruct((half, packed), jnp.bfloat16),
-            jax.ShapeDtypeStruct((half, packed), jnp.bfloat16),
+        functools.partial(backward_kernel, first, count),
+        in_specs=[IN_SMEM] + [IN_HBM] * count + [IN_VMEM] * 6 + [IN_HBM],
+        out_specs=[IN_VMEM] * (count + 3),
+        out_shape=[jax.ShapeDtypeStruct((block, packed), jnp.bfloat16)] * count
+        + [
             pltpu.VMEM((rows, packed), jnp.bfloat16),
             pltpu.VMEM((rows, 3 * units), jnp.bfloat16),
             jax.ShapeDtypeStruct((8, 128), jnp.float32),
         ],
-        scratch_shapes=[pltpu.SemaphoreType.DMA((2,))],
+        scratch_shapes=[pltpu.SemaphoreType.DMA((count,))],
         **kernel_params(0, 0),
-    )(place, own, other, *[kept(value) for value in (*saved, *weights)], after)
+    )(place, *pieces, *[kept(value) for value in (*saved, *weights)], after)
 
 
 def own_gradient_kernel(place_ref, *refs):
-    column_ref, near_ref, x_ref, column_cot, near_cot = refs[:5]
-    x_refs, weight_refs = refs[5:9], refs[9:11]
-    outs, (slope_out, swish_out, hidden_out, token_out) = refs[11:14], refs[14:18]
-    lefts, rows, gate_ref, up_ref, sems = refs[18:]
+    left_refs, x_ref, own_cot_refs = refs[:3], refs[3], refs[4:7]
+    x_refs, weight_refs = refs[7:11], refs[11:13]
+    outs, (slope_out, swish_out, hidden_out, token_out) = refs[13:16], refs[16:20]
+    lefts, rows, gate_ref, up_ref, sems = refs[20:]
     share, tile = outs[0].shape
-    units = column_ref.shape[1] // 3
+    units = left_refs[0].shape[1] // 3
     start = pl.multiple_of(place_ref[1] * share, 128)
     own = pl.ds(start, share)
     copies = [
@@ -324,11 +309,11 @@
         token_out[...] = jnp.zeros_like(token_out)
         for i in range(3):
             lefts[i] = jnp.concatenate(
-                [ref[:, pl.ds(start + i * units, share)] for ref in (column_ref, near_ref)], axis=0
+                [ref[:, pl.ds(start + i * units, share)] for ref in left_refs], axis=0
             ).T
 
     chunk = pl.ds(pl.multiple_of(pl.program_id(0) * tile, tile), tile)
-    cot_rows = jnp.concatenate([column_cot[:, chunk], near_cot[:, chunk]], axis=0)
+    cot_rows = jnp.concatenate([ref[:, chunk] for ref in own_cot_refs], axis=0)
     for i, right in enumerate((x_ref[:, chunk], x_ref[:, chunk], cot_rows)):
         outs[i][...] = jnp.dot(lefts[i], right, preferred_element_type=jnp.float32).astype(
             jnp.bfloat16
@@ -356,7 +341,7 @@
     return pl.pallas_call(
         own_gradient_kernel,
         grid=(width // tile,),
-        in_specs=[IN_SMEM] + [IN_VMEM] * 5 + [IN_HBM] * 6,
+        in_specs=[IN_SMEM] + [IN_VMEM] * 7 + [IN_HBM] * 6,
         out_specs=[pl.BlockSpec((share, tile), lambda i: (0, i))] * 3
         + [pl.BlockSpec((share, rows), lambda i: (0, 0))] * 3
         + [pl.BlockSpec((8, 128), lambda i: (0, 0))],
@@ -474,9 +459,13 @@
 
     weights = (w_gate, w_up, w_down)
     packed = jnp.concatenate([cotangent, gate_table], axis=1)
-    cot_mine_away = swap(packed, group)
-    packed, cot_mine_away, *x_far = tied(packed, cot_mine_away, *column_of(tokens))
-    x_column = jnp.concatenate([tokens, *x_far], axis=0)
+    x_high, x_low, x_both = column_of(tokens)
+    packed, x_low = tied(packed, x_low)
+    cot_mine_away, near_mine_away = swap(packed, group), swap(packed, group | near)
+    packed, cot_mine_away, near_mine_away, x_high, x_low, x_both = tied(
+        packed, cot_mine_away, near_mine_away, x_high, x_low, x_both
+    )
+    x_column = jnp.concatenate([tokens, x_high, x_low, x_both], axis=0)
     x_near = swap(x_column, near)
     x_column_away = swap(x_column, group)
     *cot_far, x_near, x_column_away = tied(*column_of(packed), x_near, x_column_away)
@@ -489,7 +478,7 @@
     )
     saved = (slope, swish, hidden)
     own_part, other_part, column_cot, column_lefts, token = backward(
-        place, cot_column, swap(cot_column, core), saved, 0, kept_weights, place
+        place, [cot_column, swap(cot_column, core)], saved, 0, kept_weights, place
     )
     column_own, column_given = own_part, swap(other_part, core)
     x_column_other = swap(x_column_away, core)
@@ -499,30 +488,33 @@
     cot_first_away = jnp.concatenate([cot_mine_away, cot_high_away], axis=0)
     cot_second_away, cot_first_other = swap(cot_first_away, low), swap(cot_first_away, core)
     x_near_other = swap(x_near_away, core)
-    near_mine_away = swap(cot_mine_away, near)
+    near_mine_other = swap(near_mine_away, core)
     near_far_away = swap(cot_near[packed.shape[0] :], group)
-    own_part, other_part, near_cot, near_lefts, _ = backward(
-        place, cot_near, swap(cot_near, core), saved, 1, kept_weights, token
-    )
-    other_part, x_near_other, column_given, cot_first_other, near_mine_away = tied(
-        other_part, x_near_other, column_given, cot_first_other, near_mine_away
-    )
-    near_mine_other = swap(near_mine_away, core)
+    half = x_rows.shape[0] // 2
+    other_part, other_cot, other_lefts, _ = backward(
+        place, [swap(cot_near, core)], saved, half + half // 2, kept_weights, token
+    )
+    own_part, own_cot, own_lefts, _ = backward(
+        place, [cot_near], saved, half, kept_weights, token
+    )
+    other_part, x_near_other, column_given, cot_first_other, near_mine_other = tied(
+        other_part, x_near_other, column_given, cot_first_other, near_mine_other
+    )
     near_sum = added(own_part, swap(other_part, core))
     partial = added(column_own, column_given, swap(near_sum, near))
     block = packed.shape[0]
     x_away = [x_column_away, x_near_away, x_column_other, x_near_other]
     *own, slope, swish, hidden, token = own_gradients(
         place,
-        [column_lefts, near_lefts],
+        [column_lefts, own_lefts, other_lefts],
         x_rows,
-        [column_cot, near_cot],
+        [column_cot, own_cot, other_cot],
         x_away,
         weights[:2],
         share,
     )
-    cot_second_away, near_far_away, near_mine_other, partial, token = tied(
-        cot_second_away, near_far_away, near_mine_other, partial, token
+    cot_second_away, near_far_away, partial, token = tied(
+        cot_second_away, near_far_away, partial, token
     )
     cot_rest_away = jnp.concatenate([cot_second_away, near_far_away], axis=0)
     cot_away = [cot_first_away, near_mine_away, cot_rest_away]

time: 89.4 us -> 86.9 us (0.972)
  waiting for transfers between devices: 20.9 us -> 18.4 us
  starting transfers between devices: 31.9 us -> 30.9 us
  Pallas kernels: 29 us -> 29.9 us
    ppermute x30, waiting for transfers between devices: 20.9 us -> 18.4 us  [swap(): return lax.ppermute(value, BOTH, [(i, i ^ flip) for i in range(count)])]
    ppermute x30, starting transfers between devices: 31.9 us -> 30.9 us  [swap(): return lax.ppermute(value, BOTH, [(i, i ^ flip) for i in range(count)])]
    pallas_call x2 -> x3, Pallas kernels: 7.23 us -> 8.15 us  [backward(): pl.pallas_call(functools.partial(backward_kernel, first, count), in_specs...]
  transfers between devices with their start and end apart: 30 -> 30, of which waited for: 11 -> 7; matrix products, arithmetic and copies ran while one was open for 4% -> 4% of each run, Pallas kernels for 32% -> 34%
where the time goes in v5:
time: 86.9 us; the launch traced here: 86.7 us
  starting transfers between devices  30.9 us (36%)
  Pallas kernels  29.9 us (34%)
  waiting for transfers between devices  18.4 us (21%)
  other arithmetic  4.33 us (5%)
  local copies, waits for them, and re-layouts  2.09 us (2%)
  between operations  1.09 us (1%)
    ppermute x30, starting transfers between devices, swap(): return lax.ppermute(value, BOTH, [(i, i ^ flip) for i in range(count)])  30.9 us
    ppermute x30, waiting for transfers between devices, swap(): return lax.ppermute(value, BOTH, [(i, i ^ flip) for i in range(count)])  18.4 us
    pallas_call x1, Pallas kernels, whole_gradients(): pl.pallas_call(whole_gradient_kernel, grid=(width // tile,), in_specs=[IN...  8.83 us
    pallas_call x3, Pallas kernels, backward(): pl.pallas_call(functools.partial(backward_kernel, first, count), in_specs...  8.15 us
    pallas_call x1, Pallas kernels, own_gradients(): pl.pallas_call(own_gradient_kernel, grid=(width // tile,), in_specs=[IN_S...  6.55 us
    pallas_call x1, Pallas kernels, forward(): pl.pallas_call(forward_kernel, in_specs=[IN_HBM] * 7, out_specs=[IN_VMEM]...  6.34 us
    unnamed x38, local copies, waits for them, and re-layouts  1.93 us
  transfers between devices with their start and end apart: 30, of which 7 were waited for; matrix products, arithmetic and copies ran while one was open for 4% of the time, Pallas kernels for 34%

profile of v5, /device:TPU:0, one launch (start us, length us, event | category | flops | bytes accessed | tf_op | source)
XLA Modules:
  0.0 86.7 jit_solution(8922640044267355162)
XLA Ops:
  0.6 3.1 %collective-permute-start = (bf16[32,2048]{1,0:T(8,128)(2,1)}, bf16[32,2048]{1,0:T(8,128)(2,1)S(1)}, u32[]{:S(2)}, u32[]{:S(2)}) collective-permute-start(bf16[32,2048]{1,0:T(8,128)(2,1)} %param.7), channel_id=1, source_target_pairs={{0,8},{1,9},{2,10},{3,11},{4,12},{5,13},{6,14},{7,15},{8,0},{9,1},... | collective-permute-start | bytes 393224 | tf_op jit(solution)/shard_map/ppermute | solution.py:115
  3.7 2.6 %collective-permute-start.3 = (bf16[32,2048]{1,0:T(8,128)(2,1)}, bf16[32,2048]{1,0:T(8,128)(2,1)S(1)}, u32[]{:S(2)}, u32[]{:S(2)}) collective-permute-start(bf16[32,2048]{1,0:T(8,128)(2,1)} %param.7), channel_id=1, source_target_pairs={{0,16},{1,17},{2,18},{3,19},{4,20},{5,21},{6,22},{7,23},{8,24},{9,... | collective-permute-start | bytes 393224 | tf_op jit(solution)/shard_map/ppermute | solution.py:115
  6.3 0.7 convert_bitcast_fusion
  7.0 0.8 select_reduce_fusion.1
  7.8 0.9 %pad_maximum_fusion = bf16[32,2176]{1,0:T(8,128)(2,1)S(1)} fusion(bf16[32,128]{1,0:T(8,128)(2,1)S(1)} %select_reduce_fusion.1, bf16[32,2048]{1,0:T(8,128)(2,1)} %param.10), kind=kLoop, calls=%fused_computation.3 | loop fusion | flops 278528 | bytes 278528 | tf_op jit(solution)/shard_map/concatenate | solution.py:461
  9.0 1.7 %collective-permute-start.1 = (bf16[32,2176]{1,0:T(8,128)(2,1)S(1)}, bf16[32,2176]{1,0:T(8,128)(2,1)S(1)}, u32[]{:S(2)}, u32[]{:S(2)}) collective-permute-start(bf16[32,2176]{1,0:T(8,128)(2,1)S(1)} %pad_maximum_fusion), channel_id=1, source_target_pairs={{0,1},{1,0},{2,3},{3,2},{4,5},{5,4},{6,7},{7,6},{8,9},{9,8},{10,11... | collective-permute-start | bytes 417800 | tf_op jit(solution)/shard_map/ppermute | solution.py:115
  10.7 1.5 %collective-permute-start.2 = (bf16[32,2176]{1,0:T(8,128)(2,1)S(1)}, bf16[32,2176]{1,0:T(8,128)(2,1)S(1)}, u32[]{:S(2)}, u32[]{:S(2)}) collective-permute-start(bf16[32,2176]{1,0:T(8,128)(2,1)S(1)} %pad_maximum_fusion), channel_id=1, source_target_pairs={{0,5},{1,4},{2,7},{3,6},{4,1},{5,0},{6,3},{7,2},{8,13},{9,12},{10,... | collective-permute-start | bytes 417800 | tf_op jit(solution)/shard_map/ppermute | solution.py:115
  12.2 0.9 %constant_dynamic-update-slice_fusion.3 = bf16[128,2048]{1,0:T(8,128)(2,1)S(1)} fusion(bf16[32,2048]{1,0:T(8,128)(2,1)} %param.7), kind=kLoop, calls=%fused_computation.10 | loop fusion | bytes 262144
  13.1 3.8 %collective-permute-done.3 = bf16[32,2048]{1,0:T(8,128)(2,1)S(1)} collective-permute-done((bf16[32,2048]{1,0:T(8,128)(2,1)}, bf16[32,2048]{1,0:T(8,128)(2,1)S(1)}, u32[]{:S(2)}, u32[]{:S(2)}) %collective-permute-start.3) | collective-permute-done | bytes 131104 | tf_op jit(solution)/shard_map/ppermute | solution.py:115
  16.9 0.7 collective-permute-done.2.refs_1_
  17.7 0.9 %collective-permute-start.8 = (bf16[128,2048]{1,0:T(8,128)(2,1)S(1)}, bf16[128,2048]{1,0:T(8,128)(2,1)S(1)}, u32[]{:S(2)}, u32[]{:S(2)}) collective-permute-start(bf16[128,2048]{1,0:T(8,128)(2,1)S(1)} %constant_dynamic-update-slice_fusion.refs_0_), channel_id=1, source_target_pairs={{0,4},{1,5},{2,6},{3,7},{4,0},{5,1},{6,2},{7,3},{8,12},{9,13},{10,... | collective-permute-start | bytes 1572872 | tf_op jit(solution)/shard_map/ppermute | solution.py:115
  18.6 1.4 %collective-permute-start.9 = (bf16[128,2048]{1,0:T(8,128)(2,1)S(1)}, bf16[128,2048]{1,0:T(8,128)(2,1)S(1)}, u32[]{:S(2)}, u32[]{:S(2)}) collective-permute-start(bf16[128,2048]{1,0:T(8,128)(2,1)S(1)} %constant_dynamic-update-slice_fusion.refs_0_), channel_id=1, source_target_pairs={{0,1},{1,0},{2,3},{3,2},{4,5},{5,4},{6,7},{7,6},{8,9},{9,8},{10,11... | collective-permute-start | bytes 1572872 | tf_op jit(solution)/shard_map/ppermute | solution.py:115
  20.1 2.9 %collective-permute-start.5 = (bf16[32,2176]{1,0:T(8,128)(2,1)S(1)}, bf16[32,2176]{1,0:T(8,128)(2,1)S(1)}, u32[]{:S(2)}, u32[]{:S(2)}) collective-permute-start(bf16[32,2176]{1,0:T(8,128)(2,1)S(1)} %pad_maximum_fusion), channel_id=1, source_target_pairs={{0,16},{1,17},{2,18},{3,19},{4,20},{5,21},{6,22},{7,23},{8,24},{9,... | collective-permute-start | bytes 417800 | tf_op jit(solution)/shard_map/ppermute | solution.py:115
  23.1 1.0 %collective-permute-start.6 = (bf16[32,2176]{1,0:T(8,128)(2,1)S(1)}, bf16[32,2176]{1,0:T(8,128)(2,1)S(1)}, u32[]{:S(2)}, u32[]{:S(2)}) collective-permute-start(bf16[32,2176]{1,0:T(8,128)(2,1)S(1)} %pad_maximum_fusion), channel_id=1, source_target_pairs={{0,8},{1,9},{2,10},{3,11},{4,12},{5,13},{6,14},{7,15},{8,0},{9,1},... | collective-permute-start | bytes 417800 | tf_op jit(solution)/shard_map/ppermute | solution.py:115
  24.6 7.6 %collective-permute-done.5 = bf16[32,2176]{1,0:T(8,128)(2,1)S(1)} collective-permute-done((bf16[32,2176]{1,0:T(8,128)(2,1)S(1)}, bf16[32,2176]{1,0:T(8,128)(2,1)S(1)}, u32[]{:S(2)}, u32[]{:S(2)}) %collective-permute-start.5) | collective-permute-done | bytes 139296 | tf_op jit(solution)/shard_map/ppermute | solution.py:115
  32.9 1.1 %collective-permute-start.10 = (bf16[128,2176]{1,0:T(8,128)(2,1)S(1)}, bf16[128,2176]{1,0:T(8,128)(2,1)S(1)}, u32[]{:S(2)}, u32[]{:S(2)}) collective-permute-start(bf16[128,2176]{1,0:T(8,128)(2,1)S(1)} %constant_dynamic-update-slice_fusion.4.refs_0_), channel_id=1, source_target_pairs={{0,4},{1,5},{2,6},{3,7},{4,0},{5,1},{6,2},{7,3},{8,12},{9,13},{10,... | collective-permute-start | bytes 1671176 | tf_op jit(solution)/shard_map/ppermute | solution.py:115
  34.8 3.6 %collective-permute-start.16 = (bf16[32,2176]{1,0:T(8,128)(2,1)S(1)}, bf16[32,2176]{1,0:T(8,128)(2,1)S(1)}, u32[]{:S(2)}, u32[]{:S(2)}) collective-permute-start(bf16[32,2176]{1,0:T(8,128)(2,1)S(1)} %collective-permute-done.1), channel_id=1, source_target_pairs={{0,16},{1,17},{2,18},{3,19},{4,20},{5,21},{6,22},{7,23},{8,24},{9,... | collective-permute-start | bytes 417800 | tf_op jit(solution)/shard_map/ppermute | solution.py:115
  38.5 6.3 %shard_map.110 = (bf16[768,2048]{1,0:T(8,128)(2,1)S(1)}, bf16[768,2048]{1,0:T(8,128)(2,1)S(1)}, bf16[2048,768]{1,0:T(8,128)(2,1)S(1)}, bf16[512,2048]{1,0:T(8,12...) custom-call(bf16[128,2048]{1,0:T(8,128)(2,1)} %copy-done.10, ...), custom_call_target="tpu_custom_call" | custom-call | flops 3221225472 | bytes 2097152 | tf_op jit(solution)/shard_map/pallas_call | solution.py:210
  44.8 3.7 %shard_map.111 = (bf16[128,2176]{1,0:T(8,128)(2,1)S(1)}, bf16[128,2176]{1,0:T(8,128)(2,1)S(1)}, bf16[256,2176]{1,0:T(8,128)(2,1)S(1)}, bf16[256,2304]{1,0:T(8,128)(2,1)S(1)}, f32[8,128]{1,0:T(8,128)S(1)}) custom-call(s32[2]{0:T(128)S(1)} %pad_add_fusion.place_ref.refs_8_, bf16[128,2176]{1,0:T(8,128)(2,1)S(1)} %constant_dynamic-update-slice_fusion.4.refs_0_, ...), custom_call_target="tpu_custom_call" | custom-call | tf_op jit(solution)/shard_map/pallas_call | solution.py:273
  50.0 0.6 collective-permute-done.19.refs_0_
  50.6 2.2 %shard_map.112 = (bf16[128,2176]{1,0:T(8,128)(2,1)S(1)}, bf16[128,2176]{1,0:T(8,128)(2,1)S(1)}, bf16[128,2304]{1,0:T(8,128)(2,1)S(1)}, f32[8,128]{1,0:T(8,128)}) custom-call(s32[2]{0:T(128)S(1)} %pad_add_fusion.place_ref.refs_8_, bf16[128,2176]{1,0:T(8,128)(2,1)S(1)} %collective-permute-done.19.refs_0_, f32[512,768]{1,0:T(8,128)S(1)} %get-tuple-element.76.refs_2_.refs_1_, ...), custom_call_target="tpu_custom_call" | custom-call | tf_op jit(solution)/shard_map/pallas_call | solution.py:273
  53.2 2.2 %shard_map.113 = (bf16[128,2176]{1,0:T(8,128)(2,1)S(1)}, bf16[128,2176]{1,0:T(8,128)(2,1)S(1)}, bf16[128,2304]{1,0:T(8,128)(2,1)S(1)}, f32[8,128]{1,0:T(8,128)}) custom-call(s32[2]{0:T(128)S(1)} %pad_add_fusion.place_ref.refs_8_, bf16[128,2176]{1,0:T(8,128)(2,1)S(1)} %collective-permute-done.10.refs_0_, f32[512,768]{1,0:T(8,128)S(1)} %get-tuple-element.76.refs_2_.refs_1_, ...), custom_call_target="tpu_custom_call" | custom-call | tf_op jit(solution)/shard_map/pallas_call | solution.py:273
  55.7 1.7 %collective-permute-start.25 = (bf16[128,2176]{1,0:T(8,128)(2,1)S(1)}, bf16[128,2176]{1,0:T(8,128)(2,1)S(1)}, u32[]{:S(2)}, u32[]{:S(2)}) collective-permute-start(bf16[128,2176]{1,0:T(8,128)(2,1)S(1)} %add_convert_fusion.1), channel_id=1, source_target_pairs={{0,4},{1,5},{2,6},{3,7},{4,0},{5,1},{6,2},{7,3},{8,12},{9,13},{10,... | collective-permute-start | bytes 1671176 | tf_op jit(solution)/shard_map/ppermute | solution.py:115
  57.4 0.9 %collective-permute-start.17 = (bf16[64,2176]{1,0:T(8,128)(2,1)S(1)}, bf16[64,2176]{1,0:T(8,128)(2,1)S(1)}, u32[]{:S(2)}, u32[]{:S(2)}) collective-permute-start(bf16[64,2176]{1,0:T(8,128)(2,1)S(1)} %constant_dynamic-update-slice_fusion.8.refs_0_), channel_id=1, source_target_pairs={{0,8},{1,9},{2,10},{3,11},{4,12},{5,13},{6,14},{7,15},{8,0},{9,1},... | collective-permute-start | bytes 835592 | tf_op jit(solution)/shard_map/ppermute | solution.py:115
  58.9 6.6 %shard_map.114 = (bf16[384,2048]{1,0:T(8,128)(2,1)S(1)}, bf16[384,2048]{1,0:T(8,128)(2,1)S(1)}, bf16[384,2048]{1,0:T(8,128)(2,1)S(1)}, bf16[384,512]{1,0:T(8,128...) custom-call(s32[2]{0:T(128)S(1)} %pad_add_fusion.place_ref.refs_8_, ...), custom_call_target="tpu_custom_call" | custom-call | tf_op jit(solution)/shard_map/pallas_call | solution.py:341
  65.4 5.1 %collective-permute-done.25 = bf16[128,2176]{1,0:T(8,128)(2,1)S(1)} collective-permute-done((bf16[128,2176]{1,0:T(8,128)(2,1)S(1)}, bf16[128,2176]{1,0:T(8,128)(2,1)S(1)}, u32[]{:S(2)}, u32[]{:S(2)}) %collective-permute-start.25) | collective-permute-done | bytes 557088 | tf_op jit(solution)/shard_map/ppermute | solution.py:115
  71.0 2.8 %collective-permute-start.26 = (bf16[32,2176]{1,0:T(8,128)(2,1)S(1)}, bf16[32,2176]{1,0:T(8,128)(2,1)S(1)}, u32[]{:S(2)}, u32[]{:S(2)}) collective-permute-start(bf16[32,2176]{1,0:T(8,128)(2,1)S(1)} %get-tuple-element.127), channel_id=1, source_target_pairs={{0,16},{1,17},{2,18},{3,19},{4,20},{5,21},{6,22},{7,23},{8,24},{9,... | collective-permute-start | bytes 417800 | tf_op jit(solution)/shard_map/ppermute | solution.py:115
  74.2 1.2 %collective-permute-start.28 = (bf16[32,2176]{1,0:T(8,128)(2,1)S(1)}, bf16[32,2176]{1,0:T(8,128)(2,1)S(1)}, u32[]{:S(2)}, u32[]{:S(2)}) collective-permute-start(bf16[32,2176]{1,0:T(8,128)(2,1)S(1)} %get-tuple-element.125), channel_id=1, source_target_pairs={{0,24},{1,25},{2,26},{3,27},{4,28},{5,29},{6,30},{7,31},{8,16},{9,... | collective-permute-start | bytes 417800 | tf_op jit(solution)/shard_map/ppermute | solution.py:115
  75.5 0.9 copy-done.5
  76.3 8.8 %shard_map.115 = (bf16[1,384,2048]{2,1,0:T(8,128)(2,1)}, bf16[1,384,2048]{2,1,0:T(8,128)(2,1)}, bf16[1,384,2048]{2,1,0:T(8,128)(2,1)}) custom-call(s32[2]{0:T(128)S(1)} %pad_add_fusion.place_ref.refs_8_, bf16[64,2176]{1,0:T(8,128)(2,1)} %copy-done.6, bf16[32,2176]{1,0:T(8,128)(2,1)} %copy-done.8, bf16[160,2176]{1,0:T(8,128)(2,1)} %copy-done.4, ...), custom_call_target="tpu_custom_call" | custom-call | flops 3221225472 | bytes 13631488 | tf_op jit(solution)/shard_map/pallas_call | solution.py:412
  85.2 0.7 add_convert_fusion.2
  85.9 0.8 select_reduce_fusion
  (87 shorter events, 5.8 us)
Async XLA Ops:
  0.6 8.3 %collective-permute-start = (bf16[32,2048]{1,0:T(8,128)(2,1)}, bf16[32,2048]{1,0:T(8,128)(2,1)S(1)}, u32[]{:S(2)}, u32[]{:S(2)}) collective-permute-start(bf16[32,2048]{1,0:T(8,128)(2,1)} %param.7), channel_id=1, source_target_pairs={{0,8},{1,9},{2,10},{3,11},{4,12},{5,13},{6,14},{7,15},{8,0},{9,1},... | collective-permute-start | bytes 393224 | tf_op jit(solution)/shard_map/ppermute | solution.py:115
  3.7 13.2 %collective-permute-start.3 = (bf16[32,2048]{1,0:T(8,128)(2,1)}, bf16[32,2048]{1,0:T(8,128)(2,1)S(1)}, u32[]{:S(2)}, u32[]{:S(2)}) collective-permute-start(bf16[32,2048]{1,0:T(8,128)(2,1)} %param.7), channel_id=1, source_target_pairs={{0,16},{1,17},{2,18},{3,19},{4,20},{5,21},{6,22},{7,23},{8,24},{9,... | collective-permute-start | bytes 393224 | tf_op jit(solution)/shard_map/ppermute | solution.py:115
  6.3 10.6 %collective-permute-start.4 = (bf16[32,2048]{1,0:T(8,128)(2,1)}, bf16[32,2048]{1,0:T(8,128)(2,1)S(1)}, u32[]{:S(2)}, u32[]{:S(2)}) collective-permute-start(bf16[32,2048]{1,0:T(8,128)(2,1)} %param.7), channel_id=1, source_target_pairs={{0,24},{1,25},{2,26},{3,27},{4,28},{5,29},{6,30},{7,31},{8,16},{9,... | collective-permute-start | bytes 393224 | tf_op jit(solution)/shard_map/ppermute | solution.py:115
  9.0 7.9 %collective-permute-start.1 = (bf16[32,2176]{1,0:T(8,128)(2,1)S(1)}, bf16[32,2176]{1,0:T(8,128)(2,1)S(1)}, u32[]{:S(2)}, u32[]{:S(2)}) collective-permute-start(bf16[32,2176]{1,0:T(8,128)(2,1)S(1)} %pad_maximum_fusion), channel_id=1, source_target_pairs={{0,1},{1,0},{2,3},{3,2},{4,5},{5,4},{6,7},{7,6},{8,9},{9,8},{10,11... | collective-permute-start | bytes 417800 | tf_op jit(solution)/shard_map/ppermute | solution.py:115
  10.7 6.9 %collective-permute-start.2 = (bf16[32,2176]{1,0:T(8,128)(2,1)S(1)}, bf16[32,2176]{1,0:T(8,128)(2,1)S(1)}, u32[]{:S(2)}, u32[]{:S(2)}) collective-permute-start(bf16[32,2176]{1,0:T(8,128)(2,1)S(1)} %pad_maximum_fusion), channel_id=1, source_target_pairs={{0,5},{1,4},{2,7},{3,6},{4,1},{5,0},{6,3},{7,2},{8,13},{9,12},{10,... | collective-permute-start | bytes 417800 | tf_op jit(solution)/shard_map/ppermute | solution.py:115
  17.6 32.2 %copy-start.8 = (bf16[32,2176]{1,0:T(8,128)(2,1)}, bf16[32,2176]{1,0:T(8,128)(2,1)S(1)}, u32[]{:S(2)}) copy-start(bf16[32,2176]{1,0:T(8,128)(2,1)S(1)} %collective-permute-done.2.refs_1_) | copy-start | bytes 417796
  17.7 20.8 %copy-start.10 = (bf16[128,2048]{1,0:T(8,128)(2,1)}, bf16[128,2048]{1,0:T(8,128)(2,1)S(1)}, u32[]{:S(2)}) copy-start(bf16[128,2048]{1,0:T(8,128)(2,1)S(1)} %constant_dynamic-update-slice_fusion.refs_0_) | copy-start | bytes 1572868
  17.7 14.5 %collective-permute-start.8 = (bf16[128,2048]{1,0:T(8,128)(2,1)S(1)}, bf16[128,2048]{1,0:T(8,128)(2,1)S(1)}, u32[]{:S(2)}, u32[]{:S(2)}) collective-permute-start(bf16[128,2048]{1,0:T(8,128)(2,1)S(1)} %constant_dynamic-update-slice_fusion.refs_0_), channel_id=1, source_target_pairs={{0,4},{1,5},{2,6},{3,7},{4,0},{5,1},{6,2},{7,3},{8,12},{9,13},{10,... | collective-permute-start | bytes 1572872 | tf_op jit(solution)/shard_map/ppermute | solution.py:115
  18.6 13.6 %collective-permute-start.9 = (bf16[128,2048]{1,0:T(8,128)(2,1)S(1)}, bf16[128,2048]{1,0:T(8,128)(2,1)S(1)}, u32[]{:S(2)}, u32[]{:S(2)}) collective-permute-start(bf16[128,2048]{1,0:T(8,128)(2,1)S(1)} %constant_dynamic-update-slice_fusion.refs_0_), channel_id=1, source_target_pairs={{0,1},{1,0},{2,3},{3,2},{4,5},{5,4},{6,7},{7,6},{8,9},{9,8},{10,11... | collective-permute-start | bytes 1572872 | tf_op jit(solution)/shard_map/ppermute | solution.py:115
  20.1 12.1 %collective-permute-start.5 = (bf16[32,2176]{1,0:T(8,128)(2,1)S(1)}, bf16[32,2176]{1,0:T(8,128)(2,1)S(1)}, u32[]{:S(2)}, u32[]{:S(2)}) collective-permute-start(bf16[32,2176]{1,0:T(8,128)(2,1)S(1)} %pad_maximum_fusion), channel_id=1, source_target_pairs={{0,16},{1,17},{2,18},{3,19},{4,20},{5,21},{6,22},{7,23},{8,24},{9,... | collective-permute-start | bytes 417800 | tf_op jit(solution)/shard_map/ppermute | solution.py:115
  23.1 9.1 %collective-permute-start.6 = (bf16[32,2176]{1,0:T(8,128)(2,1)S(1)}, bf16[32,2176]{1,0:T(8,128)(2,1)S(1)}, u32[]{:S(2)}, u32[]{:S(2)}) collective-permute-start(bf16[32,2176]{1,0:T(8,128)(2,1)S(1)} %pad_maximum_fusion), channel_id=1, source_target_pairs={{0,8},{1,9},{2,10},{3,11},{4,12},{5,13},{6,14},{7,15},{8,0},{9,1},... | collective-permute-start | bytes 417800 | tf_op jit(solution)/shard_map/ppermute | solution.py:115
  24.0 8.2 %collective-permute-start.7 = (bf16[32,2176]{1,0:T(8,128)(2,1)S(1)}, bf16[32,2176]{1,0:T(8,128)(2,1)S(1)}, u32[]{:S(2)}, u32[]{:S(2)}) collective-permute-start(bf16[32,2176]{1,0:T(8,128)(2,1)S(1)} %pad_maximum_fusion), channel_id=1, source_target_pairs={{0,24},{1,25},{2,26},{3,27},{4,28},{5,29},{6,30},{7,31},{8,16},{9,... | collective-permute-start | bytes 417800 | tf_op jit(solution)/shard_map/ppermute | solution.py:115
  32.2 2.4 %collective-permute-start.12 = (bf16[128,2048]{1,0:T(8,128)(2,1)S(1)}, bf16[128,2048]{1,0:T(8,128)(2,1)S(1)}, u32[]{:S(2)}, u32[]{:S(2)}) collective-permute-start(bf16[128,2048]{1,0:T(8,128)(2,1)S(1)} %constant_dynamic-update-slice_fusion.refs_0_), channel_id=1, source_target_pairs={{0,2},{1,3},{2,0},{3,1},{4,6},{5,7},{6,4},{7,5},{8,10},{9,11},{10,... | collective-permute-start | bytes 1572872 | tf_op jit(solution)/shard_map/ppermute | solution.py:115
  32.2 2.6 %collective-permute-start.13 = (bf16[128,2048]{1,0:T(8,128)(2,1)S(1)}, bf16[128,2048]{1,0:T(8,128)(2,1)S(1)}, u32[]{:S(2)}, u32[]{:S(2)}) collective-permute-start(bf16[128,2048]{1,0:T(8,128)(2,1)S(1)} %collective-permute-done.8.refs_2_), channel_id=1, source_target_pairs={{0,2},{1,3},{2,0},{3,1},{4,6},{5,7},{6,4},{7,5},{8,10},{9,11},{10,... | collective-permute-start | bytes 1572872 | tf_op jit(solution)/shard_map/ppermute | solution.py:115
  32.9 12.0 %collective-permute-start.11 = (bf16[128,2176]{1,0:T(8,128)(2,1)S(1)}, bf16[128,2176]{1,0:T(8,128)(2,1)S(1)}, u32[]{:S(2)}, u32[]{:S(2)}) collective-permute-start(bf16[128,2176]{1,0:T(8,128)(2,1)S(1)} %constant_dynamic-update-slice_fusion.4.refs_0_), channel_id=1, source_target_pairs={{0,2},{1,3},{2,0},{3,1},{4,6},{5,7},{6,4},{7,5},{8,10},{9,11},{10,... | collective-permute-start | bytes 1671176 | tf_op jit(solution)/shard_map/ppermute | solution.py:115
  32.9 15.7 %collective-permute-start.10 = (bf16[128,2176]{1,0:T(8,128)(2,1)S(1)}, bf16[128,2176]{1,0:T(8,128)(2,1)S(1)}, u32[]{:S(2)}, u32[]{:S(2)}) collective-permute-start(bf16[128,2176]{1,0:T(8,128)(2,1)S(1)} %constant_dynamic-update-slice_fusion.4.refs_0_), channel_id=1, source_target_pairs={{0,4},{1,5},{2,6},{3,7},{4,0},{5,1},{6,2},{7,3},{8,12},{9,13},{10,... | collective-permute-start | bytes 1671176 | tf_op jit(solution)/shard_map/ppermute | solution.py:115
  34.0 14.6 %collective-permute-start.14 = (bf16[128,2048]{1,0:T(8,128)(2,1)S(1)}, bf16[128,2048]{1,0:T(8,128)(2,1)S(1)}, u32[]{:S(2)}, u32[]{:S(2)}) collective-permute-start(bf16[128,2048]{1,0:T(8,128)(2,1)S(1)} %collective-permute-done.8.refs_2_), channel_id=1, source_target_pairs={{0,1},{1,0},{2,3},{3,2},{4,5},{5,4},{6,7},{7,6},{8,9},{9,8},{10,11... | collective-permute-start | bytes 1572872 | tf_op jit(solution)/shard_map/ppermute | solution.py:115
  34.6 14.0 %collective-permute-start.15 = (bf16[128,2048]{1,0:T(8,128)(2,1)S(1)}, bf16[128,2048]{1,0:T(8,128)(2,1)S(1)}, u32[]{:S(2)}, u32[]{:S(2)}) collective-permute-start(bf16[128,2048]{1,0:T(8,128)(2,1)S(1)} %collective-permute-done.9.refs_7_.refs_10_), channel_id=1, source_target_pairs={{0,2},{1,3},{2,0},{3,1},{4,6},{5,7},{6,4},{7,5},{8,10},{9,11},{10,... | collective-permute-start | bytes 1572872 | tf_op jit(solution)/shard_map/ppermute | solution.py:115
  34.8 13.7 %collective-permute-start.16 = (bf16[32,2176]{1,0:T(8,128)(2,1)S(1)}, bf16[32,2176]{1,0:T(8,128)(2,1)S(1)}, u32[]{:S(2)}, u32[]{:S(2)}) collective-permute-start(bf16[32,2176]{1,0:T(8,128)(2,1)S(1)} %collective-permute-done.1), channel_id=1, source_target_pairs={{0,16},{1,17},{2,18},{3,19},{4,20},{5,21},{6,22},{7,23},{8,24},{9,... | collective-permute-start | bytes 417800 | tf_op jit(solution)/shard_map/ppermute | solution.py:115
  48.6 2.0 %collective-permute-start.19 = (bf16[128,2176]{1,0:T(8,128)(2,1)S(1)}, bf16[128,2176]{1,0:T(8,128)(2,1)S(1)}, u32[]{:S(2)}, u32[]{:S(2)}) collective-permute-start(bf16[128,2176]{1,0:T(8,128)(2,1)S(1)} %collective-permute-done.10.refs_0_), channel_id=1, source_target_pairs={{0,2},{1,3},{2,0},{3,1},{4,6},{5,7},{6,4},{7,5},{8,10},{9,11},{10,... | collective-permute-start | bytes 1671176 | tf_op jit(solution)/shard_map/ppermute | solution.py:115
  48.9 4.0 %collective-permute-start.20 = (bf16[128,2048]{1,0:T(8,128)(2,1)S(1)}, bf16[128,2048]{1,0:T(8,128)(2,1)S(1)}, u32[]{:S(2)}, u32[]{:S(2)}) collective-permute-start(bf16[128,2048]{1,0:T(8,128)(2,1)S(1)} %collective-permute-done.14.refs_8_.refs_11_), channel_id=1, source_target_pairs={{0,2},{1,3},{2,0},{3,1},{4,6},{5,7},{6,4},{7,5},{8,10},{9,11},{10,... | collective-permute-start | bytes 1572872 | tf_op jit(solution)/shard_map/ppermute | solution.py:115
  49.2 3.7 %collective-permute-start.21 = (bf16[128,2176]{1,0:T(8,128)(2,1)S(1)}, bf16[128,2176]{1,0:T(8,128)(2,1)S(1)}, u32[]{:S(2)}, u32[]{:S(2)}) collective-permute-start(bf16[128,2176]{1,0:T(8,128)(2,1)S(1)} %get-tuple-element.90), channel_id=1, source_target_pairs={{0,2},{1,3},{2,0},{3,1},{4,6},{5,7},{6,4},{7,5},{8,10},{9,11},{10,... | collective-permute-start | bytes 1671176 | tf_op jit(solution)/shard_map/ppermute | solution.py:115
  49.4 3.5 %collective-permute-start.22 = (bf16[64,2176]{1,0:T(8,128)(2,1)S(1)}, bf16[64,2176]{1,0:T(8,128)(2,1)S(1)}, u32[]{:S(2)}, u32[]{:S(2)}) collective-permute-start(bf16[64,2176]{1,0:T(8,128)(2,1)S(1)} %constant_dynamic-update-slice_fusion.8.refs_0_), channel_id=1, source_target_pairs={{0,2},{1,3},{2,0},{3,1},{4,6},{5,7},{6,4},{7,5},{8,10},{9,11},{10,... | collective-permute-start | bytes 835592 | tf_op jit(solution)/shard_map/ppermute | solution.py:115
  49.8 3.1 %collective-permute-start.23 = (bf16[32,2176]{1,0:T(8,128)(2,1)S(1)}, bf16[32,2176]{1,0:T(8,128)(2,1)S(1)}, u32[]{:S(2)}, u32[]{:S(2)}) collective-permute-start(bf16[32,2176]{1,0:T(8,128)(2,1)S(1)} %collective-permute-done.2.refs_1_), channel_id=1, source_target_pairs={{0,2},{1,3},{2,0},{3,1},{4,6},{5,7},{6,4},{7,5},{8,10},{9,11},{10,... | collective-permute-start | bytes 417800 | tf_op jit(solution)/shard_map/ppermute | solution.py:115
  53.0 2.6 %collective-permute-start.24 = (bf16[128,2176]{1,0:T(8,128)(2,1)S(1)}, bf16[128,2176]{1,0:T(8,128)(2,1)S(1)}, u32[]{:S(2)}, u32[]{:S(2)}) collective-permute-start(bf16[128,2176]{1,0:T(8,128)(2,1)S(1)} %get-tuple-element.94), channel_id=1, source_target_pairs={{0,2},{1,3},{2,0},{3,1},{4,6},{5,7},{6,4},{7,5},{8,10},{9,11},{10,... | collective-permute-start | bytes 1671176 | tf_op jit(solution)/shard_map/ppermute | solution.py:115
  55.7 14.9 %collective-permute-start.25 = (bf16[128,2176]{1,0:T(8,128)(2,1)S(1)}, bf16[128,2176]{1,0:T(8,128)(2,1)S(1)}, u32[]{:S(2)}, u32[]{:S(2)}) collective-permute-start(bf16[128,2176]{1,0:T(8,128)(2,1)S(1)} %add_convert_fusion.1), channel_id=1, source_target_pairs={{0,4},{1,5},{2,6},{3,7},{4,0},{5,1},{6,2},{7,3},{8,12},{9,13},{10,... | collective-permute-start | bytes 1671176 | tf_op jit(solution)/shard_map/ppermute | solution.py:115
  57.4 13.3 %collective-permute-start.17 = (bf16[64,2176]{1,0:T(8,128)(2,1)S(1)}, bf16[64,2176]{1,0:T(8,128)(2,1)S(1)}, u32[]{:S(2)}, u32[]{:S(2)}) collective-permute-start(bf16[64,2176]{1,0:T(8,128)(2,1)S(1)} %constant_dynamic-update-slice_fusion.8.refs_0_), channel_id=1, source_target_pairs={{0,8},{1,9},{2,10},{3,11},{4,12},{5,13},{6,14},{7,15},{8,0},{9,1},... | collective-permute-start | bytes 835592 | tf_op jit(solution)/shard_map/ppermute | solution.py:115
  58.3 12.4 %collective-permute-start.18 = (bf16[96,2176]{1,0:T(8,128)(2,1)S(1)}, bf16[96,2176]{1,0:T(8,128)(2,1)S(1)}, u32[]{:S(2)}, u32[]{:S(2)}) collective-permute-start(bf16[96,2176]{1,0:T(8,128)(2,1)S(1)} %slice.39), channel_id=1, source_target_pairs={{0,1},{1,0},{2,3},{3,2},{4,5},{5,4},{6,7},{7,6},{8,9},{9,8},{10,11... | collective-permute-start | bytes 1253384 | tf_op jit(solution)/shard_map/ppermute | solution.py:115
  70.9 4.6 %collective-permute-start.29 = (bf16[160,2176]{1,0:T(8,128)(2,1)S(1)}, bf16[160,2176]{1,0:T(8,128)(2,1)S(1)}, u32[]{:S(2)}, u32[]{:S(2)}) collective-permute-start(bf16[160,2176]{1,0:T(8,128)(2,1)S(1)} %constant_dynamic-update-slice_fusion.10.refs_2_), channel_id=1, source_target_pairs={{0,2},{1,3},{2,0},{3,1},{4,6},{5,7},{6,4},{7,5},{8,10},{9,11},{10,... | collective-permute-start | bytes 2088968 | tf_op jit(solution)/shard_map/ppermute | solution.py:115
  71.0 14.2 %collective-permute-start.26 = (bf16[32,2176]{1,0:T(8,128)(2,1)S(1)}, bf16[32,2176]{1,0:T(8,128)(2,1)S(1)}, u32[]{:S(2)}, u32[]{:S(2)}) collective-permute-start(bf16[32,2176]{1,0:T(8,128)(2,1)S(1)} %get-tuple-element.127), channel_id=1, source_target_pairs={{0,16},{1,17},{2,18},{3,19},{4,20},{5,21},{6,22},{7,23},{8,24},{9,... | collective-permute-start | bytes 417800 | tf_op jit(solution)/shard_map/ppermute | solution.py:115
  73.8 11.4 %collective-permute-start.27 = (bf16[32,2176]{1,0:T(8,128)(2,1)S(1)}, bf16[32,2176]{1,0:T(8,128)(2,1)S(1)}, u32[]{:S(2)}, u32[]{:S(2)}) collective-permute-start(bf16[32,2176]{1,0:T(8,128)(2,1)S(1)} %get-tuple-element.126), channel_id=1, source_target_pairs={{0,8},{1,9},{2,10},{3,11},{4,12},{5,13},{6,14},{7,15},{8,0},{9,1},... | collective-permute-start | bytes 417800 | tf_op jit(solution)/shard_map/ppermute | solution.py:115
  74.2 11.0 %collective-permute-start.28 = (bf16[32,2176]{1,0:T(8,128)(2,1)S(1)}, bf16[32,2176]{1,0:T(8,128)(2,1)S(1)}, u32[]{:S(2)}, u32[]{:S(2)}) collective-permute-start(bf16[32,2176]{1,0:T(8,128)(2,1)S(1)} %get-tuple-element.125), channel_id=1, source_target_pairs={{0,24},{1,25},{2,26},{3,27},{4,28},{5,29},{6,30},{7,31},{8,16},{9,... | collective-permute-start | bytes 417800 | tf_op jit(solution)/shard_map/ppermute | solution.py:115
  (13 other events, 65.8 us)

commit v6 on v5

--- a/solution.py
+++ b/solution.py
@@ -433,12 +433,51 @@
         ),
     )(
         place,
-        *[left_out(value) for value in (*cot_rows, w_down)],
+        *[left_out(value) for value in cot_rows[:-1]],
+        cot_rows[-1],
+        left_out(w_down),
         *saved,
         *[left_out(value) for value in x_rows],
         *own,
         after,
     )
+
+
+def finish_kernel(*refs):
+    part_refs, ids_ref, (token_out, gate_out) = refs[:-3], refs[-3], refs[-2:]
+    rows, width = token_out.shape
+    lanes = part_refs[0].shape[1] - width
+    token_out[...] = added(*[ref[:, :width] for ref in part_refs])
+    scores = added(*[ref[:, width:] for ref in part_refs]).astype(jnp.float32)
+    scores = jnp.concatenate([scores, jnp.zeros((lanes - rows, lanes), jnp.float32)], axis=0).T
+    expert = lax.broadcasted_iota(jnp.int32, (lanes, rows), 0)
+    named = [
+        jnp.sum(
+            jnp.where(ids_ref[k : k + 1] == expert, scores[:, :rows], 0.0), axis=0, keepdims=True
+        )
+        for k in range(ids_ref.shape[0])
+    ]
+    gate_out[...] = jnp.concatenate(named, axis=0).astype(jnp.bfloat16)
+
+
+def finished(parts, ids, width):
+    top, rows = ids.shape
+    packed = parts[0].shape[1]
+    return pl.pallas_call(
+        finish_kernel,
+        grid=(1,),
+        in_specs=[pl.BlockSpec((rows, packed), lambda i: (0, 0))] * len(parts)
+        + [pl.BlockSpec((top, rows), lambda i: (0, 0))],
+        out_specs=[
+            pl.BlockSpec((rows, width), lambda i: (0, 0)),
+            pl.BlockSpec((top, rows), lambda i: (0, 0)),
+        ],
+        out_shape=[
+            jax.ShapeDtypeStruct((rows, width), jnp.bfloat16),
+            jax.ShapeDtypeStruct((top, rows), jnp.bfloat16),
+        ],
+        **kernel_params(0, 0, 0, 8),
+    )(*parts, ids)
 
 
 def dense_body(tokens, expert_ids, gate_weights, cotangent, w_gate, w_up, w_down):
@@ -522,15 +561,13 @@
     saved = (slope, swish, hidden)
     grads = list(whole_gradients(place, cot_away, w_down, saved, x_away, own, token))
     parts = [
-        partial[:block],
+        partial,
         swap(partial[block : 2 * block], high),
         swap(partial[2 * block : 3 * block], low),
         swap(partial[3 * block :], low | high),
     ]
     *parts, grads[0] = tied(*parts, grads[0])
-    token_grad = added(*[value[:, :model_width] for value in parts])
-    scores = added(*[value[:, model_width:] for value in parts]).astype(jnp.float32)
-    gate_grad = jnp.sum(jnp.where(named, scores[None], 0.0), axis=2).astype(jnp.bfloat16)
+    token_grad, gate_grad = finished(parts, expert_ids.T, model_width)
     return (token_grad, gate_grad.T, *grads)
 
 

time: 86.9 us -> 86.2 us (level)
  other arithmetic: 4.33 us -> 2.84 us
  local copies, waits for them, and re-layouts: 2.09 us -> 1.22 us
    pallas_call x0 -> x1, Pallas kernels: none -> 0.91 us  [finished(): pl.pallas_call(finish_kernel, grid=(1,), in_specs=[pl.BlockSpec((rows, pa...]
    unnamed x38 -> x36, local copies, waits for them, and re-layouts: 1.93 us -> 1.07 us
  transfers between devices with their start and end apart: 30 -> 30, of which waited for: 7 -> 8; matrix products, arithmetic and copies ran while one was open for 4% -> 4% of each run, Pallas kernels for 34% -> 35%
where the time goes in v6:
time: 86.2 us; the launch traced here: 85.9 us
  starting transfers between devices  31 us (36%)
  Pallas kernels  30.7 us (36%)
  waiting for transfers between devices  19.2 us (22%)
  other arithmetic  2.84 us (3%)
  local copies, waits for them, and re-layouts  1.22 us (1%)
  between operations  1.07 us (1%)
    ppermute x30, starting transfers between devices, swap(): return lax.ppermute(value, BOTH, [(i, i ^ flip) for i in range(count)])  31 us
    ppermute x30, waiting for transfers between devices, swap(): return lax.ppermute(value, BOTH, [(i, i ^ flip) for i in range(count)])  19.2 us
    pallas_call x1, Pallas kernels, whole_gradients(): pl.pallas_call(whole_gradient_kernel, grid=(width // tile,), in_specs=[IN...  8.71 us
    pallas_call x3, Pallas kernels, backward(): pl.pallas_call(functools.partial(backward_kernel, first, count), in_specs...  8.16 us
    pallas_call x1, Pallas kernels, own_gradients(): pl.pallas_call(own_gradient_kernel, grid=(width // tile,), in_specs=[IN_S...  6.57 us
    pallas_call x1, Pallas kernels, forward(): pl.pallas_call(forward_kernel, in_specs=[IN_HBM] * 7, out_specs=[IN_VMEM]...  6.34 us
  transfers between devices with their start and end apart: 30, of which 8 were waited for; matrix products, arithmetic and copies ran while one was open for 4% of the time, Pallas kernels for 35%

profile of v6, /device:TPU:0, one launch (start us, length us, event | category | flops | bytes accessed | tf_op | source)
XLA Modules:
  0.0 85.9 jit_solution(13799057555109969137)
XLA Ops:
  0.6 3.1 %collective-permute-start = (bf16[32,2048]{1,0:T(8,128)(2,1)}, bf16[32,2048]{1,0:T(8,128)(2,1)S(1)}, u32[]{:S(2)}, u32[]{:S(2)}) collective-permute-start(bf16[32,2048]{1,0:T(8,128)(2,1)} %param.7), channel_id=1, source_target_pairs={{0,8},{1,9},{2,10},{3,11},{4,12},{5,13},{6,14},{7,15},{8,0},{9,1},... | collective-permute-start | bytes 393224 | tf_op jit(solution)/shard_map/ppermute | solution.py:115
  3.7 2.6 %collective-permute-start.3 = (bf16[32,2048]{1,0:T(8,128)(2,1)}, bf16[32,2048]{1,0:T(8,128)(2,1)S(1)}, u32[]{:S(2)}, u32[]{:S(2)}) collective-permute-start(bf16[32,2048]{1,0:T(8,128)(2,1)} %param.7), channel_id=1, source_target_pairs={{0,16},{1,17},{2,18},{3,19},{4,20},{5,21},{6,22},{7,23},{8,24},{9,... | collective-permute-start | bytes 393224 | tf_op jit(solution)/shard_map/ppermute | solution.py:115
  6.3 0.7 convert_bitcast_fusion
  7.0 0.8 select_reduce_fusion
  7.8 0.9 %pad_maximum_fusion = bf16[32,2176]{1,0:T(8,128)(2,1)S(1)} fusion(bf16[32,128]{1,0:T(8,128)(2,1)S(1)} %select_reduce_fusion, bf16[32,2048]{1,0:T(8,128)(2,1)} %param.10), kind=kLoop, calls=%fused_computation.2 | loop fusion | flops 278528 | bytes 278528 | tf_op jit(solution)/shard_map/concatenate | solution.py:500
  9.0 1.7 %collective-permute-start.1 = (bf16[32,2176]{1,0:T(8,128)(2,1)S(1)}, bf16[32,2176]{1,0:T(8,128)(2,1)S(1)}, u32[]{:S(2)}, u32[]{:S(2)}) collective-permute-start(bf16[32,2176]{1,0:T(8,128)(2,1)S(1)} %pad_maximum_fusion), channel_id=1, source_target_pairs={{0,1},{1,0},{2,3},{3,2},{4,5},{5,4},{6,7},{7,6},{8,9},{9,8},{10,11... | collective-permute-start | bytes 417800 | tf_op jit(solution)/shard_map/ppermute | solution.py:115
  10.7 1.5 %collective-permute-start.2 = (bf16[32,2176]{1,0:T(8,128)(2,1)S(1)}, bf16[32,2176]{1,0:T(8,128)(2,1)S(1)}, u32[]{:S(2)}, u32[]{:S(2)}) collective-permute-start(bf16[32,2176]{1,0:T(8,128)(2,1)S(1)} %pad_maximum_fusion), channel_id=1, source_target_pairs={{0,5},{1,4},{2,7},{3,6},{4,1},{5,0},{6,3},{7,2},{8,13},{9,12},{10,... | collective-permute-start | bytes 417800 | tf_op jit(solution)/shard_map/ppermute | solution.py:115
  12.2 0.9 %constant_dynamic-update-slice_fusion.3 = bf16[128,2048]{1,0:T(8,128)(2,1)S(1)} fusion(bf16[32,2048]{1,0:T(8,128)(2,1)} %param.7), kind=kLoop, calls=%fused_computation.8 | loop fusion | bytes 262144
  13.1 3.8 %collective-permute-done.3 = bf16[32,2048]{1,0:T(8,128)(2,1)S(1)} collective-permute-done((bf16[32,2048]{1,0:T(8,128)(2,1)}, bf16[32,2048]{1,0:T(8,128)(2,1)S(1)}, u32[]{:S(2)}, u32[]{:S(2)}) %collective-permute-start.3) | collective-permute-done | bytes 131104 | tf_op jit(solution)/shard_map/ppermute | solution.py:115
  16.9 0.7 collective-permute-done.2.refs_1_
  17.7 0.9 %collective-permute-start.8 = (bf16[128,2048]{1,0:T(8,128)(2,1)S(1)}, bf16[128,2048]{1,0:T(8,128)(2,1)S(1)}, u32[]{:S(2)}, u32[]{:S(2)}) collective-permute-start(bf16[128,2048]{1,0:T(8,128)(2,1)S(1)} %constant_dynamic-update-slice_fusion.refs_0_), channel_id=1, source_target_pairs={{0,4},{1,5},{2,6},{3,7},{4,0},{5,1},{6,2},{7,3},{8,12},{9,13},{10,... | collective-permute-start | bytes 1572872 | tf_op jit(solution)/shard_map/ppermute | solution.py:115
  18.6 1.4 %collective-permute-start.9 = (bf16[128,2048]{1,0:T(8,128)(2,1)S(1)}, bf16[128,2048]{1,0:T(8,128)(2,1)S(1)}, u32[]{:S(2)}, u32[]{:S(2)}) collective-permute-start(bf16[128,2048]{1,0:T(8,128)(2,1)S(1)} %constant_dynamic-update-slice_fusion.refs_0_), channel_id=1, source_target_pairs={{0,1},{1,0},{2,3},{3,2},{4,5},{5,4},{6,7},{7,6},{8,9},{9,8},{10,11... | collective-permute-start | bytes 1572872 | tf_op jit(solution)/shard_map/ppermute | solution.py:115
  20.1 2.9 %collective-permute-start.5 = (bf16[32,2176]{1,0:T(8,128)(2,1)S(1)}, bf16[32,2176]{1,0:T(8,128)(2,1)S(1)}, u32[]{:S(2)}, u32[]{:S(2)}) collective-permute-start(bf16[32,2176]{1,0:T(8,128)(2,1)S(1)} %pad_maximum_fusion), channel_id=1, source_target_pairs={{0,16},{1,17},{2,18},{3,19},{4,20},{5,21},{6,22},{7,23},{8,24},{9,... | collective-permute-start | bytes 417800 | tf_op jit(solution)/shard_map/ppermute | solution.py:115
  23.1 1.0 %collective-permute-start.6 = (bf16[32,2176]{1,0:T(8,128)(2,1)S(1)}, bf16[32,2176]{1,0:T(8,128)(2,1)S(1)}, u32[]{:S(2)}, u32[]{:S(2)}) collective-permute-start(bf16[32,2176]{1,0:T(8,128)(2,1)S(1)} %pad_maximum_fusion), channel_id=1, source_target_pairs={{0,8},{1,9},{2,10},{3,11},{4,12},{5,13},{6,14},{7,15},{8,0},{9,1},... | collective-permute-start | bytes 417800 | tf_op jit(solution)/shard_map/ppermute | solution.py:115
  24.0 0.6 collective-permute-start.7
  24.6 7.6 %collective-permute-done.5 = bf16[32,2176]{1,0:T(8,128)(2,1)S(1)} collective-permute-done((bf16[32,2176]{1,0:T(8,128)(2,1)S(1)}, bf16[32,2176]{1,0:T(8,128)(2,1)S(1)}, u32[]{:S(2)}, u32[]{:S(2)}) %collective-permute-start.5) | collective-permute-done | bytes 139296 | tf_op jit(solution)/shard_map/ppermute | solution.py:115
  32.9 1.1 %collective-permute-start.10 = (bf16[128,2176]{1,0:T(8,128)(2,1)S(1)}, bf16[128,2176]{1,0:T(8,128)(2,1)S(1)}, u32[]{:S(2)}, u32[]{:S(2)}) collective-permute-start(bf16[128,2176]{1,0:T(8,128)(2,1)S(1)} %constant_dynamic-update-slice_fusion.4.refs_0_), channel_id=1, source_target_pairs={{0,4},{1,5},{2,6},{3,7},{4,0},{5,1},{6,2},{7,3},{8,12},{9,13},{10,... | collective-permute-start | bytes 1671176 | tf_op jit(solution)/shard_map/ppermute | solution.py:115
  34.8 3.6 %collective-permute-start.16 = (bf16[32,2176]{1,0:T(8,128)(2,1)S(1)}, bf16[32,2176]{1,0:T(8,128)(2,1)S(1)}, u32[]{:S(2)}, u32[]{:S(2)}) collective-permute-start(bf16[32,2176]{1,0:T(8,128)(2,1)S(1)} %collective-permute-done.1), channel_id=1, source_target_pairs={{0,16},{1,17},{2,18},{3,19},{4,20},{5,21},{6,22},{7,23},{8,24},{9,... | collective-permute-start | bytes 417800 | tf_op jit(solution)/shard_map/ppermute | solution.py:115
  38.5 6.3 %shard_map.110 = (bf16[768,2048]{1,0:T(8,128)(2,1)S(1)}, bf16[768,2048]{1,0:T(8,128)(2,1)S(1)}, bf16[2048,768]{1,0:T(8,128)(2,1)S(1)}, bf16[512,2048]{1,0:T(8,12...) custom-call(bf16[128,2048]{1,0:T(8,128)(2,1)} %copy-done.10, ...), custom_call_target="tpu_custom_call" | custom-call | flops 3221225472 | bytes 2097152 | tf_op jit(solution)/shard_map/pallas_call | solution.py:210
  44.8 3.7 %shard_map.111 = (bf16[128,2176]{1,0:T(8,128)(2,1)S(1)}, bf16[128,2176]{1,0:T(8,128)(2,1)S(1)}, bf16[256,2176]{1,0:T(8,128)(2,1)S(1)}, bf16[256,2304]{1,0:T(8,128)(2,1)S(1)}, f32[8,128]{1,0:T(8,128)S(1)}) custom-call(s32[2]{0:T(128)S(1)} %pad_add_fusion.place_ref.refs_8_, bf16[128,2176]{1,0:T(8,128)(2,1)S(1)} %constant_dynamic-update-slice_fusion.4.refs_0_, ...), custom_call_target="tpu_custom_call" | custom-call | tf_op jit(solution)/shard_map/pallas_call | solution.py:273
  50.0 0.6 collective-permute-done.19.refs_0_
  50.6 2.2 %shard_map.112 = (bf16[128,2176]{1,0:T(8,128)(2,1)S(1)}, bf16[128,2176]{1,0:T(8,128)(2,1)S(1)}, bf16[128,2304]{1,0:T(8,128)(2,1)S(1)}, f32[8,128]{1,0:T(8,128)}) custom-call(s32[2]{0:T(128)S(1)} %pad_add_fusion.place_ref.refs_8_, bf16[128,2176]{1,0:T(8,128)(2,1)S(1)} %collective-permute-done.19.refs_0_, f32[512,768]{1,0:T(8,128)S(1)} %get-tuple-element.78.refs_2_.refs_1_, ...), custom_call_target="tpu_custom_call" | custom-call | tf_op jit(solution)/shard_map/pallas_call | solution.py:273
  53.2 2.2 %shard_map.113 = (bf16[128,2176]{1,0:T(8,128)(2,1)S(1)}, bf16[128,2176]{1,0:T(8,128)(2,1)S(1)}, bf16[128,2304]{1,0:T(8,128)(2,1)S(1)}, f32[8,128]{1,0:T(8,128)}) custom-call(s32[2]{0:T(128)S(1)} %pad_add_fusion.place_ref.refs_8_, bf16[128,2176]{1,0:T(8,128)(2,1)S(1)} %collective-permute-done.10.refs_0_, f32[512,768]{1,0:T(8,128)S(1)} %get-tuple-element.78.refs_2_.refs_1_, ...), custom_call_target="tpu_custom_call" | custom-call | tf_op jit(solution)/shard_map/pallas_call | solution.py:273
  55.7 1.7 %collective-permute-start.25 = (bf16[128,2176]{1,0:T(8,128)(2,1)S(1)}, bf16[128,2176]{1,0:T(8,128)(2,1)S(1)}, u32[]{:S(2)}, u32[]{:S(2)}) collective-permute-start(bf16[128,2176]{1,0:T(8,128)(2,1)S(1)} %add_convert_fusion.1), channel_id=1, source_target_pairs={{0,4},{1,5},{2,6},{3,7},{4,0},{5,1},{6,2},{7,3},{8,12},{9,13},{10,... | collective-permute-start | bytes 1671176 | tf_op jit(solution)/shard_map/ppermute | solution.py:115
  57.5 0.9 %collective-permute-start.17 = (bf16[64,2176]{1,0:T(8,128)(2,1)S(1)}, bf16[64,2176]{1,0:T(8,128)(2,1)S(1)}, u32[]{:S(2)}, u32[]{:S(2)}) collective-permute-start(bf16[64,2176]{1,0:T(8,128)(2,1)S(1)} %constant_dynamic-update-slice_fusion.8.refs_0_), channel_id=1, source_target_pairs={{0,8},{1,9},{2,10},{3,11},{4,12},{5,13},{6,14},{7,15},{8,0},{9,1},... | collective-permute-start | bytes 835592 | tf_op jit(solution)/shard_map/ppermute | solution.py:115
  58.9 6.6 %shard_map.114 = (bf16[384,2048]{1,0:T(8,128)(2,1)S(1)}, bf16[384,2048]{1,0:T(8,128)(2,1)S(1)}, bf16[384,2048]{1,0:T(8,128)(2,1)S(1)}, bf16[384,512]{1,0:T(8,128...) custom-call(s32[2]{0:T(128)S(1)} %pad_add_fusion.place_ref.refs_8_, ...), custom_call_target="tpu_custom_call" | custom-call | tf_op jit(solution)/shard_map/pallas_call | solution.py:341
  65.5 5.1 %collective-permute-done.25 = bf16[128,2176]{1,0:T(8,128)(2,1)S(1)} collective-permute-done((bf16[128,2176]{1,0:T(8,128)(2,1)S(1)}, bf16[128,2176]{1,0:T(8,128)(2,1)S(1)}, u32[]{:S(2)}, u32[]{:S(2)}) %collective-permute-start.25) | collective-permute-done | bytes 557088 | tf_op jit(solution)/shard_map/ppermute | solution.py:115
  71.0 2.8 %collective-permute-start.26 = (bf16[32,2176]{1,0:T(8,128)(2,1)S(1)}, bf16[32,2176]{1,0:T(8,128)(2,1)S(1)}, u32[]{:S(2)}, u32[]{:S(2)}) collective-permute-start(bf16[32,2176]{1,0:T(8,128)(2,1)S(1)} %get-tuple-element.131), channel_id=1, source_target_pairs={{0,16},{1,17},{2,18},{3,19},{4,20},{5,21},{6,22},{7,23},{8,24},{9,... | collective-permute-start | bytes 417800 | tf_op jit(solution)/shard_map/ppermute | solution.py:115
  74.2 1.2 %collective-permute-start.28 = (bf16[32,2176]{1,0:T(8,128)(2,1)S(1)}, bf16[32,2176]{1,0:T(8,128)(2,1)S(1)}, u32[]{:S(2)}, u32[]{:S(2)}) collective-permute-start(bf16[32,2176]{1,0:T(8,128)(2,1)S(1)} %get-tuple-element.129), channel_id=1, source_target_pairs={{0,24},{1,25},{2,26},{3,27},{4,28},{5,29},{6,30},{7,31},{8,16},{9,... | collective-permute-start | bytes 417800 | tf_op jit(solution)/shard_map/ppermute | solution.py:115
  75.5 8.7 %shard_map.115 = (bf16[1,384,2048]{2,1,0:T(8,128)(2,1)}, bf16[1,384,2048]{2,1,0:T(8,128)(2,1)}, bf16[1,384,2048]{2,1,0:T(8,128)(2,1)}) custom-call(s32[2]{0:T(128)S(1)} %pad_add_fusion.place_ref.refs_8_, bf16[64,2176]{1,0:T(8,128)(2,1)} %copy-done.6, bf16[32,2176]{1,0:T(8,128)(2,1)} %copy-done.8, bf16[160,2176]{1,0:T(8,128)(2,1)} %copy-done.5, ...), custom_call_target="tpu_custom_call" | custom-call | flops 3221225472 | bytes 13631488 | tf_op jit(solution)/shard_map/pallas_call | solution.py:412
  84.2 0.8 collective-permute-done.28.refs_3_
  85.0 0.9 %shard_map.116 = (bf16[32,2048]{1,0:T(8,128)(2,1)}, bf16[8,32]{1,0:T(8,128)(2,1)}) custom-call(bf16[128,2176]{1,0:T(8,128)(2,1)S(1)} %add_convert_fusion.refs_0_, bf16[32,2176]{1,0:T(8,128)(2,1)S(1)} %collective-permute-done.26.refs_1_, bf16[32,2176]{1,0:T(8,128)(2,1)S(1)} %collective-permute-done.27.refs_2_, ...), custom_call_target="tpu_custom_call" | custom-call | tf_op jit(solution)/shard_map/pallas_call | solution.py:466
  (83 shorter events, 5.2 us)
Async XLA Ops:
  0.6 8.3 %collective-permute-start = (bf16[32,2048]{1,0:T(8,128)(2,1)}, bf16[32,2048]{1,0:T(8,128)(2,1)S(1)}, u32[]{:S(2)}, u32[]{:S(2)}) collective-permute-start(bf16[32,2048]{1,0:T(8,128)(2,1)} %param.7), channel_id=1, source_target_pairs={{0,8},{1,9},{2,10},{3,11},{4,12},{5,13},{6,14},{7,15},{8,0},{9,1},... | collective-permute-start | bytes 393224 | tf_op jit(solution)/shard_map/ppermute | solution.py:115
  3.7 13.2 %collective-permute-start.3 = (bf16[32,2048]{1,0:T(8,128)(2,1)}, bf16[32,2048]{1,0:T(8,128)(2,1)S(1)}, u32[]{:S(2)}, u32[]{:S(2)}) collective-permute-start(bf16[32,2048]{1,0:T(8,128)(2,1)} %param.7), channel_id=1, source_target_pairs={{0,16},{1,17},{2,18},{3,19},{4,20},{5,21},{6,22},{7,23},{8,24},{9,... | collective-permute-start | bytes 393224 | tf_op jit(solution)/shard_map/ppermute | solution.py:115
  6.3 10.6 %collective-permute-start.4 = (bf16[32,2048]{1,0:T(8,128)(2,1)}, bf16[32,2048]{1,0:T(8,128)(2,1)S(1)}, u32[]{:S(2)}, u32[]{:S(2)}) collective-permute-start(bf16[32,2048]{1,0:T(8,128)(2,1)} %param.7), channel_id=1, source_target_pairs={{0,24},{1,25},{2,26},{3,27},{4,28},{5,29},{6,30},{7,31},{8,16},{9,... | collective-permute-start | bytes 393224 | tf_op jit(solution)/shard_map/ppermute | solution.py:115
  9.0 7.9 %collective-permute-start.1 = (bf16[32,2176]{1,0:T(8,128)(2,1)S(1)}, bf16[32,2176]{1,0:T(8,128)(2,1)S(1)}, u32[]{:S(2)}, u32[]{:S(2)}) collective-permute-start(bf16[32,2176]{1,0:T(8,128)(2,1)S(1)} %pad_maximum_fusion), channel_id=1, source_target_pairs={{0,1},{1,0},{2,3},{3,2},{4,5},{5,4},{6,7},{7,6},{8,9},{9,8},{10,11... | collective-permute-start | bytes 417800 | tf_op jit(solution)/shard_map/ppermute | solution.py:115
  10.7 6.9 %collective-permute-start.2 = (bf16[32,2176]{1,0:T(8,128)(2,1)S(1)}, bf16[32,2176]{1,0:T(8,128)(2,1)S(1)}, u32[]{:S(2)}, u32[]{:S(2)}) collective-permute-start(bf16[32,2176]{1,0:T(8,128)(2,1)S(1)} %pad_maximum_fusion), channel_id=1, source_target_pairs={{0,5},{1,4},{2,7},{3,6},{4,1},{5,0},{6,3},{7,2},{8,13},{9,12},{10,... | collective-permute-start | bytes 417800 | tf_op jit(solution)/shard_map/ppermute | solution.py:115
  17.6 32.2 %copy-start.8 = (bf16[32,2176]{1,0:T(8,128)(2,1)}, bf16[32,2176]{1,0:T(8,128)(2,1)S(1)}, u32[]{:S(2)}) copy-start(bf16[32,2176]{1,0:T(8,128)(2,1)S(1)} %collective-permute-done.2.refs_1_) | copy-start | bytes 417796
  17.7 20.8 %copy-start.10 = (bf16[128,2048]{1,0:T(8,128)(2,1)}, bf16[128,2048]{1,0:T(8,128)(2,1)S(1)}, u32[]{:S(2)}) copy-start(bf16[128,2048]{1,0:T(8,128)(2,1)S(1)} %constant_dynamic-update-slice_fusion.refs_0_) | copy-start | bytes 1572868
  17.7 14.5 %collective-permute-start.8 = (bf16[128,2048]{1,0:T(8,128)(2,1)S(1)}, bf16[128,2048]{1,0:T(8,128)(2,1)S(1)}, u32[]{:S(2)}, u32[]{:S(2)}) collective-permute-start(bf16[128,2048]{1,0:T(8,128)(2,1)S(1)} %constant_dynamic-update-slice_fusion.refs_0_), channel_id=1, source_target_pairs={{0,4},{1,5},{2,6},{3,7},{4,0},{5,1},{6,2},{7,3},{8,12},{9,13},{10,... | collective-permute-start | bytes 1572872 | tf_op jit(solution)/shard_map/ppermute | solution.py:115
  18.6 13.6 %collective-permute-start.9 = (bf16[128,2048]{1,0:T(8,128)(2,1)S(1)}, bf16[128,2048]{1,0:T(8,128)(2,1)S(1)}, u32[]{:S(2)}, u32[]{:S(2)}) collective-permute-start(bf16[128,2048]{1,0:T(8,128)(2,1)S(1)} %constant_dynamic-update-slice_fusion.refs_0_), channel_id=1, source_target_pairs={{0,1},{1,0},{2,3},{3,2},{4,5},{5,4},{6,7},{7,6},{8,9},{9,8},{10,11... | collective-permute-start | bytes 1572872 | tf_op jit(solution)/shard_map/ppermute | solution.py:115
  20.1 12.1 %collective-permute-start.5 = (bf16[32,2176]{1,0:T(8,128)(2,1)S(1)}, bf16[32,2176]{1,0:T(8,128)(2,1)S(1)}, u32[]{:S(2)}, u32[]{:S(2)}) collective-permute-start(bf16[32,2176]{1,0:T(8,128)(2,1)S(1)} %pad_maximum_fusion), channel_id=1, source_target_pairs={{0,16},{1,17},{2,18},{3,19},{4,20},{5,21},{6,22},{7,23},{8,24},{9,... | collective-permute-start | bytes 417800 | tf_op jit(solution)/shard_map/ppermute | solution.py:115
  23.1 9.1 %collective-permute-start.6 = (bf16[32,2176]{1,0:T(8,128)(2,1)S(1)}, bf16[32,2176]{1,0:T(8,128)(2,1)S(1)}, u32[]{:S(2)}, u32[]{:S(2)}) collective-permute-start(bf16[32,2176]{1,0:T(8,128)(2,1)S(1)} %pad_maximum_fusion), channel_id=1, source_target_pairs={{0,8},{1,9},{2,10},{3,11},{4,12},{5,13},{6,14},{7,15},{8,0},{9,1},... | collective-permute-start | bytes 417800 | tf_op jit(solution)/shard_map/ppermute | solution.py:115
  24.0 8.2 %collective-permute-start.7 = (bf16[32,2176]{1,0:T(8,128)(2,1)S(1)}, bf16[32,2176]{1,0:T(8,128)(2,1)S(1)}, u32[]{:S(2)}, u32[]{:S(2)}) collective-permute-start(bf16[32,2176]{1,0:T(8,128)(2,1)S(1)} %pad_maximum_fusion), channel_id=1, source_target_pairs={{0,24},{1,25},{2,26},{3,27},{4,28},{5,29},{6,30},{7,31},{8,16},{9,... | collective-permute-start | bytes 417800 | tf_op jit(solution)/shard_map/ppermute | solution.py:115
  32.2 2.4 %collective-permute-start.12 = (bf16[128,2048]{1,0:T(8,128)(2,1)S(1)}, bf16[128,2048]{1,0:T(8,128)(2,1)S(1)}, u32[]{:S(2)}, u32[]{:S(2)}) collective-permute-start(bf16[128,2048]{1,0:T(8,128)(2,1)S(1)} %constant_dynamic-update-slice_fusion.refs_0_), channel_id=1, source_target_pairs={{0,2},{1,3},{2,0},{3,1},{4,6},{5,7},{6,4},{7,5},{8,10},{9,11},{10,... | collective-permute-start | bytes 1572872 | tf_op jit(solution)/shard_map/ppermute | solution.py:115
  32.2 2.6 %collective-permute-start.13 = (bf16[128,2048]{1,0:T(8,128)(2,1)S(1)}, bf16[128,2048]{1,0:T(8,128)(2,1)S(1)}, u32[]{:S(2)}, u32[]{:S(2)}) collective-permute-start(bf16[128,2048]{1,0:T(8,128)(2,1)S(1)} %collective-permute-done.8.refs_2_), channel_id=1, source_target_pairs={{0,2},{1,3},{2,0},{3,1},{4,6},{5,7},{6,4},{7,5},{8,10},{9,11},{10,... | collective-permute-start | bytes 1572872 | tf_op jit(solution)/shard_map/ppermute | solution.py:115
  32.9 12.0 %collective-permute-start.11 = (bf16[128,2176]{1,0:T(8,128)(2,1)S(1)}, bf16[128,2176]{1,0:T(8,128)(2,1)S(1)}, u32[]{:S(2)}, u32[]{:S(2)}) collective-permute-start(bf16[128,2176]{1,0:T(8,128)(2,1)S(1)} %constant_dynamic-update-slice_fusion.4.refs_0_), channel_id=1, source_target_pairs={{0,2},{1,3},{2,0},{3,1},{4,6},{5,7},{6,4},{7,5},{8,10},{9,11},{10,... | collective-permute-start | bytes 1671176 | tf_op jit(solution)/shard_map/ppermute | solution.py:115
  32.9 15.7 %collective-permute-start.10 = (bf16[128,2176]{1,0:T(8,128)(2,1)S(1)}, bf16[128,2176]{1,0:T(8,128)(2,1)S(1)}, u32[]{:S(2)}, u32[]{:S(2)}) collective-permute-start(bf16[128,2176]{1,0:T(8,128)(2,1)S(1)} %constant_dynamic-update-slice_fusion.4.refs_0_), channel_id=1, source_target_pairs={{0,4},{1,5},{2,6},{3,7},{4,0},{5,1},{6,2},{7,3},{8,12},{9,13},{10,... | collective-permute-start | bytes 1671176 | tf_op jit(solution)/shard_map/ppermute | solution.py:115
  34.0 14.5 %collective-permute-start.14 = (bf16[128,2048]{1,0:T(8,128)(2,1)S(1)}, bf16[128,2048]{1,0:T(8,128)(2,1)S(1)}, u32[]{:S(2)}, u32[]{:S(2)}) collective-permute-start(bf16[128,2048]{1,0:T(8,128)(2,1)S(1)} %collective-permute-done.8.refs_2_), channel_id=1, source_target_pairs={{0,1},{1,0},{2,3},{3,2},{4,5},{5,4},{6,7},{7,6},{8,9},{9,8},{10,11... | collective-permute-start | bytes 1572872 | tf_op jit(solution)/shard_map/ppermute | solution.py:115
  34.6 14.0 %collective-permute-start.15 = (bf16[128,2048]{1,0:T(8,128)(2,1)S(1)}, bf16[128,2048]{1,0:T(8,128)(2,1)S(1)}, u32[]{:S(2)}, u32[]{:S(2)}) collective-permute-start(bf16[128,2048]{1,0:T(8,128)(2,1)S(1)} %collective-permute-done.9.refs_7_.refs_10_), channel_id=1, source_target_pairs={{0,2},{1,3},{2,0},{3,1},{4,6},{5,7},{6,4},{7,5},{8,10},{9,11},{10,... | collective-permute-start | bytes 1572872 | tf_op jit(solution)/shard_map/ppermute | solution.py:115
  34.8 13.7 %collective-permute-start.16 = (bf16[32,2176]{1,0:T(8,128)(2,1)S(1)}, bf16[32,2176]{1,0:T(8,128)(2,1)S(1)}, u32[]{:S(2)}, u32[]{:S(2)}) collective-permute-start(bf16[32,2176]{1,0:T(8,128)(2,1)S(1)} %collective-permute-done.1), channel_id=1, source_target_pairs={{0,16},{1,17},{2,18},{3,19},{4,20},{5,21},{6,22},{7,23},{8,24},{9,... | collective-permute-start | bytes 417800 | tf_op jit(solution)/shard_map/ppermute | solution.py:115
  48.6 2.0 %collective-permute-start.19 = (bf16[128,2176]{1,0:T(8,128)(2,1)S(1)}, bf16[128,2176]{1,0:T(8,128)(2,1)S(1)}, u32[]{:S(2)}, u32[]{:S(2)}) collective-permute-start(bf16[128,2176]{1,0:T(8,128)(2,1)S(1)} %collective-permute-done.10.refs_0_), channel_id=1, source_target_pairs={{0,2},{1,3},{2,0},{3,1},{4,6},{5,7},{6,4},{7,5},{8,10},{9,11},{10,... | collective-permute-start | bytes 1671176 | tf_op jit(solution)/shard_map/ppermute | solution.py:115
  48.9 4.0 %collective-permute-start.20 = (bf16[128,2048]{1,0:T(8,128)(2,1)S(1)}, bf16[128,2048]{1,0:T(8,128)(2,1)S(1)}, u32[]{:S(2)}, u32[]{:S(2)}) collective-permute-start(bf16[128,2048]{1,0:T(8,128)(2,1)S(1)} %collective-permute-done.14.refs_8_.refs_11_), channel_id=1, source_target_pairs={{0,2},{1,3},{2,0},{3,1},{4,6},{5,7},{6,4},{7,5},{8,10},{9,11},{10,... | collective-permute-start | bytes 1572872 | tf_op jit(solution)/shard_map/ppermute | solution.py:115
  49.2 3.8 %collective-permute-start.21 = (bf16[128,2176]{1,0:T(8,128)(2,1)S(1)}, bf16[128,2176]{1,0:T(8,128)(2,1)S(1)}, u32[]{:S(2)}, u32[]{:S(2)}) collective-permute-start(bf16[128,2176]{1,0:T(8,128)(2,1)S(1)} %get-tuple-element.92), channel_id=1, source_target_pairs={{0,2},{1,3},{2,0},{3,1},{4,6},{5,7},{6,4},{7,5},{8,10},{9,11},{10,... | collective-permute-start | bytes 1671176 | tf_op jit(solution)/shard_map/ppermute | solution.py:115
  49.4 3.5 %collective-permute-start.22 = (bf16[64,2176]{1,0:T(8,128)(2,1)S(1)}, bf16[64,2176]{1,0:T(8,128)(2,1)S(1)}, u32[]{:S(2)}, u32[]{:S(2)}) collective-permute-start(bf16[64,2176]{1,0:T(8,128)(2,1)S(1)} %constant_dynamic-update-slice_fusion.8.refs_0_), channel_id=1, source_target_pairs={{0,2},{1,3},{2,0},{3,1},{4,6},{5,7},{6,4},{7,5},{8,10},{9,11},{10,... | collective-permute-start | bytes 835592 | tf_op jit(solution)/shard_map/ppermute | solution.py:115
  49.8 3.1 %collective-permute-start.23 = (bf16[32,2176]{1,0:T(8,128)(2,1)S(1)}, bf16[32,2176]{1,0:T(8,128)(2,1)S(1)}, u32[]{:S(2)}, u32[]{:S(2)}) collective-permute-start(bf16[32,2176]{1,0:T(8,128)(2,1)S(1)} %collective-permute-done.2.refs_1_), channel_id=1, source_target_pairs={{0,2},{1,3},{2,0},{3,1},{4,6},{5,7},{6,4},{7,5},{8,10},{9,11},{10,... | collective-permute-start | bytes 417800 | tf_op jit(solution)/shard_map/ppermute | solution.py:115
  53.0 2.6 %collective-permute-start.24 = (bf16[128,2176]{1,0:T(8,128)(2,1)S(1)}, bf16[128,2176]{1,0:T(8,128)(2,1)S(1)}, u32[]{:S(2)}, u32[]{:S(2)}) collective-permute-start(bf16[128,2176]{1,0:T(8,128)(2,1)S(1)} %get-tuple-element.96), channel_id=1, source_target_pairs={{0,2},{1,3},{2,0},{3,1},{4,6},{5,7},{6,4},{7,5},{8,10},{9,11},{10,... | collective-permute-start | bytes 1671176 | tf_op jit(solution)/shard_map/ppermute | solution.py:115
  55.7 14.9 %collective-permute-start.25 = (bf16[128,2176]{1,0:T(8,128)(2,1)S(1)}, bf16[128,2176]{1,0:T(8,128)(2,1)S(1)}, u32[]{:S(2)}, u32[]{:S(2)}) collective-permute-start(bf16[128,2176]{1,0:T(8,128)(2,1)S(1)} %add_convert_fusion.1), channel_id=1, source_target_pairs={{0,4},{1,5},{2,6},{3,7},{4,0},{5,1},{6,2},{7,3},{8,12},{9,13},{10,... | collective-permute-start | bytes 1671176 | tf_op jit(solution)/shard_map/ppermute | solution.py:115
  57.5 13.3 %collective-permute-start.17 = (bf16[64,2176]{1,0:T(8,128)(2,1)S(1)}, bf16[64,2176]{1,0:T(8,128)(2,1)S(1)}, u32[]{:S(2)}, u32[]{:S(2)}) collective-permute-start(bf16[64,2176]{1,0:T(8,128)(2,1)S(1)} %constant_dynamic-update-slice_fusion.8.refs_0_), channel_id=1, source_target_pairs={{0,8},{1,9},{2,10},{3,11},{4,12},{5,13},{6,14},{7,15},{8,0},{9,1},... | collective-permute-start | bytes 835592 | tf_op jit(solution)/shard_map/ppermute | solution.py:115
  58.3 12.4 %collective-permute-start.18 = (bf16[96,2176]{1,0:T(8,128)(2,1)S(1)}, bf16[96,2176]{1,0:T(8,128)(2,1)S(1)}, u32[]{:S(2)}, u32[]{:S(2)}) collective-permute-start(bf16[96,2176]{1,0:T(8,128)(2,1)S(1)} %slice.12), channel_id=1, source_target_pairs={{0,1},{1,0},{2,3},{3,2},{4,5},{5,4},{6,7},{7,6},{8,9},{9,8},{10,11... | collective-permute-start | bytes 1253384 | tf_op jit(solution)/shard_map/ppermute | solution.py:115
  70.9 4.6 %collective-permute-start.29 = (bf16[160,2176]{1,0:T(8,128)(2,1)S(1)}, bf16[160,2176]{1,0:T(8,128)(2,1)S(1)}, u32[]{:S(2)}, u32[]{:S(2)}) collective-permute-start(bf16[160,2176]{1,0:T(8,128)(2,1)S(1)} %constant_dynamic-update-slice_fusion.10.refs_2_), channel_id=1, source_target_pairs={{0,2},{1,3},{2,0},{3,1},{4,6},{5,7},{6,4},{7,5},{8,10},{9,11},{10,... | collective-permute-start | bytes 2088968 | tf_op jit(solution)/shard_map/ppermute | solution.py:115
  71.0 13.2 %collective-permute-start.26 = (bf16[32,2176]{1,0:T(8,128)(2,1)S(1)}, bf16[32,2176]{1,0:T(8,128)(2,1)S(1)}, u32[]{:S(2)}, u32[]{:S(2)}) collective-permute-start(bf16[32,2176]{1,0:T(8,128)(2,1)S(1)} %get-tuple-element.131), channel_id=1, source_target_pairs={{0,16},{1,17},{2,18},{3,19},{4,20},{5,21},{6,22},{7,23},{8,24},{9,... | collective-permute-start | bytes 417800 | tf_op jit(solution)/shard_map/ppermute | solution.py:115
  73.8 10.4 %collective-permute-start.27 = (bf16[32,2176]{1,0:T(8,128)(2,1)S(1)}, bf16[32,2176]{1,0:T(8,128)(2,1)S(1)}, u32[]{:S(2)}, u32[]{:S(2)}) collective-permute-start(bf16[32,2176]{1,0:T(8,128)(2,1)S(1)} %get-tuple-element.130), channel_id=1, source_target_pairs={{0,8},{1,9},{2,10},{3,11},{4,12},{5,13},{6,14},{7,15},{8,0},{9,1},... | collective-permute-start | bytes 417800 | tf_op jit(solution)/shard_map/ppermute | solution.py:115
  74.2 10.8 %collective-permute-start.28 = (bf16[32,2176]{1,0:T(8,128)(2,1)S(1)}, bf16[32,2176]{1,0:T(8,128)(2,1)S(1)}, u32[]{:S(2)}, u32[]{:S(2)}) collective-permute-start(bf16[32,2176]{1,0:T(8,128)(2,1)S(1)} %get-tuple-element.129), channel_id=1, source_target_pairs={{0,24},{1,25},{2,26},{3,27},{4,28},{5,29},{6,30},{7,31},{8,16},{9,... | collective-permute-start | bytes 417800 | tf_op jit(solution)/shard_map/ppermute | solution.py:115
  (12 other events, 64.9 us)

commit v7 on v6

--- a/solution.py
+++ b/solution.py
@@ -406,7 +406,7 @@
 
 def whole_gradients(place, cot_rows, w_down, saved, x_rows, own, after):
     share, width = own[0].shape
-    tile = 2 * TILE
+    tile = 4 * TILE
     rows = sum(piece.shape[0] for piece in x_rows)
     half = pltpu.VMEM((share, rows), jnp.bfloat16)
     return pl.pallas_call(
@@ -573,7 +573,8 @@
 
 def body(tokens, expert_ids, *rest):
     tok_rows, top_count = expert_ids.shape
-    if 2 * tok_rows * top_count // lax.axis_size("expert") < tok_rows:
+    sizes = (lax.axis_size("expert"), lax.axis_size("dp"))
+    if sizes != (16, 2) or 2 * tok_rows * top_count // sizes[0] < tok_rows:
         return routed_body(tokens, expert_ids, *rest)
     return dense_body(tokens, expert_ids, *rest)
 

time: 86.2 us -> 86.2 us (level)
  transfers between devices with their start and end apart: 30 -> 30, of which waited for: 8 -> 8; matrix products, arithmetic and copies ran while one was open for 4% -> 4% of each run, Pallas kernels for 35% -> 34%
where the time goes in v7:
time: 86.2 us; the launch traced here: 85.9 us
  starting transfers between devices  31 us (36%)
  Pallas kernels  30.3 us (35%)
  waiting for transfers between devices  19.5 us (23%)
  other arithmetic  2.84 us (3%)
  local copies, waits for them, and re-layouts  1.22 us (1%)
  between operations  1.07 us (1%)
    ppermute x30, starting transfers between devices, swap(): return lax.ppermute(value, BOTH, [(i, i ^ flip) for i in range(count)])  31 us
    ppermute x30, waiting for transfers between devices, swap(): return lax.ppermute(value, BOTH, [(i, i ^ flip) for i in range(count)])  19.5 us
    pallas_call x1, Pallas kernels, whole_gradients(): pl.pallas_call(whole_gradient_kernel, grid=(width // tile,), in_specs=[IN...  8.34 us
    pallas_call x3, Pallas kernels, backward(): pl.pallas_call(functools.partial(backward_kernel, first, count), in_specs...  8.16 us
    pallas_call x1, Pallas kernels, own_gradients(): pl.pallas_call(own_gradient_kernel, grid=(width // tile,), in_specs=[IN_S...  6.57 us
    pallas_call x1, Pallas kernels, forward(): pl.pallas_call(forward_kernel, in_specs=[IN_HBM] * 7, out_specs=[IN_VMEM]...  6.34 us
  transfers between devices with their start and end apart: 30, of which 8 were waited for; matrix products, arithmetic and copies ran while one was open for 4% of the time, Pallas kernels for 34%

profile of v7, /device:TPU:0, one launch (start us, length us, event | category | flops | bytes accessed | tf_op | source)
XLA Modules:
  0.0 85.9 jit_solution(3375206123514449026)
XLA Ops:
  0.6 3.1 %collective-permute-start = (bf16[32,2048]{1,0:T(8,128)(2,1)}, bf16[32,2048]{1,0:T(8,128)(2,1)S(1)}, u32[]{:S(2)}, u32[]{:S(2)}) collective-permute-start(bf16[32,2048]{1,0:T(8,128)(2,1)} %param.7), channel_id=1, source_target_pairs={{0,8},{1,9},{2,10},{3,11},{4,12},{5,13},{6,14},{7,15},{8,0},{9,1},... | collective-permute-start | bytes 393224 | tf_op jit(solution)/shard_map/ppermute | solution.py:115
  3.7 2.6 %collective-permute-start.3 = (bf16[32,2048]{1,0:T(8,128)(2,1)}, bf16[32,2048]{1,0:T(8,128)(2,1)S(1)}, u32[]{:S(2)}, u32[]{:S(2)}) collective-permute-start(bf16[32,2048]{1,0:T(8,128)(2,1)} %param.7), channel_id=1, source_target_pairs={{0,16},{1,17},{2,18},{3,19},{4,20},{5,21},{6,22},{7,23},{8,24},{9,... | collective-permute-start | bytes 393224 | tf_op jit(solution)/shard_map/ppermute | solution.py:115
  6.3 0.7 convert_bitcast_fusion
  7.0 0.8 select_reduce_fusion
  7.8 0.9 %pad_maximum_fusion = bf16[32,2176]{1,0:T(8,128)(2,1)S(1)} fusion(bf16[32,128]{1,0:T(8,128)(2,1)S(1)} %select_reduce_fusion, bf16[32,2048]{1,0:T(8,128)(2,1)} %param.10), kind=kLoop, calls=%fused_computation.2 | loop fusion | flops 278528 | bytes 278528 | tf_op jit(solution)/shard_map/concatenate | solution.py:500
  9.0 1.7 %collective-permute-start.1 = (bf16[32,2176]{1,0:T(8,128)(2,1)S(1)}, bf16[32,2176]{1,0:T(8,128)(2,1)S(1)}, u32[]{:S(2)}, u32[]{:S(2)}) collective-permute-start(bf16[32,2176]{1,0:T(8,128)(2,1)S(1)} %pad_maximum_fusion), channel_id=1, source_target_pairs={{0,1},{1,0},{2,3},{3,2},{4,5},{5,4},{6,7},{7,6},{8,9},{9,8},{10,11... | collective-permute-start | bytes 417800 | tf_op jit(solution)/shard_map/ppermute | solution.py:115
  10.7 1.5 %collective-permute-start.2 = (bf16[32,2176]{1,0:T(8,128)(2,1)S(1)}, bf16[32,2176]{1,0:T(8,128)(2,1)S(1)}, u32[]{:S(2)}, u32[]{:S(2)}) collective-permute-start(bf16[32,2176]{1,0:T(8,128)(2,1)S(1)} %pad_maximum_fusion), channel_id=1, source_target_pairs={{0,5},{1,4},{2,7},{3,6},{4,1},{5,0},{6,3},{7,2},{8,13},{9,12},{10,... | collective-permute-start | bytes 417800 | tf_op jit(solution)/shard_map/ppermute | solution.py:115
  12.2 0.9 %constant_dynamic-update-slice_fusion.3 = bf16[128,2048]{1,0:T(8,128)(2,1)S(1)} fusion(bf16[32,2048]{1,0:T(8,128)(2,1)} %param.7), kind=kLoop, calls=%fused_computation.8 | loop fusion | bytes 262144
  13.1 3.8 %collective-permute-done.3 = bf16[32,2048]{1,0:T(8,128)(2,1)S(1)} collective-permute-done((bf16[32,2048]{1,0:T(8,128)(2,1)}, bf16[32,2048]{1,0:T(8,128)(2,1)S(1)}, u32[]{:S(2)}, u32[]{:S(2)}) %collective-permute-start.3) | collective-permute-done | bytes 131104 | tf_op jit(solution)/shard_map/ppermute | solution.py:115
  16.9 0.7 collective-permute-done.2.refs_1_
  17.7 0.9 %collective-permute-start.8 = (bf16[128,2048]{1,0:T(8,128)(2,1)S(1)}, bf16[128,2048]{1,0:T(8,128)(2,1)S(1)}, u32[]{:S(2)}, u32[]{:S(2)}) collective-permute-start(bf16[128,2048]{1,0:T(8,128)(2,1)S(1)} %constant_dynamic-update-slice_fusion.refs_0_), channel_id=1, source_target_pairs={{0,4},{1,5},{2,6},{3,7},{4,0},{5,1},{6,2},{7,3},{8,12},{9,13},{10,... | collective-permute-start | bytes 1572872 | tf_op jit(solution)/shard_map/ppermute | solution.py:115
  18.6 1.4 %collective-permute-start.9 = (bf16[128,2048]{1,0:T(8,128)(2,1)S(1)}, bf16[128,2048]{1,0:T(8,128)(2,1)S(1)}, u32[]{:S(2)}, u32[]{:S(2)}) collective-permute-start(bf16[128,2048]{1,0:T(8,128)(2,1)S(1)} %constant_dynamic-update-slice_fusion.refs_0_), channel_id=1, source_target_pairs={{0,1},{1,0},{2,3},{3,2},{4,5},{5,4},{6,7},{7,6},{8,9},{9,8},{10,11... | collective-permute-start | bytes 1572872 | tf_op jit(solution)/shard_map/ppermute | solution.py:115
  20.1 2.9 %collective-permute-start.5 = (bf16[32,2176]{1,0:T(8,128)(2,1)S(1)}, bf16[32,2176]{1,0:T(8,128)(2,1)S(1)}, u32[]{:S(2)}, u32[]{:S(2)}) collective-permute-start(bf16[32,2176]{1,0:T(8,128)(2,1)S(1)} %pad_maximum_fusion), channel_id=1, source_target_pairs={{0,16},{1,17},{2,18},{3,19},{4,20},{5,21},{6,22},{7,23},{8,24},{9,... | collective-permute-start | bytes 417800 | tf_op jit(solution)/shard_map/ppermute | solution.py:115
  23.1 1.0 %collective-permute-start.6 = (bf16[32,2176]{1,0:T(8,128)(2,1)S(1)}, bf16[32,2176]{1,0:T(8,128)(2,1)S(1)}, u32[]{:S(2)}, u32[]{:S(2)}) collective-permute-start(bf16[32,2176]{1,0:T(8,128)(2,1)S(1)} %pad_maximum_fusion), channel_id=1, source_target_pairs={{0,8},{1,9},{2,10},{3,11},{4,12},{5,13},{6,14},{7,15},{8,0},{9,1},... | collective-permute-start | bytes 417800 | tf_op jit(solution)/shard_map/ppermute | solution.py:115
  24.0 0.6 collective-permute-start.7
  24.6 7.6 %collective-permute-done.5 = bf16[32,2176]{1,0:T(8,128)(2,1)S(1)} collective-permute-done((bf16[32,2176]{1,0:T(8,128)(2,1)S(1)}, bf16[32,2176]{1,0:T(8,128)(2,1)S(1)}, u32[]{:S(2)}, u32[]{:S(2)}) %collective-permute-start.5) | collective-permute-done | bytes 139296 | tf_op jit(solution)/shard_map/ppermute | solution.py:115
  32.9 1.1 %collective-permute-start.10 = (bf16[128,2176]{1,0:T(8,128)(2,1)S(1)}, bf16[128,2176]{1,0:T(8,128)(2,1)S(1)}, u32[]{:S(2)}, u32[]{:S(2)}) collective-permute-start(bf16[128,2176]{1,0:T(8,128)(2,1)S(1)} %constant_dynamic-update-slice_fusion.4.refs_0_), channel_id=1, source_target_pairs={{0,4},{1,5},{2,6},{3,7},{4,0},{5,1},{6,2},{7,3},{8,12},{9,13},{10,... | collective-permute-start | bytes 1671176 | tf_op jit(solution)/shard_map/ppermute | solution.py:115
  34.8 3.6 %collective-permute-start.16 = (bf16[32,2176]{1,0:T(8,128)(2,1)S(1)}, bf16[32,2176]{1,0:T(8,128)(2,1)S(1)}, u32[]{:S(2)}, u32[]{:S(2)}) collective-permute-start(bf16[32,2176]{1,0:T(8,128)(2,1)S(1)} %collective-permute-done.1), channel_id=1, source_target_pairs={{0,16},{1,17},{2,18},{3,19},{4,20},{5,21},{6,22},{7,23},{8,24},{9,... | collective-permute-start | bytes 417800 | tf_op jit(solution)/shard_map/ppermute | solution.py:115
  38.5 6.3 %shard_map.110 = (bf16[768,2048]{1,0:T(8,128)(2,1)S(1)}, bf16[768,2048]{1,0:T(8,128)(2,1)S(1)}, bf16[2048,768]{1,0:T(8,128)(2,1)S(1)}, bf16[512,2048]{1,0:T(8,12...) custom-call(bf16[128,2048]{1,0:T(8,128)(2,1)} %copy-done.10, ...), custom_call_target="tpu_custom_call" | custom-call | flops 3221225472 | bytes 2097152 | tf_op jit(solution)/shard_map/pallas_call | solution.py:210
  44.8 3.7 %shard_map.111 = (bf16[128,2176]{1,0:T(8,128)(2,1)S(1)}, bf16[128,2176]{1,0:T(8,128)(2,1)S(1)}, bf16[256,2176]{1,0:T(8,128)(2,1)S(1)}, bf16[256,2304]{1,0:T(8,128)(2,1)S(1)}, f32[8,128]{1,0:T(8,128)S(1)}) custom-call(s32[2]{0:T(128)S(1)} %pad_add_fusion.place_ref.refs_8_, bf16[128,2176]{1,0:T(8,128)(2,1)S(1)} %constant_dynamic-update-slice_fusion.4.refs_0_, ...), custom_call_target="tpu_custom_call" | custom-call | tf_op jit(solution)/shard_map/pallas_call | solution.py:273
  50.0 0.6 collective-permute-done.19.refs_0_
  50.6 2.2 %shard_map.112 = (bf16[128,2176]{1,0:T(8,128)(2,1)S(1)}, bf16[128,2176]{1,0:T(8,128)(2,1)S(1)}, bf16[128,2304]{1,0:T(8,128)(2,1)S(1)}, f32[8,128]{1,0:T(8,128)}) custom-call(s32[2]{0:T(128)S(1)} %pad_add_fusion.place_ref.refs_8_, bf16[128,2176]{1,0:T(8,128)(2,1)S(1)} %collective-permute-done.19.refs_0_, f32[512,768]{1,0:T(8,128)S(1)} %get-tuple-element.78.refs_2_.refs_1_, ...), custom_call_target="tpu_custom_call" | custom-call | tf_op jit(solution)/shard_map/pallas_call | solution.py:273
  53.2 2.2 %shard_map.113 = (bf16[128,2176]{1,0:T(8,128)(2,1)S(1)}, bf16[128,2176]{1,0:T(8,128)(2,1)S(1)}, bf16[128,2304]{1,0:T(8,128)(2,1)S(1)}, f32[8,128]{1,0:T(8,128)}) custom-call(s32[2]{0:T(128)S(1)} %pad_add_fusion.place_ref.refs_8_, bf16[128,2176]{1,0:T(8,128)(2,1)S(1)} %collective-permute-done.10.refs_0_, f32[512,768]{1,0:T(8,128)S(1)} %get-tuple-element.78.refs_2_.refs_1_, ...), custom_call_target="tpu_custom_call" | custom-call | tf_op jit(solution)/shard_map/pallas_call | solution.py:273
  55.7 1.7 %collective-permute-start.25 = (bf16[128,2176]{1,0:T(8,128)(2,1)S(1)}, bf16[128,2176]{1,0:T(8,128)(2,1)S(1)}, u32[]{:S(2)}, u32[]{:S(2)}) collective-permute-start(bf16[128,2176]{1,0:T(8,128)(2,1)S(1)} %add_convert_fusion.1), channel_id=1, source_target_pairs={{0,4},{1,5},{2,6},{3,7},{4,0},{5,1},{6,2},{7,3},{8,12},{9,13},{10,... | collective-permute-start | bytes 1671176 | tf_op jit(solution)/shard_map/ppermute | solution.py:115
  57.5 0.9 %collective-permute-start.17 = (bf16[64,2176]{1,0:T(8,128)(2,1)S(1)}, bf16[64,2176]{1,0:T(8,128)(2,1)S(1)}, u32[]{:S(2)}, u32[]{:S(2)}) collective-permute-start(bf16[64,2176]{1,0:T(8,128)(2,1)S(1)} %constant_dynamic-update-slice_fusion.8.refs_0_), channel_id=1, source_target_pairs={{0,8},{1,9},{2,10},{3,11},{4,12},{5,13},{6,14},{7,15},{8,0},{9,1},... | collective-permute-start | bytes 835592 | tf_op jit(solution)/shard_map/ppermute | solution.py:115
  58.9 6.6 %shard_map.114 = (bf16[384,2048]{1,0:T(8,128)(2,1)S(1)}, bf16[384,2048]{1,0:T(8,128)(2,1)S(1)}, bf16[384,2048]{1,0:T(8,128)(2,1)S(1)}, bf16[384,512]{1,0:T(8,128...) custom-call(s32[2]{0:T(128)S(1)} %pad_add_fusion.place_ref.refs_8_, ...), custom_call_target="tpu_custom_call" | custom-call | tf_op jit(solution)/shard_map/pallas_call | solution.py:341
  65.5 5.1 %collective-permute-done.25 = bf16[128,2176]{1,0:T(8,128)(2,1)S(1)} collective-permute-done((bf16[128,2176]{1,0:T(8,128)(2,1)S(1)}, bf16[128,2176]{1,0:T(8,128)(2,1)S(1)}, u32[]{:S(2)}, u32[]{:S(2)}) %collective-permute-start.25) | collective-permute-done | bytes 557088 | tf_op jit(solution)/shard_map/ppermute | solution.py:115
  71.0 2.8 %collective-permute-start.26 = (bf16[32,2176]{1,0:T(8,128)(2,1)S(1)}, bf16[32,2176]{1,0:T(8,128)(2,1)S(1)}, u32[]{:S(2)}, u32[]{:S(2)}) collective-permute-start(bf16[32,2176]{1,0:T(8,128)(2,1)S(1)} %get-tuple-element.131), channel_id=1, source_target_pairs={{0,16},{1,17},{2,18},{3,19},{4,20},{5,21},{6,22},{7,23},{8,24},{9,... | collective-permute-start | bytes 417800 | tf_op jit(solution)/shard_map/ppermute | solution.py:115
  74.2 1.2 %collective-permute-start.28 = (bf16[32,2176]{1,0:T(8,128)(2,1)S(1)}, bf16[32,2176]{1,0:T(8,128)(2,1)S(1)}, u32[]{:S(2)}, u32[]{:S(2)}) collective-permute-start(bf16[32,2176]{1,0:T(8,128)(2,1)S(1)} %get-tuple-element.129), channel_id=1, source_target_pairs={{0,24},{1,25},{2,26},{3,27},{4,28},{5,29},{6,30},{7,31},{8,16},{9,... | collective-permute-start | bytes 417800 | tf_op jit(solution)/shard_map/ppermute | solution.py:115
  75.5 8.3 %shard_map.115 = (bf16[1,384,2048]{2,1,0:T(8,128)(2,1)}, bf16[1,384,2048]{2,1,0:T(8,128)(2,1)}, bf16[1,384,2048]{2,1,0:T(8,128)(2,1)}) custom-call(s32[2]{0:T(128)S(1)} %pad_add_fusion.place_ref.refs_8_, bf16[64,2176]{1,0:T(8,128)(2,1)} %copy-done.6, bf16[32,2176]{1,0:T(8,128)(2,1)} %copy-done.8, bf16[160,2176]{1,0:T(8,128)(2,1)} %copy-done.5, ...), custom_call_target="tpu_custom_call" | custom-call | flops 3221225472 | bytes 13631488 | tf_op jit(solution)/shard_map/pallas_call | solution.py:412
  83.8 1.2 %collective-permute-done.28.refs_3_ = bf16[32,2176]{1,0:T(8,128)(2,1)S(1)} collective-permute-done((bf16[32,2176]{1,0:T(8,128)(2,1)S(1)}, bf16[32,2176]{1,0:T(8,128)(2,1)S(1)}, u32[]{:S(2)}, u32[]{:S(2)}) %collective-permute-start.28) | collective-permute-done | bytes 139296 | tf_op jit(solution)/shard_map/ppermute | solution.py:115
  85.0 0.9 %shard_map.116 = (bf16[32,2048]{1,0:T(8,128)(2,1)}, bf16[8,32]{1,0:T(8,128)(2,1)}) custom-call(bf16[128,2176]{1,0:T(8,128)(2,1)S(1)} %add_convert_fusion.refs_0_, bf16[32,2176]{1,0:T(8,128)(2,1)S(1)} %collective-permute-done.26.refs_1_, bf16[32,2176]{1,0:T(8,128)(2,1)S(1)} %collective-permute-done.27.refs_2_, ...), custom_call_target="tpu_custom_call" | custom-call | tf_op jit(solution)/shard_map/pallas_call | solution.py:466
  (83 shorter events, 5.2 us)
Async XLA Ops:
  0.6 8.3 %collective-permute-start = (bf16[32,2048]{1,0:T(8,128)(2,1)}, bf16[32,2048]{1,0:T(8,128)(2,1)S(1)}, u32[]{:S(2)}, u32[]{:S(2)}) collective-permute-start(bf16[32,2048]{1,0:T(8,128)(2,1)} %param.7), channel_id=1, source_target_pairs={{0,8},{1,9},{2,10},{3,11},{4,12},{5,13},{6,14},{7,15},{8,0},{9,1},... | collective-permute-start | bytes 393224 | tf_op jit(solution)/shard_map/ppermute | solution.py:115
  3.7 13.2 %collective-permute-start.3 = (bf16[32,2048]{1,0:T(8,128)(2,1)}, bf16[32,2048]{1,0:T(8,128)(2,1)S(1)}, u32[]{:S(2)}, u32[]{:S(2)}) collective-permute-start(bf16[32,2048]{1,0:T(8,128)(2,1)} %param.7), channel_id=1, source_target_pairs={{0,16},{1,17},{2,18},{3,19},{4,20},{5,21},{6,22},{7,23},{8,24},{9,... | collective-permute-start | bytes 393224 | tf_op jit(solution)/shard_map/ppermute | solution.py:115
  6.3 10.6 %collective-permute-start.4 = (bf16[32,2048]{1,0:T(8,128)(2,1)}, bf16[32,2048]{1,0:T(8,128)(2,1)S(1)}, u32[]{:S(2)}, u32[]{:S(2)}) collective-permute-start(bf16[32,2048]{1,0:T(8,128)(2,1)} %param.7), channel_id=1, source_target_pairs={{0,24},{1,25},{2,26},{3,27},{4,28},{5,29},{6,30},{7,31},{8,16},{9,... | collective-permute-start | bytes 393224 | tf_op jit(solution)/shard_map/ppermute | solution.py:115
  9.0 7.9 %collective-permute-start.1 = (bf16[32,2176]{1,0:T(8,128)(2,1)S(1)}, bf16[32,2176]{1,0:T(8,128)(2,1)S(1)}, u32[]{:S(2)}, u32[]{:S(2)}) collective-permute-start(bf16[32,2176]{1,0:T(8,128)(2,1)S(1)} %pad_maximum_fusion), channel_id=1, source_target_pairs={{0,1},{1,0},{2,3},{3,2},{4,5},{5,4},{6,7},{7,6},{8,9},{9,8},{10,11... | collective-permute-start | bytes 417800 | tf_op jit(solution)/shard_map/ppermute | solution.py:115
  10.7 6.9 %collective-permute-start.2 = (bf16[32,2176]{1,0:T(8,128)(2,1)S(1)}, bf16[32,2176]{1,0:T(8,128)(2,1)S(1)}, u32[]{:S(2)}, u32[]{:S(2)}) collective-permute-start(bf16[32,2176]{1,0:T(8,128)(2,1)S(1)} %pad_maximum_fusion), channel_id=1, source_target_pairs={{0,5},{1,4},{2,7},{3,6},{4,1},{5,0},{6,3},{7,2},{8,13},{9,12},{10,... | collective-permute-start | bytes 417800 | tf_op jit(solution)/shard_map/ppermute | solution.py:115
  17.6 32.2 %copy-start.8 = (bf16[32,2176]{1,0:T(8,128)(2,1)}, bf16[32,2176]{1,0:T(8,128)(2,1)S(1)}, u32[]{:S(2)}) copy-start(bf16[32,2176]{1,0:T(8,128)(2,1)S(1)} %collective-permute-done.2.refs_1_) | copy-start | bytes 417796
  17.7 20.8 %copy-start.10 = (bf16[128,2048]{1,0:T(8,128)(2,1)}, bf16[128,2048]{1,0:T(8,128)(2,1)S(1)}, u32[]{:S(2)}) copy-start(bf16[128,2048]{1,0:T(8,128)(2,1)S(1)} %constant_dynamic-update-slice_fusion.refs_0_) | copy-start | bytes 1572868
  17.7 14.5 %collective-permute-start.8 = (bf16[128,2048]{1,0:T(8,128)(2,1)S(1)}, bf16[128,2048]{1,0:T(8,128)(2,1)S(1)}, u32[]{:S(2)}, u32[]{:S(2)}) collective-permute-start(bf16[128,2048]{1,0:T(8,128)(2,1)S(1)} %constant_dynamic-update-slice_fusion.refs_0_), channel_id=1, source_target_pairs={{0,4},{1,5},{2,6},{3,7},{4,0},{5,1},{6,2},{7,3},{8,12},{9,13},{10,... | collective-permute-start | bytes 1572872 | tf_op jit(solution)/shard_map/ppermute | solution.py:115
  18.6 13.6 %collective-permute-start.9 = (bf16[128,2048]{1,0:T(8,128)(2,1)S(1)}, bf16[128,2048]{1,0:T(8,128)(2,1)S(1)}, u32[]{:S(2)}, u32[]{:S(2)}) collective-permute-start(bf16[128,2048]{1,0:T(8,128)(2,1)S(1)} %constant_dynamic-update-slice_fusion.refs_0_), channel_id=1, source_target_pairs={{0,1},{1,0},{2,3},{3,2},{4,5},{5,4},{6,7},{7,6},{8,9},{9,8},{10,11... | collective-permute-start | bytes 1572872 | tf_op jit(solution)/shard_map/ppermute | solution.py:115
  20.1 12.1 %collective-permute-start.5 = (bf16[32,2176]{1,0:T(8,128)(2,1)S(1)}, bf16[32,2176]{1,0:T(8,128)(2,1)S(1)}, u32[]{:S(2)}, u32[]{:S(2)}) collective-permute-start(bf16[32,2176]{1,0:T(8,128)(2,1)S(1)} %pad_maximum_fusion), channel_id=1, source_target_pairs={{0,16},{1,17},{2,18},{3,19},{4,20},{5,21},{6,22},{7,23},{8,24},{9,... | collective-permute-start | bytes 417800 | tf_op jit(solution)/shard_map/ppermute | solution.py:115
  23.1 9.1 %collective-permute-start.6 = (bf16[32,2176]{1,0:T(8,128)(2,1)S(1)}, bf16[32,2176]{1,0:T(8,128)(2,1)S(1)}, u32[]{:S(2)}, u32[]{:S(2)}) collective-permute-start(bf16[32,2176]{1,0:T(8,128)(2,1)S(1)} %pad_maximum_fusion), channel_id=1, source_target_pairs={{0,8},{1,9},{2,10},{3,11},{4,12},{5,13},{6,14},{7,15},{8,0},{9,1},... | collective-permute-start | bytes 417800 | tf_op jit(solution)/shard_map/ppermute | solution.py:115
  24.0 8.2 %collective-permute-start.7 = (bf16[32,2176]{1,0:T(8,128)(2,1)S(1)}, bf16[32,2176]{1,0:T(8,128)(2,1)S(1)}, u32[]{:S(2)}, u32[]{:S(2)}) collective-permute-start(bf16[32,2176]{1,0:T(8,128)(2,1)S(1)} %pad_maximum_fusion), channel_id=1, source_target_pairs={{0,24},{1,25},{2,26},{3,27},{4,28},{5,29},{6,30},{7,31},{8,16},{9,... | collective-permute-start | bytes 417800 | tf_op jit(solution)/shard_map/ppermute | solution.py:115
  32.2 2.4 %collective-permute-start.12 = (bf16[128,2048]{1,0:T(8,128)(2,1)S(1)}, bf16[128,2048]{1,0:T(8,128)(2,1)S(1)}, u32[]{:S(2)}, u32[]{:S(2)}) collective-permute-start(bf16[128,2048]{1,0:T(8,128)(2,1)S(1)} %constant_dynamic-update-slice_fusion.refs_0_), channel_id=1, source_target_pairs={{0,2},{1,3},{2,0},{3,1},{4,6},{5,7},{6,4},{7,5},{8,10},{9,11},{10,... | collective-permute-start | bytes 1572872 | tf_op jit(solution)/shard_map/ppermute | solution.py:115
  32.2 2.6 %collective-permute-start.13 = (bf16[128,2048]{1,0:T(8,128)(2,1)S(1)}, bf16[128,2048]{1,0:T(8,128)(2,1)S(1)}, u32[]{:S(2)}, u32[]{:S(2)}) collective-permute-start(bf16[128,2048]{1,0:T(8,128)(2,1)S(1)} %collective-permute-done.8.refs_2_), channel_id=1, source_target_pairs={{0,2},{1,3},{2,0},{3,1},{4,6},{5,7},{6,4},{7,5},{8,10},{9,11},{10,... | collective-permute-start | bytes 1572872 | tf_op jit(solution)/shard_map/ppermute | solution.py:115
  32.9 12.0 %collective-permute-start.11 = (bf16[128,2176]{1,0:T(8,128)(2,1)S(1)}, bf16[128,2176]{1,0:T(8,128)(2,1)S(1)}, u32[]{:S(2)}, u32[]{:S(2)}) collective-permute-start(bf16[128,2176]{1,0:T(8,128)(2,1)S(1)} %constant_dynamic-update-slice_fusion.4.refs_0_), channel_id=1, source_target_pairs={{0,2},{1,3},{2,0},{3,1},{4,6},{5,7},{6,4},{7,5},{8,10},{9,11},{10,... | collective-permute-start | bytes 1671176 | tf_op jit(solution)/shard_map/ppermute | solution.py:115
  32.9 15.7 %collective-permute-start.10 = (bf16[128,2176]{1,0:T(8,128)(2,1)S(1)}, bf16[128,2176]{1,0:T(8,128)(2,1)S(1)}, u32[]{:S(2)}, u32[]{:S(2)}) collective-permute-start(bf16[128,2176]{1,0:T(8,128)(2,1)S(1)} %constant_dynamic-update-slice_fusion.4.refs_0_), channel_id=1, source_target_pairs={{0,4},{1,5},{2,6},{3,7},{4,0},{5,1},{6,2},{7,3},{8,12},{9,13},{10,... | collective-permute-start | bytes 1671176 | tf_op jit(solution)/shard_map/ppermute | solution.py:115
  34.0 14.5 %collective-permute-start.14 = (bf16[128,2048]{1,0:T(8,128)(2,1)S(1)}, bf16[128,2048]{1,0:T(8,128)(2,1)S(1)}, u32[]{:S(2)}, u32[]{:S(2)}) collective-permute-start(bf16[128,2048]{1,0:T(8,128)(2,1)S(1)} %collective-permute-done.8.refs_2_), channel_id=1, source_target_pairs={{0,1},{1,0},{2,3},{3,2},{4,5},{5,4},{6,7},{7,6},{8,9},{9,8},{10,11... | collective-permute-start | bytes 1572872 | tf_op jit(solution)/shard_map/ppermute | solution.py:115
  34.6 14.0 %collective-permute-start.15 = (bf16[128,2048]{1,0:T(8,128)(2,1)S(1)}, bf16[128,2048]{1,0:T(8,128)(2,1)S(1)}, u32[]{:S(2)}, u32[]{:S(2)}) collective-permute-start(bf16[128,2048]{1,0:T(8,128)(2,1)S(1)} %collective-permute-done.9.refs_7_.refs_10_), channel_id=1, source_target_pairs={{0,2},{1,3},{2,0},{3,1},{4,6},{5,7},{6,4},{7,5},{8,10},{9,11},{10,... | collective-permute-start | bytes 1572872 | tf_op jit(solution)/shard_map/ppermute | solution.py:115
  34.8 13.7 %collective-permute-start.16 = (bf16[32,2176]{1,0:T(8,128)(2,1)S(1)}, bf16[32,2176]{1,0:T(8,128)(2,1)S(1)}, u32[]{:S(2)}, u32[]{:S(2)}) collective-permute-start(bf16[32,2176]{1,0:T(8,128)(2,1)S(1)} %collective-permute-done.1), channel_id=1, source_target_pairs={{0,16},{1,17},{2,18},{3,19},{4,20},{5,21},{6,22},{7,23},{8,24},{9,... | collective-permute-start | bytes 417800 | tf_op jit(solution)/shard_map/ppermute | solution.py:115
  48.6 2.0 %collective-permute-start.19 = (bf16[128,2176]{1,0:T(8,128)(2,1)S(1)}, bf16[128,2176]{1,0:T(8,128)(2,1)S(1)}, u32[]{:S(2)}, u32[]{:S(2)}) collective-permute-start(bf16[128,2176]{1,0:T(8,128)(2,1)S(1)} %collective-permute-done.10.refs_0_), channel_id=1, source_target_pairs={{0,2},{1,3},{2,0},{3,1},{4,6},{5,7},{6,4},{7,5},{8,10},{9,11},{10,... | collective-permute-start | bytes 1671176 | tf_op jit(solution)/shard_map/ppermute | solution.py:115
  48.9 4.0 %collective-permute-start.20 = (bf16[128,2048]{1,0:T(8,128)(2,1)S(1)}, bf16[128,2048]{1,0:T(8,128)(2,1)S(1)}, u32[]{:S(2)}, u32[]{:S(2)}) collective-permute-start(bf16[128,2048]{1,0:T(8,128)(2,1)S(1)} %collective-permute-done.14.refs_8_.refs_11_), channel_id=1, source_target_pairs={{0,2},{1,3},{2,0},{3,1},{4,6},{5,7},{6,4},{7,5},{8,10},{9,11},{10,... | collective-permute-start | bytes 1572872 | tf_op jit(solution)/shard_map/ppermute | solution.py:115
  49.2 3.8 %collective-permute-start.21 = (bf16[128,2176]{1,0:T(8,128)(2,1)S(1)}, bf16[128,2176]{1,0:T(8,128)(2,1)S(1)}, u32[]{:S(2)}, u32[]{:S(2)}) collective-permute-start(bf16[128,2176]{1,0:T(8,128)(2,1)S(1)} %get-tuple-element.92), channel_id=1, source_target_pairs={{0,2},{1,3},{2,0},{3,1},{4,6},{5,7},{6,4},{7,5},{8,10},{9,11},{10,... | collective-permute-start | bytes 1671176 | tf_op jit(solution)/shard_map/ppermute | solution.py:115
  49.4 3.5 %collective-permute-start.22 = (bf16[64,2176]{1,0:T(8,128)(2,1)S(1)}, bf16[64,2176]{1,0:T(8,128)(2,1)S(1)}, u32[]{:S(2)}, u32[]{:S(2)}) collective-permute-start(bf16[64,2176]{1,0:T(8,128)(2,1)S(1)} %constant_dynamic-update-slice_fusion.8.refs_0_), channel_id=1, source_target_pairs={{0,2},{1,3},{2,0},{3,1},{4,6},{5,7},{6,4},{7,5},{8,10},{9,11},{10,... | collective-permute-start | bytes 835592 | tf_op jit(solution)/shard_map/ppermute | solution.py:115
  49.8 3.1 %collective-permute-start.23 = (bf16[32,2176]{1,0:T(8,128)(2,1)S(1)}, bf16[32,2176]{1,0:T(8,128)(2,1)S(1)}, u32[]{:S(2)}, u32[]{:S(2)}) collective-permute-start(bf16[32,2176]{1,0:T(8,128)(2,1)S(1)} %collective-permute-done.2.refs_1_), channel_id=1, source_target_pairs={{0,2},{1,3},{2,0},{3,1},{4,6},{5,7},{6,4},{7,5},{8,10},{9,11},{10,... | collective-permute-start | bytes 417800 | tf_op jit(solution)/shard_map/ppermute | solution.py:115
  53.0 2.6 %collective-permute-start.24 = (bf16[128,2176]{1,0:T(8,128)(2,1)S(1)}, bf16[128,2176]{1,0:T(8,128)(2,1)S(1)}, u32[]{:S(2)}, u32[]{:S(2)}) collective-permute-start(bf16[128,2176]{1,0:T(8,128)(2,1)S(1)} %get-tuple-element.96), channel_id=1, source_target_pairs={{0,2},{1,3},{2,0},{3,1},{4,6},{5,7},{6,4},{7,5},{8,10},{9,11},{10,... | collective-permute-start | bytes 1671176 | tf_op jit(solution)/shard_map/ppermute | solution.py:115
  55.7 14.9 %collective-permute-start.25 = (bf16[128,2176]{1,0:T(8,128)(2,1)S(1)}, bf16[128,2176]{1,0:T(8,128)(2,1)S(1)}, u32[]{:S(2)}, u32[]{:S(2)}) collective-permute-start(bf16[128,2176]{1,0:T(8,128)(2,1)S(1)} %add_convert_fusion.1), channel_id=1, source_target_pairs={{0,4},{1,5},{2,6},{3,7},{4,0},{5,1},{6,2},{7,3},{8,12},{9,13},{10,... | collective-permute-start | bytes 1671176 | tf_op jit(solution)/shard_map/ppermute | solution.py:115
  57.5 13.3 %collective-permute-start.17 = (bf16[64,2176]{1,0:T(8,128)(2,1)S(1)}, bf16[64,2176]{1,0:T(8,128)(2,1)S(1)}, u32[]{:S(2)}, u32[]{:S(2)}) collective-permute-start(bf16[64,2176]{1,0:T(8,128)(2,1)S(1)} %constant_dynamic-update-slice_fusion.8.refs_0_), channel_id=1, source_target_pairs={{0,8},{1,9},{2,10},{3,11},{4,12},{5,13},{6,14},{7,15},{8,0},{9,1},... | collective-permute-start | bytes 835592 | tf_op jit(solution)/shard_map/ppermute | solution.py:115
  58.3 12.4 %collective-permute-start.18 = (bf16[96,2176]{1,0:T(8,128)(2,1)S(1)}, bf16[96,2176]{1,0:T(8,128)(2,1)S(1)}, u32[]{:S(2)}, u32[]{:S(2)}) collective-permute-start(bf16[96,2176]{1,0:T(8,128)(2,1)S(1)} %slice.12), channel_id=1, source_target_pairs={{0,1},{1,0},{2,3},{3,2},{4,5},{5,4},{6,7},{7,6},{8,9},{9,8},{10,11... | collective-permute-start | bytes 1253384 | tf_op jit(solution)/shard_map/ppermute | solution.py:115
  70.9 4.6 %collective-permute-start.29 = (bf16[160,2176]{1,0:T(8,128)(2,1)S(1)}, bf16[160,2176]{1,0:T(8,128)(2,1)S(1)}, u32[]{:S(2)}, u32[]{:S(2)}) collective-permute-start(bf16[160,2176]{1,0:T(8,128)(2,1)S(1)} %constant_dynamic-update-slice_fusion.10.refs_2_), channel_id=1, source_target_pairs={{0,2},{1,3},{2,0},{3,1},{4,6},{5,7},{6,4},{7,5},{8,10},{9,11},{10,... | collective-permute-start | bytes 2088968 | tf_op jit(solution)/shard_map/ppermute | solution.py:115
  71.0 12.8 %collective-permute-start.26 = (bf16[32,2176]{1,0:T(8,128)(2,1)S(1)}, bf16[32,2176]{1,0:T(8,128)(2,1)S(1)}, u32[]{:S(2)}, u32[]{:S(2)}) collective-permute-start(bf16[32,2176]{1,0:T(8,128)(2,1)S(1)} %get-tuple-element.131), channel_id=1, source_target_pairs={{0,16},{1,17},{2,18},{3,19},{4,20},{5,21},{6,22},{7,23},{8,24},{9,... | collective-permute-start | bytes 417800 | tf_op jit(solution)/shard_map/ppermute | solution.py:115
  73.8 10.1 %collective-permute-start.27 = (bf16[32,2176]{1,0:T(8,128)(2,1)S(1)}, bf16[32,2176]{1,0:T(8,128)(2,1)S(1)}, u32[]{:S(2)}, u32[]{:S(2)}) collective-permute-start(bf16[32,2176]{1,0:T(8,128)(2,1)S(1)} %get-tuple-element.130), channel_id=1, source_target_pairs={{0,8},{1,9},{2,10},{3,11},{4,12},{5,13},{6,14},{7,15},{8,0},{9,1},... | collective-permute-start | bytes 417800 | tf_op jit(solution)/shard_map/ppermute | solution.py:115
  74.2 10.8 %collective-permute-start.28 = (bf16[32,2176]{1,0:T(8,128)(2,1)S(1)}, bf16[32,2176]{1,0:T(8,128)(2,1)S(1)}, u32[]{:S(2)}, u32[]{:S(2)}) collective-permute-start(bf16[32,2176]{1,0:T(8,128)(2,1)S(1)} %get-tuple-element.129), channel_id=1, source_target_pairs={{0,24},{1,25},{2,26},{3,27},{4,28},{5,29},{6,30},{7,31},{8,16},{9,... | collective-permute-start | bytes 417800 | tf_op jit(solution)/shard_map/ppermute | solution.py:115
  (12 other events, 64.9 us)
